TPU v7x, 32 devices: a whole 2x2x4 slice. The times are simulated.
32 devices in a mesh: section: 2 (over x), tensor: 4 (over y, core), dp: 4 (over z).
Axes of the slice: x: 2, y: 2, z: 4, core: 2. Of those that a mesh axis runs over, the one named last changes fastest.
Arguments:
- inputs: bfloat16 [8, 2048, 1024], P('dp', 'tensor'), may hold values from -6 to 6
- cotangent: bfloat16 [8, 2048, 1024], P('dp', 'tensor'), may hold values from -6 to 6
- lengths: int32 [8, 8], P('dp'), may hold values from 0 to 2048, as said below
- qkv_weight: bfloat16 [2, 1024, 3, 1024], P('section', 'dp', None, 'tensor'), may hold values from -0.1875 to 0.1875
- qkv_bias: bfloat16 [2, 3, 1024], P('section', None, ('tensor', 'dp')), may hold values from -3 to 3
- dense_weight: bfloat16 [2, 1024, 1024], P('section', 'tensor', 'dp'), may hold values from -0.5 to 0.5
- in_weight: bfloat16 [2, 1024, 4096], P('section', 'dp', 'tensor'), may hold values from -0.1875 to 0.1875
- in_bias: bfloat16 [2, 4096], P('section', ('tensor', 'dp')), may hold values from -3 to 3
- out_weight: bfloat16 [2, 4096, 1024], P('section', 'tensor', 'dp'), may hold values from -0.09375 to 0.09375
- norm_gains: bfloat16 [2, 2, 1024], P('section', None, ('tensor', 'dp')), may hold values from 0.25 to 1.75
- norm_biases: bfloat16 [2, 2, 1024], P('section', None, ('tensor', 'dp')), may hold values from -2 to 2
- out_biases: bfloat16 [2, 2, 1024], P('section', None, ('tensor', 'dp')), may hold values from -3 to 3
Outputs:
- activations: bfloat16 [2, 8, 2048, 1024], P('section', 'dp', 'tensor')
- input_grads: float32 [2, 8, 2048, 1024], P('section', 'dp', 'tensor')
- qkv_weight_grad: float32 [2, 1024, 3, 1024], P('section', 'dp', None, 'tensor')
- qkv_bias_grad: float32 [2, 3, 1024], P('section', None, ('tensor', 'dp'))
- dense_weight_grad: float32 [2, 1024, 1024], P('section', 'tensor', 'dp')
- in_weight_grad: float32 [2, 1024, 4096], P('section', 'dp', 'tensor')
- in_bias_grad: float32 [2, 4096], P('section', ('tensor', 'dp'))
- out_weight_grad: float32 [2, 4096, 1024], P('section', 'tensor', 'dp')
- norm_gains_grad: float32 [2, 2, 1024], P('section', None, ('tensor', 'dp'))
- norm_biases_grad: float32 [2, 2, 1024], P('section', None, ('tensor', 'dp'))
- out_biases_grad: float32 [2, 2, 1024], P('section', None, ('tensor', 'dp'))
Inputs may be any that keep to these rules, and one draw needn't show every extreme that they name: Row j lists the lengths of the documents of sequence j in order, zeros included; they sum to 2048 or less, and the positions after that sum are padding. Among the 2 sequences of each replica (rows j with the same j // 2) one is a single document of 2048 tokens.
All inputs are finite; a program needn't handle non-finite values.
Results may differ from a plain program's by a relative error of at most 0.018.
Values may be sent and summed in bfloat16 or wider, within the bound.
No kernel may reach another device: no remote copies, remote signals or barrier semaphores. Data moves between devices by JAX's collectives and lax.ppermute only.
A program may use at most 320 MiB of HBM per device.

v0:
```python
from functools import partial
import math

import jax
import jax.numpy as jnp
from jax import lax
from jax.sharding import PartitionSpec as P

HDIM = 64
QBLK = 512


epsilon = 1e-05


def from_behind(block, axis, distance):
    devices = range(lax.axis_size(axis))
    route = [(i - distance, i) for i in devices if i - distance in devices]
    return lax.ppermute(block, axis, route)


def normalize(values, gain, shift):
    centered = values - jnp.mean(values, -1, keepdims=True)
    inverse = lax.rsqrt(jnp.mean(centered * centered, -1, keepdims=True) + epsilon)
    normal = centered * inverse
    return (normal * gain + shift, normal, inverse)


def norm_back(grad, normal, inverse, gain):
    scaled = grad * gain
    return inverse * (
        scaled
        - jnp.mean(scaled, -1, keepdims=True)
        - normal * jnp.mean(scaled * normal, -1, keepdims=True)
    )


def doc_layout(length_row, seq_len):
    positions = jnp.arange(seq_len, dtype=jnp.int32)
    ends = jnp.cumsum(length_row)
    passed = positions[:, None] >= ends[None, :]
    doc_ids = jnp.sum(passed.astype(jnp.int32), -1)
    starts = jnp.sum(jnp.where(passed, length_row[None, :], 0), -1)
    return (doc_ids, positions - starts, positions < ends[-1])


def rotary_tables(rot_pos):
    rotary = HDIM // 4
    counter = jnp.arange(rotary // 2, dtype=jnp.float32)
    inverse = jnp.exp(counter * (-2.0 * math.log(10000.0) / rotary))
    angles = rot_pos.astype(jnp.float32)[:, None] * inverse[None, :]
    return (jnp.cos(angles), jnp.sin(angles))


def rotate(values, cosine, sine):
    width = cosine.shape[-1]
    leading = values[..., :width]
    trailing = values[..., width : 2 * width]
    cosines = cosine[:, None, :]
    sines = sine[:, None, :]
    return jnp.concatenate(
        [
            leading * cosines - trailing * sines,
            trailing * cosines + leading * sines,
            values[..., 2 * width :],
        ],
        -1,
    )


def unrotate(grads, cosine, sine):
    width = cosine.shape[-1]
    leading = grads[..., :width]
    trailing = grads[..., width : 2 * width]
    cosines = cosine[:, None, :]
    sines = sine[:, None, :]
    return jnp.concatenate(
        [
            leading * cosines + trailing * sines,
            trailing * cosines - leading * sines,
            grads[..., 2 * width :],
        ],
        -1,
    )


def block_mask(doc_ids, start):
    query_docs = lax.dynamic_slice_in_dim(doc_ids, start, QBLK, 0)
    query_pos = start + jnp.arange(QBLK, dtype=jnp.int32)
    positions = jnp.arange(doc_ids.shape[0], dtype=jnp.int32)
    return (query_docs[:, None] == doc_ids[None, :]) & (positions[None, :] <= query_pos[:, None])


def attend(queries, keys_all, values_all, doc_ids):
    seq_len = queries.shape[0]
    scale = 1.0 / math.sqrt(HDIM)

    def forward_block(index):
        start = index * QBLK
        query_block = lax.dynamic_slice_in_dim(queries, start, QBLK, 0)
        scores = (
            jnp.einsum("qhd,khd->hqk", query_block, keys_all, preferred_element_type=jnp.float32)
            * scale
        )
        scores = jnp.where(block_mask(doc_ids, start)[None], scores, -1e30)
        highest = jnp.max(scores, -1, keepdims=True)
        shifted = jnp.exp(scores - highest)
        total = jnp.sum(shifted, -1, keepdims=True)
        probs = (shifted / total).astype(jnp.bfloat16)
        output = jnp.einsum("hqk,khd->qhd", probs, values_all, preferred_element_type=jnp.float32)
        return (output.astype(jnp.bfloat16), (highest + jnp.log(total))[..., 0])

    outputs, log_sums = lax.map(forward_block, jnp.arange(seq_len // QBLK, dtype=jnp.int32))
    return (outputs.reshape(seq_len, -1), log_sums)


def attend_back(queries, keys_all, values_all, log_sums, mixed_grad, doc_ids):
    seq_len = queries.shape[0]
    scale = 1.0 / math.sqrt(HDIM)
    grad_heads = mixed_grad.reshape(queries.shape)

    def backward_block(carry, index):
        key_acc, value_acc = carry
        start = index * QBLK
        query_block = lax.dynamic_slice_in_dim(queries, start, QBLK, 0)
        grad_block = lax.dynamic_slice_in_dim(grad_heads, start, QBLK, 0)
        scores = (
            jnp.einsum("qhd,khd->hqk", query_block, keys_all, preferred_element_type=jnp.float32)
            * scale
        )
        scores = jnp.where(block_mask(doc_ids, start)[None], scores, -1e30)
        probs = jnp.exp(scores - log_sums[index][..., None])
        value_acc = value_acc + jnp.einsum(
            "hqk,qhd->khd",
            probs.astype(jnp.bfloat16),
            grad_block,
            preferred_element_type=jnp.float32,
        )
        prob_grad = jnp.einsum(
            "qhd,khd->hqk", grad_block, values_all, preferred_element_type=jnp.float32
        )
        delta = jnp.sum(prob_grad * probs, -1, keepdims=True)
        score_grad = (probs * (prob_grad - delta)).astype(jnp.bfloat16)
        query_grad = (
            jnp.einsum("hqk,khd->qhd", score_grad, keys_all, preferred_element_type=jnp.float32)
            * scale
        )
        key_acc = (
            key_acc
            + jnp.einsum(
                "hqk,qhd->khd", score_grad, query_block, preferred_element_type=jnp.float32
            )
            * scale
        )
        return ((key_acc, value_acc), query_grad)

    empty = jnp.zeros(queries.shape, jnp.float32)
    (key_grad, value_grad), query_grads = lax.scan(
        backward_block, (empty, empty), jnp.arange(seq_len // QBLK, dtype=jnp.int32)
    )
    return (query_grads.reshape(queries.shape), key_grad, value_grad)


def mixing(first_all, second_all, weights, length_row):
    qkv_w, qkv_b, dense_w, in_w, in_b, out_w = weights
    seq_len = first_all.shape[0]
    local_heads = qkv_w.shape[2] // HDIM
    doc_ids, rot_pos, valid = doc_layout(length_row, seq_len)
    projected = (
        jnp.einsum("sd,dcf->scf", first_all, qkv_w, preferred_element_type=jnp.float32)
        + qkv_b.astype(jnp.float32)[None]
    )
    projected = projected.reshape(seq_len, 3, local_heads, HDIM)
    cosine, sine = rotary_tables(rot_pos)
    queries = rotate(projected[:, 0], cosine, sine).astype(jnp.bfloat16)
    keys_all = rotate(projected[:, 1], cosine, sine).astype(jnp.bfloat16)
    values_all = projected[:, 2].astype(jnp.bfloat16)
    mixed, log_sums = attend(queries, keys_all, values_all, doc_ids)
    inner = jnp.dot(second_all, in_w, preferred_element_type=jnp.float32) + in_b.astype(jnp.float32)
    activated = jax.nn.gelu(inner, approximate=False).astype(jnp.bfloat16)
    return (first_all, second_all, queries, keys_all, values_all, log_sums, mixed, inner, activated)


def spread_norms(layer_in, vectors):
    gains, shifts, _ = vectors
    first, _, _ = normalize(layer_in, gains[0], shifts[0])
    second, _, _ = normalize(layer_in, gains[1], shifts[1])
    first_all, second_all = (
        lax.all_gather(first.astype(jnp.bfloat16), "tensor", axis=0, tiled=True),
        lax.all_gather(second.astype(jnp.bfloat16), "tensor", axis=0, tiled=True),
    )
    return (first_all, second_all, ())


def forward_layer(layer_in, length_row, weights, vectors):
    out_bias = vectors[2]
    first_all, second_all, extra = spread_norms(layer_in, vectors)
    kept = mixing(first_all, second_all, weights, length_row) + extra
    branch_terms = jnp.dot(kept[6], weights[2], preferred_element_type=jnp.float32) + jnp.dot(
        kept[8], weights[5], preferred_element_type=jnp.float32
    )
    branch = lax.psum_scatter(
        branch_terms.astype(jnp.bfloat16), "tensor", scatter_dimension=0, tiled=True
    ).astype(jnp.float32)
    return (layer_in + branch + out_bias[0] + out_bias[1], kept)


def backward_layer(grad_out, layer_in, kept, length_row, weights, vectors):
    qkv_w, qkv_b, dense_w, in_w, in_b, out_w = weights
    gains, shifts, out_bias = vectors
    first_all, second_all, queries, keys_all, values_all, log_sums, mixed, inner, activated = kept[
        :9
    ]
    seq_len = first_all.shape[0]
    grad_all = lax.all_gather(grad_out.astype(jnp.bfloat16), "tensor", axis=0, tiled=True)
    dense_grad = jnp.einsum("sf,sd->fd", mixed, grad_all, preferred_element_type=jnp.float32)
    down_grad = jnp.einsum("sf,sd->fd", activated, grad_all, preferred_element_type=jnp.float32)
    mixed_grad = jnp.einsum(
        "sd,fd->sf", grad_all, dense_w, preferred_element_type=jnp.float32
    ).astype(jnp.bfloat16)
    act_grad = jnp.einsum("sd,fd->sf", grad_all, out_w, preferred_element_type=jnp.float32)
    _, gelu_back = jax.vjp(partial(jax.nn.gelu, approximate=False), inner)
    inner_grad = gelu_back(act_grad)[0].astype(jnp.bfloat16)
    up_bias_grad = jnp.sum(inner_grad.astype(jnp.float32), 0)
    up_grad = jnp.einsum("sd,sf->df", second_all, inner_grad, preferred_element_type=jnp.float32)
    second_grad = jnp.einsum("sf,df->sd", inner_grad, in_w, preferred_element_type=jnp.float32)
    doc_ids, rot_pos, _ = doc_layout(length_row, seq_len)
    cosine, sine = rotary_tables(rot_pos)
    query_grad, key_grad, value_grad = attend_back(
        queries, keys_all, values_all, log_sums, mixed_grad, doc_ids
    )
    stacked = jnp.stack(
        [unrotate(query_grad, cosine, sine), unrotate(key_grad, cosine, sine), value_grad], 1
    )
    project_grad = stacked.reshape(seq_len, 3, -1).astype(jnp.bfloat16)
    project_bias_grad = jnp.sum(project_grad.astype(jnp.float32), 0)
    project_weight_grad = jnp.einsum(
        "sd,scf->dcf", first_all, project_grad, preferred_element_type=jnp.float32
    )
    first_grad = jnp.einsum("scf,dcf->sd", project_grad, qkv_w, preferred_element_type=jnp.float32)
    first_part, second_part = (
        lax.psum_scatter(
            first_grad.astype(jnp.bfloat16), "tensor", scatter_dimension=0, tiled=True
        ).astype(jnp.float32),
        lax.psum_scatter(
            second_grad.astype(jnp.bfloat16), "tensor", scatter_dimension=0, tiled=True
        ).astype(jnp.float32),
    )
    _, first_normal, first_inverse = normalize(layer_in, gains[0], shifts[0])
    _, second_normal, second_inverse = normalize(layer_in, gains[1], shifts[1])
    input_grad = (
        grad_out
        + norm_back(first_part, first_normal, first_inverse, gains[0])
        + norm_back(second_part, second_normal, second_inverse, gains[1])
    )
    gain_grad = jnp.stack(
        [jnp.sum(first_part * first_normal, 0), jnp.sum(second_part * second_normal, 0)]
    )
    shift_grad = jnp.stack([jnp.sum(first_part, 0), jnp.sum(second_part, 0)])
    bias_row = jnp.sum(grad_out, 0)
    out_bias_grad = jnp.stack([bias_row, bias_row])
    return (
        input_grad,
        (project_weight_grad, project_bias_grad, dense_grad, up_grad, up_bias_grad, down_grad),
        (gain_grad, shift_grad, out_bias_grad),
    )


def shards(
    inputs,
    cotangent,
    lengths,
    qkv_weight,
    qkv_bias,
    dense_weight,
    in_weight,
    in_bias,
    out_weight,
    norm_gains,
    norm_biases,
    out_biases,
):
    on_first = lax.axis_index("section") == 0
    micro = inputs.shape[0]
    shard_rows = inputs.shape[1]
    width = inputs.shape[2]
    seq_len = shard_rows * lax.axis_size("tensor")
    shard_start = lax.axis_index("tensor") * shard_rows
    weights = (
        lax.all_gather(qkv_weight[0], "dp", axis=0, tiled=True),
        lax.all_gather(qkv_bias[0], "dp", axis=1, tiled=True),
        lax.all_gather(dense_weight[0], "dp", axis=1, tiled=True),
        lax.all_gather(in_weight[0], "dp", axis=0, tiled=True),
        lax.all_gather(in_bias[0], "dp", axis=0, tiled=True),
        lax.all_gather(out_weight[0], "dp", axis=1, tiled=True),
    )
    smalls = (
        lax.all_gather(norm_gains[0], ("tensor", "dp"), axis=1, tiled=True),
        lax.all_gather(norm_biases[0], ("tensor", "dp"), axis=1, tiled=True),
        lax.all_gather(out_biases[0], ("tensor", "dp"), axis=1, tiled=True),
    )
    vectors = tuple((piece.astype(jnp.float32) for piece in smalls))

    def select(for_first, for_second):
        return jax.tree.map(
            lambda first_leaf, second_leaf: jnp.where(on_first, first_leaf, second_leaf),
            for_first,
            for_second,
        )

    zeros_in = jnp.zeros((shard_rows, width), jnp.bfloat16)
    received = zeros_in
    outputs = []
    saved = []
    for tick in range(micro + 1):
        own = inputs[tick] if tick < micro else zeros_in
        layer_in = jnp.where(on_first, own, received).astype(jnp.float32)
        length_row = jnp.where(on_first, lengths[min(tick, micro - 1)], lengths[max(tick - 1, 0)])
        result, kept = forward_layer(layer_in, length_row, weights, vectors)
        result_low = result.astype(jnp.bfloat16)
        outputs.append(result_low)
        saved.append((layer_in, length_row, kept))
        if tick < micro:
            received = from_behind(result_low, "section", 1)
    activations = jnp.stack([select(outputs[index], outputs[index + 1]) for index in range(micro)])
    returned = zeros_in
    input_rows = []
    sent_rows = []
    weight_sums = None
    vector_sums = None
    for tick in range(micro + 1):
        stored = select(saved[max(tick - 1, 0)], saved[min(tick + 1, micro)])
        layer_in = stored[0]
        length_row = stored[1]
        kept = stored[2]
        if tick < micro:
            _, _, valid = doc_layout(length_row, seq_len)
            valid_rows = lax.dynamic_slice_in_dim(valid, shard_start, shard_rows, 0)
            loss_grad = cotangent[tick].astype(jnp.float32) * valid_rows[:, None].astype(
                jnp.float32
            )
        else:
            loss_grad = jnp.zeros((shard_rows, width), jnp.float32)
        grad_out = jnp.where(on_first, returned.astype(jnp.float32), loss_grad)
        input_grad, layer_grads, vector_grads = backward_layer(
            grad_out, layer_in, kept, length_row, weights, vectors
        )
        sent = input_grad.astype(jnp.bfloat16)
        input_rows.append(input_grad)
        sent_rows.append(sent)
        weight_sums = (
            layer_grads if weight_sums is None else jax.tree.map(jnp.add, weight_sums, layer_grads)
        )
        vector_sums = (
            vector_grads
            if vector_sums is None
            else jax.tree.map(jnp.add, vector_sums, vector_grads)
        )
        if tick < micro:
            returned = from_behind(sent, "section", -1)
    grad_rows = jnp.stack(
        [
            jnp.where(on_first, input_rows[index + 1], sent_rows[index].astype(jnp.float32))
            for index in range(micro)
        ]
    )
    proj_w, proj_b, dense_g, up_w, up_b, down_w = weight_sums
    proj_w, proj_b, dense_g, up_w, up_b, down_w = (
        lax.psum_scatter(proj_w.astype(jnp.bfloat16), "dp", scatter_dimension=0, tiled=True).astype(
            jnp.float32
        ),
        lax.psum_scatter(proj_b.astype(jnp.bfloat16), "dp", scatter_dimension=1, tiled=True).astype(
            jnp.float32
        ),
        lax.psum_scatter(
            dense_g.astype(jnp.bfloat16), "dp", scatter_dimension=1, tiled=True
        ).astype(jnp.float32),
        lax.psum_scatter(up_w.astype(jnp.bfloat16), "dp", scatter_dimension=0, tiled=True).astype(
            jnp.float32
        ),
        lax.psum_scatter(up_b.astype(jnp.bfloat16), "dp", scatter_dimension=0, tiled=True).astype(
            jnp.float32
        ),
        lax.psum_scatter(down_w.astype(jnp.bfloat16), "dp", scatter_dimension=1, tiled=True).astype(
            jnp.float32
        ),
    )
    gain_total, shift_total, bias_total = (
        lax.psum_scatter(vector_sums[0], ("tensor", "dp"), scatter_dimension=1, tiled=True),
        lax.psum_scatter(vector_sums[1], ("tensor", "dp"), scatter_dimension=1, tiled=True),
        lax.psum_scatter(vector_sums[2], ("tensor", "dp"), scatter_dimension=1, tiled=True),
    )
    return (
        activations[None],
        grad_rows[None],
        proj_w[None],
        proj_b[None],
        dense_g[None],
        up_w[None],
        up_b[None],
        down_w[None],
        gain_total[None],
        shift_total[None],
        bias_total[None],
    )


def solution(mesh):
    placed = (
        P("dp", "tensor", None),
        P("dp", "tensor", None),
        P("dp", None),
        P("section", "dp", None, "tensor"),
        P("section", None, ("tensor", "dp")),
        P("section", "tensor", "dp"),
        P("section", "dp", "tensor"),
        P("section", ("tensor", "dp")),
        P("section", "tensor", "dp"),
        P("section", None, ("tensor", "dp")),
        P("section", None, ("tensor", "dp")),
        P("section", None, ("tensor", "dp")),
    )
    return jax.shard_map(
        shards,
        mesh=mesh,
        in_specs=placed,
        out_specs=(
            P("section", "dp", "tensor", None),
            P("section", "dp", "tensor", None),
            P("section", "dp", None, "tensor"),
            P("section", None, ("tensor", "dp")),
            P("section", "tensor", "dp"),
            P("section", "dp", "tensor"),
            P("section", ("tensor", "dp")),
            P("section", "tensor", "dp"),
            P("section", None, ("tensor", "dp")),
            P("section", None, ("tensor", "dp")),
            P("section", None, ("tensor", "dp")),
        ),
        check_vma=False,
    )
```

profile of v0, /device:TPU:0, one launch (start us, length us, event | category | flops | bytes accessed | tf_op | source)
XLA Modules:
  0.0 2192.1 jit_solution(10371523589155553854)
XLA Ops:
  10.9 48.3 %all-gather.1 = bf16[1,2,1024]{1,0,2:T(2,128)(2,1)S(1)} all-gather(bf16[1,2,64]{1,0,2:T(2,128)(2,1)S(1)} %copy.118), channel_id=3, replica_groups=mesh['section'=2,'tensor'=4,'dp'=4] {'tensor','dp'}, dimensions={2}, use_global_device_ids=true | all-gather | bytes 4352 | tf_op jit(solution)/shard_map/all_gather | solution.py:299
  59.8 35.3 %all-gather = bf16[1,2,1024]{1,0,2:T(2,128)(2,1)S(1)} all-gather(bf16[1,2,64]{1,0,2:T(2,128)(2,1)S(1)} %copy.117), channel_id=2, replica_groups=mesh['section'=2,'tensor'=4,'dp'=4] {'tensor','dp'}, dimensions={2}, use_global_device_ids=true | all-gather | bytes 4352 | tf_op jit(solution)/shard_map/all_gather | solution.py:298
  170.8 60.2 %while.81 = (s32[]{:T(128)}, bf16[4,512,4,64]{1,3,2,0:T(8,128)(2,1)S(1)}, f32[4,4,512]{2,1,0:T(4,128)S(1)}, s32[4]{0:T(128)S(1)}, s32[2048]{0:T(1024)S(1)}, /*in...) while((s32[]{:T(128)}, ...), condition=%wide.region_8.9_spmd, body=%wide.region_5.8_spmd.sunk | while | flops 1127348736 | bytes 61425896 | solution.py:113
  232.2 26.0 %fusion.116 = (bf16[2048,1024]{1,0:T(8,128)(2,1)}, f32[2048,1024]{1,0:T(8,128)}) fusion(f32[1024]{0:T(1024)S(1)} %bitcast.618, bf16[2048,1024]{1,0:T(8,128)(2,1)} %all-gather.24.cloned.1.call-done, bf16[1,1024,1024]{2,1,0:T(8,128)(2,1)} %all-gather.42.cloned.1.call-done), kind=kOutput, calls=%fused_computation.149 | convolution fusion | flops 4433379328 | bytes 18878464 | tf_op jit(solution)/shard_map/dot_general | solution.py:179
  290.6 35.2 %all-gather.8 = bf16[1,2,1024]{1,0,2:T(2,128)(2,1)S(1)} all-gather(bf16[1,2,64]{1,0,2:T(2,128)(2,1)S(1)} %copy.123), channel_id=10, replica_groups=mesh['section'=2,'tensor'=4,'dp'=4] {'tensor','dp'}, dimensions={2}, use_global_device_ids=true | all-gather | bytes 4352 | tf_op jit(solution)/shard_map/all_gather | solution.py:300
  370.8 32.0 %all-gather.26.cloned.1.call-done = bf16[2048,1024]{1,0:T(8,128)(2,1)} async-done(((bf16[512,1024]{1,0:T(8,128)(2,1)}), bf16[2048,1024]{1,0:T(8,128)(2,1)}) %all-gather.26.cloned.1.call-update) | async-done | bytes 4194320 | tf_op jit(solution)/shard_map/all_gather | solution.py:189
  416.7 64.2 %while.82 = (s32[]{:T(128)}, bf16[4,512,4,64]{1,3,2,0:T(8,128)(2,1)}, f32[4,4,512]{2,1,0:T(4,128)S(1)}, s32[4]{0:T(128)S(1)}, s32[2048]{0:T(1024)S(1)}, /*index=...) while((s32[]{:T(128)}, ...), condition=%wide.region_18.19_spmd, body=%wide.region_15.18_spmd.sunk | while | flops 1127348736 | bytes 57231560 | solution.py:113
  483.8 26.1 %fusion.119 = (bf16[2048,1024]{1,0:T(8,128)(2,1)S(1)}, f32[2048,1024]{1,0:T(8,128)}) fusion(f32[1024]{0:T(1024)S(1)} %bitcast.619, bf16[2048,1024]{1,0:T(8,128)(2,1)} %all-gather.28.cloned.1.call-done, bf16[1,1024,1024]{2,1,0:T(8,128)(2,1)} %all-gather.42.cloned.1.call-done), kind=kOutput, calls=%fused_computation.152 | convolution fusion | flops 4433379328 | bytes 18878464 | tf_op jit(solution)/shard_map/dot_general | solution.py:179
  520.4 248.8 %while.84 = (s32[]{:T(128)}, f32[2048,4,64]{0,2,1:T(8,128)}, f32[2048,4,64]{0,2,1:T(8,128)}, f32[4,512,4,64]{1,0,3,2:T(4,128)}, s32[4]{0:T(128)S(1)}, /*index=5*...) while((s32[]{:T(128)}, f32[2048,4,64]{0,2,1:T(8,128)}, ...), condition=%wide.region_36.37_spmd.clone, body=%wide.region_34.36_spmd.clone.sunk | while | flops 2753165824 | bytes 179120496 | solution.py:158
  789.3 27.6 %convert_reduce_fusion.2 = (f32[1024]{0:T(1024)}, bf16[2048,1024]{1,0:T(8,128)(2,1)S(1)}) fusion(bf16[2048,1024]{1,0:T(8,128)(2,1)} %all-gather.34.cloned.1.call-done, bf16[1,1024,1024]{2,1,0:T(8,128)(2,1)S(1)} %copy-done.196, f32[2048,1024]{1,0:T(8,128)} %get-tuple-element.768, f32[2048,1024]{1,0:T(8,128)} %get-tuple-element.766, f32[1024]{0:T(1024)S(1)} %bitcast.620, ...), kind=kOutput, calls=%fused_computation.176 | convolution fusion | flops 4456446976 | bytes 27271168 | tf_op jit(solution)/shard_map/sd,fd->sf/dot_general | solution.py:221
  938.6 64.4 %while.83 = (s32[]{:T(128)}, bf16[4,512,4,64]{1,3,2,0:T(8,128)(2,1)}, f32[4,4,512]{2,1,0:T(4,128)S(1)}, s32[4]{0:T(128)S(1)}, s32[2048]{0:T(1024)S(1)}, /*index=...) while((s32[]{:T(128)}, ...), condition=%wide.region_28.29_spmd, body=%wide.region_25.28_spmd.sunk | while | flops 1127348736 | bytes 61425896 | solution.py:113
  1009.8 243.0 %while.85 = (s32[]{:T(128)}, f32[2048,4,64]{0,2,1:T(8,128)}, f32[2048,4,64]{0,2,1:T(8,128)}, f32[4,512,4,64]{1,0,3,2:T(4,128)}, s32[4]{0:T(128)S(1)}, /*index=5*...) while((s32[]{:T(128)}, f32[2048,4,64]{0,2,1:T(8,128)}, ...), condition=%wide.region_50.51_spmd.clone, body=%wide.region_48.50_spmd.clone.sunk | while | flops 2753165824 | bytes 179153296 | solution.py:158
  1273.0 24.6 %fusion.122 = (bf16[2048,1024]{1,0:T(8,128)(2,1)}, f32[2048,1024]{1,0:T(8,128)S(1)}) fusion(f32[1024]{0:T(1024)S(1)} %bitcast.621, bf16[2048,1024]{1,0:T(8,128)(2,1)} %all-gather.32.cloned.1.call-done, bf16[1,1024,1024]{2,1,0:T(8,128)(2,1)S(1)} %copy-done.193), kind=kOutput, calls=%fused_computation.155 | convolution fusion | flops 4433379328 | bytes 18878464 | tf_op jit(solution)/shard_map/dot_general | solution.py:179
  1297.7 27.0 %convert_reduce_fusion.1 = (f32[1024]{0:T(1024)}, bf16[2048,1024]{1,0:T(8,128)(2,1)S(1)}) fusion(bf16[2048,1024]{1,0:T(8,128)(2,1)S(1)} %copy-done.48, bf16[1,1024,1024]{2,1,0:T(8,128)(2,1)S(1)} %copy-done.197, f32[2048,1024]{1,0:T(8,128)S(1)} %get-tuple-element.770, f32[2048,1024]{1,0:T(8,128)} %get-tuple-element.766, f32[1024]{0:T(1024)S(1)} %bitcast.622, ...), kind=kOutput, calls=%fused_computation.175 | convolution fusion | flops 4456446976 | bytes 27271168 | tf_op jit(solution)/shard_map/sd,fd->sf/dot_general | solution.py:221
  1333.7 43.7 %reduce-scatter.38.cloned.1.call-done = bf16[512,1024]{1,0:T(8,128)(2,1)} async-done(((bf16[2048,1024]{1,0:T(8,128)(2,1)}), bf16[512,1024]{1,0:T(8,128)(2,1)}) %reduce-scatter.38.cloned.1.call-update) | async-done | bytes 1048592 | tf_op jit(solution)/shard_map/reduce_scatter | solution.py:245
  1387.8 25.5 %collective-permute-done.3 = bf16[512,1024]{1,0:T(8,128)(2,1)S(1)} collective-permute-done((bf16[512,1024]{1,0:T(8,128)(2,1)S(1)}, bf16[512,1024]{1,0:T(8,128)(2,1)S(1)}, u32[]{:S(2)}, u32[]{:S(2)}) %collective-permute-start.3) | collective-permute-done | bytes 1048608 | tf_op jit(solution)/shard_map/ppermute | solution.py:19
  1472.3 251.1 %while.86 = (s32[]{:T(128)}, f32[2048,4,64]{0,2,1:T(8,128)}, f32[2048,4,64]{0,2,1:T(8,128)}, f32[4,512,4,64]{1,0,3,2:T(4,128)}, s32[4]{0:T(128)S(1)}, /*index=5*...) while((s32[]{:T(128)}, f32[2048,4,64]{0,2,1:T(8,128)}, ...), condition=%wide.region_64.65_spmd.clone, body=%wide.region_62.64_spmd.clone.sunk | while | flops 2753165824 | bytes 178858288 | solution.py:158
  1779.2 27.8 %convert_reduce_fusion = (f32[1024]{0:T(1024)S(1)}, bf16[2048,1024]{1,0:T(8,128)(2,1)}) fusion(bf16[2048,1024]{1,0:T(8,128)(2,1)} %all-gather.38.cloned.1.call-done, bf16[1,1024,1024]{2,1,0:T(8,128)(2,1)S(1)} %copy-done.199, f32[2048,1024]{1,0:T(8,128)} %copy-done.214, f32[2048,1024]{1,0:T(8,128)} %get-tuple-element.768, f32[1024]{0:T(1024)S(1)} %bitcast.623, ...), kind=kOutput, calls=%fused_computation.174 | convolution fusion | flops 4456446976 | bytes 27271168 | tf_op jit(solution)/shard_map/sd,fd->sf/dot_general | solution.py:221
  1865.6 43.3 %reduce-scatter.48.cloned.1.call-done = bf16[256,1024]{1,0:T(8,128)(2,1)} async-done(((bf16[1024,1024]{1,0:T(8,128)(2,1)}), bf16[256,1024]{1,0:T(8,128)(2,1)}) %reduce-scatter.48.cloned.1.call-update) | async-done | bytes 524304 | tf_op jit(solution)/shard_map/reduce_scatter | solution.py:378
  1911.0 44.8 %reduce-scatter.40.cloned.1.call-done = bf16[512,1024]{1,0:T(8,128)(2,1)} async-done(((bf16[2048,1024]{1,0:T(8,128)(2,1)}), bf16[512,1024]{1,0:T(8,128)(2,1)}) %reduce-scatter.40.cloned.1.call-update) | async-done | bytes 1048592 | tf_op jit(solution)/shard_map/reduce_scatter | solution.py:242
  1955.9 47.1 %reduce-scatter.42.cloned.1.call-done = bf16[512,1024]{1,0:T(8,128)(2,1)} async-done(((bf16[2048,1024]{1,0:T(8,128)(2,1)}), bf16[512,1024]{1,0:T(8,128)(2,1)}) %reduce-scatter.42.cloned.1.call-update) | async-done | bytes 1048592 | tf_op jit(solution)/shard_map/reduce_scatter | solution.py:245
  2017.2 49.5 %reduce-scatter.58.cloned.1.call-done = f32[64,2]{1,0:T(8,128)} async-done(((f32[1024,2]{1,0:T(8,128)}), f32[64,2]{1,0:T(8,128)}) %reduce-scatter.58.cloned.1.call-update) | async-done | bytes 528
  2068.1 57.4 %reduce-scatter.54.cloned.1.call-done = f32[64,2]{1,0:T(8,128)} async-done(((f32[1024,2]{1,0:T(8,128)}), f32[64,2]{1,0:T(8,128)}) %reduce-scatter.54.cloned.1.call-update) | async-done | bytes 528
  2126.9 57.1 %reduce-scatter.56.cloned.1.call-done = f32[64,2]{1,0:T(8,128)} async-done(((f32[1024,2]{1,0:T(8,128)}), f32[64,2]{1,0:T(8,128)}) %reduce-scatter.56.cloned.1.call-update) | async-done | bytes 528
  (1053 shorter events, 1454.0 us)
Async XLA Ops:
  7.2 153.5 %all-gather.40.cloned.1.call-start = ((), (), s32[]{:S(2)}) async-start(), calls=%async_computation.39 | async-start | bytes 1966080 | tf_op jit(solution)/shard_map/all_gather | solution.py:290
  9.3 151.4 %all-gather.22.cloned.1.call-start = ((), (), s32[]{:S(2)}) async-start(), calls=%async_computation.17 | async-start | bytes 5242880 | tf_op jit(solution)/shard_map/all_gather | solution.py:189
  113.0 119.1 %all-gather.42.cloned.1.call-start = ((), (), s32[]{:S(2)}) async-start(), calls=%async_computation.40 | async-start | bytes 2621440 | tf_op jit(solution)/shard_map/all_gather | solution.py:293
  113.8 118.4 %all-gather.24.cloned.1.call-start = ((), (), s32[]{:S(2)}) async-start(), calls=%async_computation.18 | async-start | bytes 5242880 | tf_op jit(solution)/shard_map/all_gather | solution.py:190
  114.4 160.6 %all-gather.44.cloned.1.call-start = ((), (), s32[]{:S(2)}) async-start(), calls=%async_computation.41 | async-start | bytes 2621440 | tf_op jit(solution)/shard_map/all_gather | solution.py:295
  114.9 218.7 %reduce-scatter.26.cloned.1.call-start = ((), (), s32[]{:S(2)}) async-start(), calls=%async_computation.19 | async-start | bytes 5242880 | tf_op jit(solution)/shard_map/reduce_scatter | solution.py:202
  290.4 112.3 %all-gather.26.cloned.1.call-start = ((), (), s32[]{:S(2)}) async-start(), calls=%async_computation.20 | async-start | bytes 5242880 | tf_op jit(solution)/shard_map/all_gather | solution.py:189
  361.6 122.1 %all-gather.28.cloned.1.call-start = ((), (), s32[]{:S(2)}) async-start(), calls=%async_computation.21 | async-start | bytes 5242880 | tf_op jit(solution)/shard_map/all_gather | solution.py:190
  370.5 455.3 %reduce-scatter.28.cloned.1.call-start = ((), (), s32[]{:S(2)}) async-start(), calls=%async_computation.22 | async-start | bytes 5242880 | tf_op jit(solution)/shard_map/reduce_scatter | solution.py:202
  518.0 340.8 %reduce-scatter.32.cloned.1.call-start = ((), (), s32[]{:S(2)}) async-start(), calls=%async_computation.27 | async-start | bytes 5242880 | tf_op jit(solution)/shard_map/reduce_scatter | solution.py:242
  886.9 116.7 %all-gather.36.cloned.1.call-start = ((), (), s32[]{:S(2)}) async-start(), calls=%async_computation.29 | async-start | bytes 5242880 | tf_op jit(solution)/shard_map/all_gather | solution.py:215
  921.0 350.5 %all-gather.32.cloned.1.call-start = ((), (), s32[]{:S(2)}) async-start(), calls=%async_computation.24 | async-start | bytes 5242880 | tf_op jit(solution)/shard_map/all_gather | solution.py:190
  921.6 412.1 %reduce-scatter.36.cloned.1.call-start = ((), (), s32[]{:S(2)}) async-start(), calls=%async_computation.30 | async-start | bytes 5242880 | tf_op jit(solution)/shard_map/reduce_scatter | solution.py:242
  1333.1 133.0 %all-gather.38.cloned.1.call-start = ((), (), s32[]{:S(2)}) async-start(), calls=%async_computation.32 | async-start | bytes 5242880 | tf_op jit(solution)/shard_map/all_gather | solution.py:215
  1415.5 418.8 %reduce-scatter.30.cloned.1.call-start = ((), (), s32[]{:S(2)}) async-start(), calls=%async_computation.25 | async-start | bytes 5242880 | tf_op jit(solution)/shard_map/reduce_scatter | solution.py:202
  1451.6 398.7 %reduce-scatter.52.cloned.1.call-start = ((), (), s32[]{:S(2)}) async-start(), calls=%async_computation.42 | async-start | bytes 81920
  1739.2 112.4 %reduce-scatter.46.cloned.1.call-start = ((), (), s32[]{:S(2)}) async-start(), calls=%async_computation.36 | async-start | bytes 655360 | tf_op jit(solution)/shard_map/reduce_scatter | solution.py:375
  1753.8 109.8 %reduce-scatter.50.cloned.1.call-start = ((), (), s32[]{:S(2)}) async-start(), calls=%async_computation.38 | async-start | bytes 2621440 | tf_op jit(solution)/shard_map/reduce_scatter | solution.py:384
  1779.0 129.9 %reduce-scatter.48.cloned.1.call-start = ((), (), s32[]{:S(2)}) async-start(), calls=%async_computation.37 | async-start | bytes 2621440 | tf_op jit(solution)/shard_map/reduce_scatter | solution.py:378
  1815.4 140.5 %reduce-scatter.40.cloned.1.call-start = ((), (), s32[]{:S(2)}) async-start(), calls=%async_computation.33 | async-start | bytes 5242880 | tf_op jit(solution)/shard_map/reduce_scatter | solution.py:242
  1821.8 181.1 %reduce-scatter.42.cloned.1.call-start = ((), (), s32[]{:S(2)}) async-start(), calls=%async_computation.34 | async-start | bytes 5242880 | tf_op jit(solution)/shard_map/reduce_scatter | solution.py:245
  1832.4 234.3 %reduce-scatter.58.cloned.1.call-start = ((), (), s32[]{:S(2)}) async-start(), calls=%async_computation.45 | async-start | bytes 557056
  2010.8 114.7 %reduce-scatter.54.cloned.1.call-start = ((), (), s32[]{:S(2)}) async-start(), calls=%async_computation.43 | async-start | bytes 557056
  2011.9 172.0 %reduce-scatter.56.cloned.1.call-start = ((), (), s32[]{:S(2)}) async-start(), calls=%async_computation.44 | async-start | bytes 557056
  (254 other events, 4400.0 us)
Sparse Core Ops, SparseCore 0:
  10.2 47.5 all-gather.39
  146.1 46.1 all-gather.41
  228.8 46.1 all-gather.43
  285.5 44.8 reduce-scatter.25
  332.0 33.9 all-gather.33
  368.2 34.4 all-gather.25
  404.4 34.4 all-gather.27
  518.1 44.4 reduce-scatter.27
  787.9 44.6 reduce-scatter.31
  835.1 44.5 reduce-scatter.33
  887.0 34.4 all-gather.29
  923.0 34.4 all-gather.35
  958.9 34.4 all-gather.31
  1271.6 44.1 reduce-scatter.35
  1333.2 44.1 reduce-scatter.37
  1415.6 33.5 all-gather.37
  1451.8 45.2 reduce-scatter.29
  1820.4 43.1 reduce-scatter.49
  1865.8 43.1 reduce-scatter.47
  1912.0 43.7 reduce-scatter.39
  1958.4 44.5 reduce-scatter.41
  2010.9 55.7 reduce-scatter.57
  2070.7 54.7 reduce-scatter.53
  2129.1 54.8 reduce-scatter.55
  (5 shorter events, 137.5 us)
where the time goes:
time: 2210 us; the launch traced here: 2190 us
  matrix products  849 us (38%)
  waiting for transfers between devices  520 us (24%)
  other arithmetic  324 us (15%)
  local copies, waits for them, and re-layouts  259 us (12%)
  blocking collectives  168 us (8%)
  loops' own time  41.9 us (2%)
    unnamed x33, waiting for transfers between devices  167 us
    dynamic_update_slice x24, local copies, waits for them, and re-layouts, attend_back(): lax.scan(backward_block, (empty, empty), jnp.arange(seq_len // QBLK, dtyp...  140 us
    dot_general x12, matrix products, backward_block(): jnp.einsum('qhd,khd->hqk', grad_block, values_all, preferred_element_type...  137 us
    convert_element_type x12, other arithmetic, backward_block(): score_grad = (probs * (prob_grad - delta)).astype(jnp.bfloat16)  131 us
    reduce_scatter x3, waiting for transfers between devices, backward_layer(): lax.psum_scatter(second_grad.astype(jnp.bfloat16), 'tensor', scatter_dime...  112 us
    ppermute x4, waiting for transfers between devices, from_behind(): return lax.ppermute(block, axis, route)  91.7 us
    dot_general x12, matrix products, backward_block(): jnp.einsum('hqk,qhd->khd', probs.astype(jnp.bfloat16), grad_block, prefer...  90.5 us
    dot_general x3, matrix products, backward_layer(): jnp.einsum('sd,fd->sf', grad_all, out_w, preferred_element_type=jnp.float32)  82.4 us
  transfers between devices with their start and end apart: 33, of which 16 were waited for; matrix products, arithmetic and copies ran while one was open for 61% of the time, Pallas kernels for 0%

commit v1 on v0

v1 whole, which is shorter than its diff:
```python
import functools
import math

import jax
import jax.numpy as jnp
from jax import lax
from jax.experimental import pallas as pl
from jax.experimental.pallas import tpu as pltpu
from jax.sharding import PartitionSpec as P

HDIM = 64
EPSILON = 1e-05
TILE = 256
NT = (((1,), (1,)), ((), ()))
NN = (((1,), (0,)), ((), ()))
TN = (((0,), (0,)), ((), ()))
LOG2E = math.log2(math.e)
FAR = 1e15
HURRY = 0.05
LIMIT = pltpu.CompilerParams(vmem_limit_bytes=28 * 2**20)


def mm(a, b, dims=NN):
    return lax.dot_general(a, b, dims, preferred_element_type=jnp.float32)


def cost(flops, moved, special=0):
    return pl.CostEstimate(flops=int(flops * HURRY), bytes_accessed=int(moved * HURRY), transcendentals=int(special))


def flip(block, axis, bit=1):
    return lax.ppermute(block, axis, [(i, i ^ bit) for i in range(lax.axis_size(axis))])


def turn(values, cosine, lead, trail):
    return values * cosine + pltpu.roll(values, 120, 1) * lead + pltpu.roll(values, 8, 1) * trail


def turn_back(grads, cosine, lead, trail):
    return grads * cosine - pltpu.roll(grads, 120, 1) * lead - pltpu.roll(grads, 8, 1) * trail


def spot(table, tile, shard_rows):
    per = shard_rows // TILE
    return pl.multiple_of(table[tile // per] * shard_rows + (tile % per) * TILE, TILE)


def head_part(block, head):
    lane = lax.broadcasted_iota(jnp.int32, block.shape, 1)
    return jnp.where((lane >= head * 64) & (lane < head * 64 + 64), block, jnp.zeros_like(block))


def attend_kernel(shard_rows, tiles, table, q_ref, k_ref, v_ref, fq_ref, fk_ref, out_ref, lse_ref, vt):
    step = pl.program_id(0)

    @pl.when(step == 0)
    def _():
        flipped = v_ref[...].T
        for head in range(2):
            vt[head, 0:64, :] = flipped[head * 64 : head * 64 + 64, :]
            vt[head, 64:80, :] = jnp.ones((16, flipped.shape[1]), jnp.bfloat16)

    def body(last):
        query = q_ref[...]
        feats = fq_ref[...]
        outs = []
        for head in range(2):
            wide = jnp.concatenate([head_part(query, head), feats], 1)
            scores = []
            for tile in range(last + 1):
                at = spot(table, tile, shard_rows)
                keys = jnp.concatenate([k_ref[pl.ds(at, TILE), :], fk_ref[pl.ds(at, TILE), :]], 1)
                block = mm(keys, wide, NT)
                if tile == last:
                    rows = lax.broadcasted_iota(jnp.int32, block.shape, 0)
                    cols = lax.broadcasted_iota(jnp.int32, block.shape, 1)
                    block = jnp.where(rows <= cols, block, -1e30)
                scores.append(block)
            top = jnp.max(scores[0], 0, keepdims=True)
            for block in scores[1:]:
                top = jnp.maximum(top, jnp.max(block, 0, keepdims=True))
            shift = top * LOG2E
            total = None
            for tile in range(last + 1):
                at = spot(table, tile, shard_rows)
                probs = jnp.exp2(scores[tile] * LOG2E - shift).astype(jnp.bfloat16)
                term = mm(vt[head, :, pl.ds(at, TILE)], probs, NN)
                total = term if total is None else total + term
            norm = total[64:65, :]
            outs.append(total[0:64, :] / norm)
            lse_ref[head : head + 1, :] = shift + jnp.log2(norm)
        lse_ref[2:8, :] = jnp.zeros((6, TILE), jnp.float32)
        both = jnp.concatenate(outs, 0)
        out_ref[...] = both.T.astype(jnp.bfloat16)

    for last in range(tiles):
        pl.when(step == last)(functools.partial(body, last))


def attend(table, qkv, fq, fk):
    seq = qkv.shape[0]
    shard_rows = seq // 4
    tiles = seq // TILE
    per = shard_rows // TILE

    def place(step, table):
        return table[step // per] * per + step % per

    return pl.pallas_call(
        functools.partial(attend_kernel, shard_rows, tiles),
        grid_spec=pltpu.PrefetchScalarGridSpec(
            num_scalar_prefetch=1,
            grid=(tiles,),
            in_specs=[
                pl.BlockSpec((TILE, 128), lambda i, t: (place(i, t), 0)),
                pl.BlockSpec((seq, 128), lambda i, t: (0, 1)),
                pl.BlockSpec((seq, 128), lambda i, t: (0, 2)),
                pl.BlockSpec((TILE, 128), lambda i, t: (place(i, t), 0)),
                pl.BlockSpec((seq, 128), lambda i, t: (0, 0)),
            ],
            out_specs=[
                pl.BlockSpec((TILE, 128), lambda i, t: (place(i, t), 0)),
                pl.BlockSpec((8, TILE), lambda i, t: (0, place(i, t))),
            ],
            scratch_shapes=[pltpu.VMEM((2, 80, seq), jnp.bfloat16)],
        ),
        out_shape=[
            jax.ShapeDtypeStruct((seq, 128), jnp.bfloat16),
            jax.ShapeDtypeStruct((8, seq), jnp.float32),
        ],
        compiler_params=LIMIT,
        cost_estimate=cost(4e9, 3e6, 5e6),
        name="attend",
    )(table, qkv, qkv, qkv, fq, fk)


def attend_back_kernel(shard_rows, tiles, table, q_ref, k_ref, v_ref, gm_ref, o_ref, lse_ref, fq_ref, fk_ref,
                       cos_ref, lead_ref, trail_ref, out_ref, kt, dk, dv):
    step = pl.program_id(0)

    @pl.when(step == 0)
    def _():
        kt[...] = k_ref[...].T
        dk[...] = jnp.zeros_like(dk)
        dv[...] = jnp.zeros_like(dv)

    def body(last):
        here = spot(table, last, shard_rows)
        query = q_ref[...]
        feats = fq_ref[...]
        grad = gm_ref[...]
        product = grad.astype(jnp.float32) * o_ref[...].astype(jnp.float32)
        high = product.astype(jnp.bfloat16)
        low = (product - high.astype(jnp.float32)).astype(jnp.bfloat16)
        lane = lax.broadcasted_iota(jnp.int32, (8, 128), 1)
        wides, grads, shifts, deltas, queries = [], [], [], [], []
        for head in range(2):
            ones = jnp.where((lane >= head * 64) & (lane < head * 64 + 64), 1.0, 0.0).astype(jnp.bfloat16)
            deltas.append((mm(ones, high, NT) + mm(ones, low, NT))[0:1, :])
            queries.append(head_part(query, head))
            wides.append(jnp.concatenate([queries[head], feats], 1))
            grads.append(head_part(grad, head))
            shifts.append(lse_ref[head : head + 1, :])
        turned = [None, None]
        for tile in range(last + 1):
            at = spot(table, tile, shard_rows)
            keys = jnp.concatenate([k_ref[pl.ds(at, TILE), :], fk_ref[pl.ds(at, TILE), :]], 1)
            values = v_ref[pl.ds(at, TILE), :]
            dk_term = dv_term = None
            for head in range(2):
                block = mm(keys, wides[head], NT)
                probs = jnp.exp2(block * LOG2E - shifts[head])
                if tile == last:
                    rows = lax.broadcasted_iota(jnp.int32, block.shape, 0)
                    cols = lax.broadcasted_iota(jnp.int32, block.shape, 1)
                    probs = jnp.where(rows <= cols, probs, 0.0)
                back = mm(values, grads[head], NT)
                slope = (probs * (back - deltas[head])).astype(jnp.bfloat16)
                dv_one = mm(probs.astype(jnp.bfloat16), grads[head], NN)
                dk_one = mm(slope, queries[head], NN)
                dv_term = dv_one if head == 0 else dv_term + dv_one
                dk_term = dk_one if head == 0 else dk_term + dk_one
                dq = mm(kt[head * 64 : head * 64 + 64, pl.ds(at, TILE)], slope, NN)
                turned[head] = dq if tile == 0 else turned[head] + dq
            dv[pl.ds(at, TILE), :] += dv_term
            dk[pl.ds(at, TILE), :] += dk_term
        dq = jnp.concatenate(turned, 0).T * 0.125
        dq = turn_back(dq, cos_ref[pl.ds(here, TILE), :], lead_ref[pl.ds(here, TILE), :], trail_ref[pl.ds(here, TILE), :])
        out_ref[pl.ds(here, TILE), 0:128] = dq.astype(jnp.bfloat16)

    for last in range(tiles):
        pl.when(step == last)(functools.partial(body, last))

    @pl.when(step == tiles - 1)
    def _():
        def finish(block, carry):
            rows = pl.ds(pl.multiple_of(block * TILE, TILE), TILE)
            turned = turn_back(dk[rows, :], cos_ref[rows, :], lead_ref[rows, :], trail_ref[rows, :])
            out_ref[rows, 128:256] = turned.astype(jnp.bfloat16)
            out_ref[rows, 256:384] = dv[rows, :].astype(jnp.bfloat16)
            return carry

        lax.fori_loop(0, tiles, finish, 0)


def attend_back(table, qkv, grad_mixed, mixed, lse, fq, fk, turns):
    seq = qkv.shape[0]
    shard_rows = seq // 4
    tiles = seq // TILE
    per = shard_rows // TILE

    def place(step, table):
        return table[step // per] * per + step % per

    whole = pl.BlockSpec((seq, 128), lambda i, t: (0, 0))
    block = pl.BlockSpec((TILE, 128), lambda i, t: (place(i, t), 0))
    return pl.pallas_call(
        functools.partial(attend_back_kernel, shard_rows, tiles),
        grid_spec=pltpu.PrefetchScalarGridSpec(
            num_scalar_prefetch=1,
            grid=(tiles,),
            in_specs=[
                block,
                pl.BlockSpec((seq, 128), lambda i, t: (0, 1)),
                pl.BlockSpec((seq, 128), lambda i, t: (0, 2)),
                block,
                block,
                pl.BlockSpec((8, TILE), lambda i, t: (0, place(i, t))),
                block,
                whole,
                whole,
                whole,
                whole,
            ],
            out_specs=pl.BlockSpec((seq, 384), lambda i, t: (0, 0)),
            scratch_shapes=[
                pltpu.VMEM((128, seq), jnp.bfloat16),
                pltpu.VMEM((seq, 128), jnp.float32),
                pltpu.VMEM((seq, 128), jnp.float32),
            ],
        ),
        out_shape=jax.ShapeDtypeStruct((seq, 384), jnp.bfloat16),
        compiler_params=LIMIT,
        cost_estimate=cost(10e9, 6e6, 5e6),
        name="attend_back",
    )(table, qkv, qkv, qkv, grad_mixed, mixed, lse, fq, fk, *turns)


def normal_of(values):
    centered = values - jnp.mean(values, -1, keepdims=True)
    inverse = lax.rsqrt(jnp.mean(centered * centered, -1, keepdims=True) + EPSILON)
    return centered * inverse, inverse


def whole_of(array):
    return pl.BlockSpec(array.shape, lambda *i: (0,) * array.ndim)


def heads_of(first, weight, bias, turns, out_ref):
    projected = mm(first, weight) + bias
    for part in range(3):
        piece = projected[:, 128 * part : 128 * part + 128]
        if part < 2:
            piece = turn(piece, *turns)
        if part == 0:
            piece = piece * 0.125
        out_ref[:, 128 * part : 128 * part + 128] = piece.astype(jnp.bfloat16)


def settle(slots, source, target, start=0):
    @pl.when(pl.program_id(0) == 0)
    def _():
        rows = target.shape[0] // source.shape[0]
        for block in range(source.shape[0]):
            target[block * rows : block * rows + rows, :] = source[slots[block], 0:rows, start : start + target.shape[1]]


def weight_scratch(width, weight, cols=None):
    return pltpu.VMEM((width, cols or weight.shape[2]), weight.dtype)


def choose(pieces, target):
    for step, piece in enumerate(pieces):

        @pl.when(pl.program_id(0) == step)
        def _():
            target[...] = piece[...]


def call(kernel, name, grid, in_specs, out_specs, out_shape, scratch, flops, moved, special=0, scalars=1, aliases=None):
    return pl.pallas_call(
        kernel,
        grid_spec=pltpu.PrefetchScalarGridSpec(
            num_scalar_prefetch=scalars, grid=grid, in_specs=in_specs, out_specs=out_specs, scratch_shapes=scratch
        ),
        out_shape=out_shape,
        compiler_params=LIMIT,
        cost_estimate=cost(flops, moved, special),
        input_output_aliases=aliases or {},
        name=name,
    )


def struct(*shape):
    return jax.ShapeDtypeStruct(shape, jnp.bfloat16)


def project_kernel(
    slots, h0, h1, h2, h3, weight_ref, bias_ref, norm_ref, cos_ref, lead_ref, trail_ref,
    out_ref, first_ref, second_ref, flip_ref, weight, h_ref
):
    settle(slots, weight_ref, weight)
    choose((h0, h1, h2, h3), h_ref)
    normal, _ = normal_of(h_ref[...].astype(jnp.float32))
    flip_ref[...] = normal.astype(jnp.bfloat16).T
    first = (normal * norm_ref[0:1, :] + norm_ref[2:3, :]).astype(jnp.bfloat16)
    first_ref[...] = first
    second_ref[...] = (normal * norm_ref[1:2, :] + norm_ref[3:4, :]).astype(jnp.bfloat16)
    heads_of(first, weight[...], bias_ref[0:1, 0 : weight.shape[1]], (cos_ref[...], lead_ref[...], trail_ref[...]), out_ref)


def project(slots, pieces, weight, cols, bias, norms, turns):
    rows, width = pieces[0].shape
    seq = rows * len(pieces)
    block = pl.BlockSpec((rows, width), lambda i, s: (i, 0))
    return call(
        project_kernel,
        "project",
        (seq // rows,),
        [whole_of(x) for x in (*pieces, weight, bias, norms)] + [pl.BlockSpec((rows, 128), lambda i, s: (i, 0))] * 3,
        [pl.BlockSpec((rows, cols), lambda i, s: (i, 0)), block, block, pl.BlockSpec((width, rows), lambda i, s: (0, i))],
        [struct(seq, cols), struct(seq, width), struct(seq, width), struct(width, seq)],
        [weight_scratch(width, weight, cols), pltpu.VMEM((rows, width), jnp.bfloat16)],
        4e9,
        18e6,
    )(slots, *pieces, weight, bias, norms, *turns)


def project_more_kernel(slots, first_ref, weight_ref, bias_ref, cos_ref, lead_ref, trail_ref, out_ref, weight):
    settle(slots, weight_ref, weight)
    heads_of(
        first_ref[...], weight[...], bias_ref[1:2, 0 : weight.shape[1]], (cos_ref[...], lead_ref[...], trail_ref[...]), out_ref
    )


def project_more(slots, first, weight, cols, bias, turns):
    seq, width = first.shape
    rows = 512
    return call(
        project_more_kernel,
        "project_more",
        (seq // rows,),
        [pl.BlockSpec((rows, width), lambda i, s: (i, 0)), whole_of(weight), whole_of(bias)]
        + [pl.BlockSpec((rows, 128), lambda i, s: (i, 0))] * 3,
        pl.BlockSpec((rows, cols), lambda i, s: (i, 0)),
        struct(seq, cols),
        [weight_scratch(width, weight, cols)],
        3e9,
        8e6,
    )(slots, first, weight, bias, *turns)


def gelu_kernel(part, slots, a_ref, weight_ref, bias_ref, out_ref, slope_ref, weight):
    settle(slots, weight_ref, weight, weight_ref.shape[2] - weight.shape[1])
    inner = mm(a_ref[...], weight[...]) + bias_ref[part : part + 1, bias_ref.shape[1] - weight.shape[1] :]
    size = jnp.abs(inner)
    t = 1.0 / (1.0 + (0.3275911 * math.sqrt(0.5)) * size)
    bell = jnp.exp2((-0.5 * LOG2E) * inner * inner)
    poly = 0.5 * 1.061405429 * t + 0.5 * -1.453152027
    poly = poly * t + 0.5 * 1.421413741
    poly = poly * t + 0.5 * -0.284496736
    poly = poly * t + 0.5 * 0.254829592
    tail = poly * t * bell
    below = jnp.where(inner >= 0, 1.0 - tail, tail)
    out_ref[...] = (inner * below).astype(jnp.bfloat16)
    slope_ref[...] = (below + inner * bell * (1.0 / math.sqrt(2 * math.pi))).astype(jnp.bfloat16)


def gelu_up(slots, second, weight, cols, bias, part):
    seq, width = second.shape
    rows = 256
    block = pl.BlockSpec((rows, cols), lambda i, s: (i, 0))
    return call(
        functools.partial(gelu_kernel, part),
        "gelu_up",
        (seq // rows,),
        [pl.BlockSpec((rows, width), lambda i, s: (i, 0)), whole_of(weight), whole_of(bias)],
        [block, block],
        [struct(seq, cols), struct(seq, cols)],
        [weight_scratch(width, weight, cols)],
        5e9,
        10e6,
        2e6,
    )(slots, second, weight, bias)


def deal(value, *targets):
    for step, target in enumerate(targets):

        @pl.when(pl.program_id(0) == step)
        def _():
            target[...] = value


def down_kernel(slots, mixed_mine, mixed_other, act_mine, act_other, mine_ref, other_ref, near_ref, beside_ref, mine, other):
    settle(slots, mine_ref, mine)
    settle(slots, other_ref, other)
    heads = mixed_mine.shape[1]
    total = mm(mixed_mine[...], mine[:, 0:heads], NT) + mm(act_mine[...], mine[:, heads:], NT)
    total += mm(mixed_other[...], other[:, 0:heads], NT) + mm(act_other[...], other[:, heads:], NT)
    deal(total.astype(jnp.bfloat16), near_ref, beside_ref)


def down(slots, mixed, act, weights, half):
    seq = mixed[0].shape[0]
    width = weights[0].shape[0] * weights[0].shape[1]
    rows = 512
    steps = seq // rows // 2
    return call(
        down_kernel,
        "down",
        (steps,),
        [pl.BlockSpec((rows, x.shape[1]), lambda i, s: (i + half * steps, 0)) for x in (*mixed, *act)]
        + [whole_of(w) for w in weights],
        [pl.BlockSpec((rows, width), lambda i, s: (0, 0))] * 2,
        [struct(rows, width)] * 2,
        [weight_scratch(width, w) for w in weights],
        4e9,
        8e6,
    )(slots, *mixed, *act, *weights)


def down_back_kernel(
    slots, g0, g1, g2, g3, slope_mine, slope_other, mine_ref, other_ref,
    mixed_mine, mixed_other, inner_mine, inner_other, flip_ref, mine, other, grad_ref
):
    choose((g0, g1, g2, g3), grad_ref)
    settle(slots, mine_ref, mine)
    settle(slots, other_ref, other)
    heads = mixed_mine.shape[1]
    flip_ref[...] = grad_ref[...].T
    for slope, weight, mixed, inner in (
        (slope_mine, mine, mixed_mine, inner_mine),
        (slope_other, other, mixed_other, inner_other),
    ):
        mixed[...] = mm(grad_ref[...], weight[:, 0:heads]).astype(jnp.bfloat16)
        inner[...] = (mm(grad_ref[...], weight[:, heads:]) * slope[...].astype(jnp.float32)).astype(jnp.bfloat16)


def down_back(slots, pieces, slopes, weights, heads):
    rows, width = pieces[0].shape
    seq = rows * len(pieces)
    hidden = slopes[0].shape[1]
    wide = pl.BlockSpec((rows, hidden), lambda i, s: (i, 0))
    return call(
        down_back_kernel,
        "down_back",
        (seq // rows,),
        [whole_of(x) for x in pieces] + [wide, wide] + [whole_of(w) for w in weights],
        [pl.BlockSpec((rows, heads), lambda i, s: (i, 0))] * 2 + [wide, wide, pl.BlockSpec((width, rows), lambda i, s: (0, i))],
        [struct(seq, heads)] * 2 + [struct(seq, hidden)] * 2 + [struct(width, seq)],
        [weight_scratch(width, w) for w in weights] + [pltpu.VMEM((rows, width), jnp.bfloat16)],
        8e9,
        18e6,
    )(slots, *pieces, *slopes, *weights)


def up_back_kernel(
    slots, proj_mine, proj_other, inner_mine, inner_other, qkv_mine, qkv_other, in_mine, in_other, gain_ref, near_ref, beside_ref, *weights
):
    for source, target in zip((qkv_mine, qkv_other), weights[:2]):
        settle(slots, source, target)
    for source, target in zip((in_mine, in_other), weights[2:]):
        settle(slots, source, target, source.shape[2] - target.shape[1])
    qkv_a, qkv_b, in_a, in_b = weights
    first = mm(proj_mine[...], qkv_a[...], NT) + mm(proj_other[...], qkv_b[...], NT)
    second = mm(inner_mine[...], in_a[...], NT) + mm(inner_other[...], in_b[...], NT)
    deal((first * gain_ref[0:1, :] + second * gain_ref[1:2, :]).astype(jnp.bfloat16), near_ref, beside_ref)


def up_back(slots, proj, inner, qkv_w, in_w, gains, half):
    seq = proj[0].shape[0]
    width = gains.shape[1]
    rows = 512
    steps = seq // rows // 2
    return call(
        up_back_kernel,
        "up_back",
        (steps,),
        [pl.BlockSpec((rows, x.shape[1]), lambda i, s: (i + half * steps, 0)) for x in (*proj, *inner)]
        + [whole_of(w) for w in (*qkv_w, *in_w, gains)],
        [pl.BlockSpec((rows, width), lambda i, s: (0, 0))] * 2,
        [struct(rows, width)] * 2,
        [weight_scratch(width, w, x.shape[1]) for w, x in zip((*qkv_w, *in_w), (*proj, *inner))],
        4e9,
        10e6,
    )(slots, *proj, *inner, *qkv_w, *in_w, gains)


def grads_kernel(ups, downs, adds, slots, *refs):
    refs = list(refs)
    normal = refs.pop(0) if ups else None
    flipped = refs.pop(0) if downs else None
    backs = [refs.pop(0) for _ in range(ups)]
    sources = [refs.pop(0) for _ in range(downs)]
    weights = [refs.pop(0) for _ in range(ups)]
    norm_ref = refs.pop(0)
    got_ref = refs.pop(0) if adds else None
    out_ref = refs.pop(0)
    row = 1 if downs else 0
    norm = norm_ref[...].T
    gain_column, bias_column = norm[:, row : row + 1], norm[:, 2 + row : 3 + row]

    def store(first, last, value):
        if adds:
            value += got_ref[0, :, first:last].astype(jnp.float32)
        out_ref[0, :, first:last] = value.astype(jnp.bfloat16)

    at = 0
    for k in range(ups):
        stat_ref, sum_ref = refs[2 * k : 2 * k + 2]
        cols = backs[k].shape[1]
        raw = mm(normal[...], backs[k][...])
        total = mm(jnp.ones((8, backs[k].shape[0]), jnp.bfloat16), backs[k][...])
        sum_ref[...] = total
        total = total[0:1, :]
        store(at, at + cols, raw * gain_column + total * bias_column)
        first = weights[k].shape[2] - cols if downs else 0
        wide = weights[k][0, :, first : first + cols].astype(jnp.float32)
        lane = lax.broadcasted_iota(jnp.int32, stat_ref.shape, 1)
        gain = jnp.sum(raw * wide, 1, keepdims=True)
        shift = jnp.sum(wide * total, 1, keepdims=True)
        stat_ref[...] = jnp.where(lane == 0, gain, jnp.where(lane == 1, shift, 0.0))
        at += cols
    for source in sources:
        cols = source.shape[1]
        store(at, at + cols, mm(flipped[...], source[...]))
        at += cols


def weight_grads(slots, normal, flipped, ups, downs, norms, got=None):
    width, seq = (normal if ups else flipped).shape
    groups = 4
    rows = width // groups
    strip = pl.BlockSpec((rows, seq), lambda i, s: (i, 0))
    args, specs = [], []
    for array, used in ((normal, ups), (flipped, downs)):
        if used:
            args.append(array)
            specs.append(strip)
    for array in [back for back, _ in ups] + list(downs):
        args.append(array)
        specs.append(whole_of(array))
    for _, weight in ups:
        args.append(weight)
        specs.append(pl.BlockSpec((1, rows, weight.shape[2]), lambda i, s: (s[i], 0, 0)))
    args.append(norms)
    specs.append(pl.BlockSpec((norms.shape[0], rows), lambda i, s: (0, i)))
    cols = sum(back.shape[1] for back, _ in ups) + sum(source.shape[1] for source in downs)
    out_specs = [pl.BlockSpec((1, rows, cols), lambda i, s: (i, 0, 0))]
    if got is not None:
        args.append(got)
        specs.append(out_specs[0])
    out_shape = [struct(groups, rows, cols)]
    for back, _ in ups:
        out_specs += [pl.BlockSpec((rows, 8), lambda i, s: (i, 0)), pl.BlockSpec((8, back.shape[1]), lambda i, s: (0, 0))]
        out_shape += [jax.ShapeDtypeStruct((width, 8), jnp.float32), jax.ShapeDtypeStruct((8, back.shape[1]), jnp.float32)]
    return call(
        functools.partial(grads_kernel, len(ups), len(downs), got is not None),
        "weight_grads",
        (groups,),
        specs,
        out_specs,
        out_shape,
        [],
        2 * seq * width * cols,
        8e6,
    )(slots, *args)


def shards(
    inputs,
    cotangent,
    lengths,
    qkv_weight,
    qkv_bias,
    dense_weight,
    in_weight,
    in_bias,
    out_weight,
    norm_gains,
    norm_biases,
    out_biases,
):
    f32, bf16 = jnp.float32, jnp.bfloat16
    lefthand = lax.axis_index("section") == 0
    me, depth = lax.axis_index("tensor"), lax.axis_index("dp")
    n_tensor, n_dp = lax.axis_size("tensor"), lax.axis_size("dp")
    shard_rows, width = inputs.shape[1:]
    heads = qkv_weight.shape[3]
    hidden = in_weight.shape[2]
    groups = 4
    direct = n_dp == groups

    def pick(first, second):
        return jnp.where(lefthand, first, second)

    def ordered(mine, other):
        return pick(mine, other), pick(other, mine)

    steps = jnp.arange(groups, dtype=jnp.int32)
    slots = (depth - steps) % groups if direct else steps

    def gather_deep(piece):
        if not direct:
            return lax.all_gather(piece, "dp", axis=0, tiled=True).reshape(groups, -1, piece.shape[1])
        pieces = [piece]
        for hop in range(1, n_dp):
            pieces.append(lax.ppermute(piece, "dp", [(i, (i + hop) % n_dp) for i in range(n_dp)]))
        return jnp.stack(pieces)

    def scatter_late(total):
        return lax.psum_scatter(total.reshape(-1, total.shape[2]), "dp", scatter_dimension=0, tiled=True)

    def pin(*values):
        return lax.optimization_barrier(values)

    h_own = pick(inputs[0], inputs[1])
    cot = pick(cotangent[0], cotangent[1])
    row = pick(lengths[0], lengths[1])

    def halves(group):
        return pick(group[0], group[1]), pick(group[1], group[0])

    def cut(array, axis, k):
        size = array.shape[axis] // 2
        return lax.slice_in_dim(array, k * size, k * size + size, axis=axis)

    small = jnp.concatenate([piece[0].reshape(-1) for piece in (qkv_bias, norm_gains, norm_biases, out_biases, in_bias)])
    part = qkv_bias.shape[2]
    n_small = small.shape[0]
    qkv_cols, in_cols = 3 * heads // 2, hidden // 2
    qkv_half = halves([cut(qkv_weight[0], 2, k).reshape(-1, qkv_cols) for k in range(2)])
    qkv_got = flip(qkv_half[1], "section")
    pair = jnp.stack([small, flip(small, "tensor", 2)])
    h_own, pair = pin(h_own, pair)
    h_far = flip(h_own, "tensor", 2)
    pair = jnp.stack([pair, flip(pair, "tensor", 1)], 1)
    pair = jnp.stack(ordered(pair, flip(pair, "section"))).reshape(-1)
    extra = -(-pair.shape[0] // (16 * qkv_cols)) * 16
    pair = jnp.zeros((extra * qkv_cols,), bf16).at[: pair.shape[0]].set(pair).reshape(extra, qkv_cols)
    deep = qkv_half[0].shape[0]
    qkv_shard = ordered(qkv_half[0], qkv_got)
    rest_half = halves(
        [
            jnp.concatenate([cut(in_weight[0], 1, k), cut(dense_weight[0], 0, k).T, cut(out_weight[0], 0, k).T], 1)
            for k in range(2)
        ]
    )
    first = jnp.concatenate([qkv_shard[0], pair], 0)
    first, row, cot, rest_mine, rest_other = pin(first, row, cot, *rest_half)
    first = gather_deep(first) if direct else lax.all_gather(first, "dp", axis=0)
    rest_shard = ordered(rest_mine, flip(rest_other, "section"))
    qkv0 = first if direct else first[:, :deep].reshape(groups, -1, qkv_cols)
    pair = first[:, deep:].reshape(n_dp, -1)[:, : 2 * n_tensor * n_small].reshape(n_dp, 2, n_tensor, n_small)
    order = jnp.arange(n_tensor) ^ me
    small_all = pair.astype(f32).transpose(1, 2, 0, 3)

    def chosen(array, index, axis):
        size = index.shape[0]
        shape = [1] * array.ndim
        shape[axis] = size
        return sum(
            jnp.where(index.reshape(shape) == place, lax.slice_in_dim(array, place, place + 1, axis=axis), 0.0)
            for place in range(size)
        )

    if direct:
        small_all = chosen(small_all, slots, 2)
    here = small_all[:, 0]
    small_all = chosen(small_all, order, 1)

    def gather_early(piece):
        return lax.all_gather(piece, "dp", axis=0, tiled=True).reshape(groups, -1, piece.shape[1])

    def shares(rest):
        return rest[:, :in_cols], rest[:, in_cols:]

    table = jnp.arange(n_tensor, dtype=jnp.int32) ^ me
    positions = jnp.concatenate(
        [slot * shard_rows + jnp.arange(shard_rows, dtype=jnp.int32) for slot in (me, me ^ 1, me ^ 2, me ^ 3)]
    )
    ends = jnp.cumsum(row)
    passed = positions[:, None] >= ends[None, :]
    doc = jnp.sum(passed.astype(jnp.int32), -1)
    offset = positions - jnp.sum(jnp.where(passed, row[None, :], 0), -1)
    valid_own = (positions < ends[-1])[:shard_rows]
    lane = jnp.arange(128, dtype=jnp.int32)
    same = doc[:, None] == lane[None, :]
    feats_q = jnp.where(same, -FAR, 0.0).astype(bf16)
    feats_k = jnp.where(same | (lane[None, :] > row.shape[0]), 0.0, FAR).astype(bf16)
    place = lane % HDIM
    rotary = HDIM // 4
    counter = (place % (rotary // 2)).astype(f32)
    inverse = jnp.exp(counter * (-2.0 * math.log(10000.0) / rotary))
    angles = offset.astype(f32)[:, None] * inverse[None, :]
    turned = (place < rotary)[None, :]
    sine = jnp.sin(angles)
    rotary_turns = (
        jnp.where(turned, jnp.cos(angles), 1.0),
        jnp.where((place < rotary // 2)[None, :], -sine, 0.0),
        jnp.where(turned & (place >= rotary // 2)[None, :], sine, 0.0),
    )

    rows_all = small_all[..., 3 * part : 9 * part].reshape(2, n_tensor, n_dp, 6, part).transpose(0, 3, 1, 2, 4)
    rows_all = jnp.pad(rows_all.reshape(2, 6, width), ((0, 0), (0, 2), (0, 0)))
    qkv_parts = here[..., : 3 * part].reshape(2, n_dp, 3, part).transpose(0, 2, 1, 3).reshape(2, 3, 2, heads // 2)
    qkv_parts = qkv_parts.transpose(0, 2, 1, 3).reshape(2, 2, qkv_cols)
    bias_all = jnp.concatenate([qkv_parts, here[..., 9 * part : n_small].reshape(2, 2, in_cols)], 2)
    bias_all = pick(bias_all, bias_all[:, ::-1])

    def chip_sum(terms):
        return terms[0].astype(f32) + flip(terms[1], "tensor", 1).astype(f32)

    def branch_sum(make):
        far = chip_sum(make(1)).astype(bf16)
        return chip_sum(make(0)), far

    def result_of(own, near, far, rows):
        return (own.astype(f32) + near + far.astype(f32) + rows[4:5] + rows[5:6]).astype(bf16)

    def input_back(own, grad_own, partial):
        n, inverse = normal_of(own.astype(f32))
        return grad_own.astype(f32) + inverse * (
            partial - jnp.mean(partial, -1, keepdims=True) - n * jnp.mean(partial * n, -1, keepdims=True)
        )

    def attend_one(qkv):
        return attend(table, qkv, feats_q, feats_k)

    def attend_back_one(qkv, attended, grad_mixed):
        mixed, lse = attended
        return attend_back(table, qkv, grad_mixed, mixed, lse, feats_q, feats_k, rotary_turns)

    def rows_of(own, far):
        return own, flip(own, "tensor", 1), far, flip(far, "tensor", 1)

    (in_shard0, out_shard0), (in_shard1, out_shard1) = shares(rest_shard[0]), shares(rest_shard[1])
    qkv0, rows_all, bias_all, *h_all = pin(qkv0, rows_all, bias_all, *rows_of(h_own, h_far))
    (norms0, norms1), (bias0, bias1) = rows_all, bias_all
    qkv0_other = flip(qkv0, "section")
    qkv_a0, normed, second, normal0 = project(slots, h_all, qkv0, qkv_cols, bias0, norms0, rotary_turns)
    qkv_a0, cot, in_shard0, out_shard0 = pin(qkv_a0, cot, in_shard0, out_shard0)
    in0 = gather_deep(in_shard0)
    out0 = gather_early(out_shard0)
    grad2 = cot * valid_own[:, None].astype(bf16)
    grad2_far = flip(grad2, "tensor", 2)
    mixed_a0 = attend_one(qkv_a0)
    in0, qkv0_other, normed, *mixed_a0 = pin(in0, qkv0_other, normed, *mixed_a0)
    in0_other = flip(in0, "section")
    qkv0 = (qkv0, qkv0_other)
    qkv_b0 = project_more(slots, normed, qkv0[1], qkv_cols, bias0, rotary_turns)
    mixed_b0 = attend_one(qkv_b0)
    up_shard1 = jnp.concatenate([qkv_shard[1], in_shard1], 1)
    second, grad2_far, in0_other, out0, up_shard1, out_shard1, *mixed_b0 = pin(
        second, grad2_far, in0_other, out0, up_shard1, out_shard1, *mixed_b0
    )
    in0, out0 = (in0, in0_other), (out0, flip(out0, "section"))
    up1 = gather_early(up_shard1)
    hid_a0 = gelu_up(slots, second, in0[0], in_cols, bias0, 0)
    grad_all1 = rows_of(grad2, grad2_far)
    hid_b0 = gelu_up(slots, second, in0[1], in_cols, bias0, 1)
    mixed0 = (mixed_a0[0], mixed_b0[0])
    near, far = branch_sum(lambda half: down(steps, mixed0, (hid_a0[0], hid_b0[0]), out0, half))
    far, up1, out_shard1, *grad_all1 = pin(far, up1, out_shard1, *grad_all1)
    out1 = gather_early(out_shard1)
    qkv1_other = flip(up1[:, :, :qkv_cols], "section")
    middle = result_of(h_own, near, flip(far, "tensor", 2), norms0)
    middle, up1, qkv1_other = pin(middle, up1, qkv1_other)
    in1_other = flip(up1[:, :, qkv_cols:], "section")

    h_all = rows_of(middle, flip(middle, "tensor", 2))
    in1_other, *h_all = pin(in1_other, *h_all)
    qkv1, in1 = (up1, qkv1_other), (up1, in1_other)
    qkv_a1, normed, second, normal1 = project(steps, h_all, qkv1[0], qkv_cols, bias1, norms1, rotary_turns)
    mixed_a1 = attend_one(qkv_a1)
    normed, out1, *mixed_a1 = pin(normed, out1, *mixed_a1)
    out1_other = flip(out1, "section")
    qkv_b1 = project_more(steps, normed, qkv1[1], qkv_cols, bias1, rotary_turns)
    mixed_b1 = attend_one(qkv_b1)
    second, *mixed_b1 = pin(second, *mixed_b1)
    hid_a1 = gelu_up(steps, second, in1[0], in_cols, bias1, 0)
    hid_b1 = gelu_up(steps, second, in1[1], in_cols, bias1, 1)
    mixed1 = (mixed_a1[0], mixed_b1[0])
    out1_other, hid_a1, hid_b1 = pin(out1_other, hid_a1, hid_b1)
    out1 = (out1, out1_other)

    gm_a, gm_b, gi_a1, gi_b1, flipped1 = down_back(steps, grad_all1, (hid_a1[1], hid_b1[1]), out1, heads // 2)

    def rest_grads(blocks, normal, flipped, gi, in_w, mixed, hid, norms, got=None):
        return weight_grads(blocks, normal, flipped, ((gi, in_w),), (mixed, hid[0]), norms, got)

    def qkv_grads(blocks, normal, gp, qkv_w, norms, got=None):
        return weight_grads(blocks, normal, None, ((gp, qkv_w),), (), norms, got)

    rest_b1 = rest_grads(steps, normal1, flipped1, gi_b1, in1[1], mixed1[1], hid_b1, norms1)
    gm_a, gm_b, rest_b1_grad = pin(gm_a, gm_b, rest_b1[0])
    rest_got1 = flip(rest_b1_grad, "section")
    gp_b1 = attend_back_one(qkv_b1, mixed_b1, gm_b)
    gm_a, gp_b1 = pin(gm_a, gp_b1)
    gp_a1 = attend_back_one(qkv_a1, mixed_a1, gm_a)
    gp_a1, rest_got1 = pin(gp_a1, rest_got1)
    near, far = branch_sum(lambda half: up_back(steps, (gp_a1, gp_b1), (gi_a1, gi_b1), qkv1, in1, norms1, half))
    far, normal1, flipped1, rest_got1 = pin(far, normal1, flipped1, rest_got1)
    far = flip(far, "tensor", 2)
    rest_a1 = rest_grads(steps, normal1, flipped1, gi_a1, in1[0], mixed1[0], hid_a1, norms1, rest_got1)
    normal1, rest_a1_grad = pin(normal1, rest_a1[0])
    qkv_g_b1 = qkv_grads(steps, normal1, gp_b1, qkv1[1], norms1)
    normal1, qkv_b1_grad, mixed1_a, mixed1_b = pin(normal1, qkv_g_b1[0], *mixed1)
    qkv_got1 = flip(qkv_b1_grad, "section")
    final_far = chip_sum(down(steps, (mixed1_a, mixed1_b), (hid_a1[0], hid_b1[0]), out1, 1)).astype(bf16)
    far, normal1, rest_a1_grad = pin(far, normal1, rest_a1_grad)
    grad1 = input_back(middle, grad2, near + far.astype(f32))
    grad1_low = grad1.astype(bf16)
    grad1_low, rest_a1_grad, normal1, final_far, mixed1_a, mixed1_b = pin(
        grad1_low, rest_a1_grad, normal1, final_far, mixed1_a, mixed1_b
    )
    grad1_far = flip(grad1_low, "tensor", 2)
    reduced_rest1 = scatter_late(rest_a1_grad)
    qkv_g_a1 = qkv_grads(steps, normal1, gp_a1, qkv1[0], norms1, qkv_got1)
    near_terms = down(steps, (mixed1_a, mixed1_b), (hid_a1[0], hid_b1[0]), out1, 0)
    grad1_far, qkv_a1_grad, *near_terms = pin(grad1_far, qkv_g_a1[0], *near_terms)
    grad_all0 = rows_of(grad1_low, grad1_far)
    final_far, *grad_all0 = pin(final_far, *grad_all0)
    final_far = flip(final_far, "tensor", 2)

    gm_a, gm_b, gi_a0, gi_b0, flipped0 = down_back(steps, grad_all0, (hid_a0[1], hid_b0[1]), out0, heads // 2)
    rest_b0 = rest_grads(slots, normal0, flipped0, gi_b0, in0[1], mixed0[1], hid_b0, norms0)
    gm_a, gm_b, rest_b0_grad, qkv_a1_grad, reduced_rest1 = pin(gm_a, gm_b, rest_b0[0], qkv_a1_grad, reduced_rest1)
    rest_got0 = flip(rest_b0_grad, "section")
    reduced_qkv1 = scatter_late(qkv_a1_grad)
    gp_b0 = attend_back_one(qkv_b0, mixed_b0, gm_b)
    gp_b0, gm_a, normal0, final_far = pin(gp_b0, gm_a, normal0, final_far)
    final = result_of(middle, chip_sum(near_terms), final_far, norms1)
    qkv_g_b0 = qkv_grads(slots, normal0, gp_b0, qkv0[1], norms0)
    normal0, qkv_b0_grad = pin(normal0, qkv_g_b0[0])
    rest_a0 = rest_grads(slots, normal0, flipped0, gi_a0, in0[0], mixed0[0], hid_a0, norms0)
    gm_a, qkv_b0_grad, rest_a0_grad, rest_got0, final, reduced_qkv1 = pin(
        gm_a, qkv_b0_grad, rest_a0[0], rest_got0, final, reduced_qkv1
    )
    qkv_got0 = flip(qkv_b0_grad, "section")
    reduced_rest0 = scatter_late((rest_a0_grad.astype(f32) + rest_got0.astype(f32)).astype(bf16))
    gp_a0 = attend_back_one(qkv_a0, mixed_a0, gm_a)
    gp_a0, normal0, qkv_got0 = pin(gp_a0, normal0, qkv_got0)
    qkv_g_a0 = qkv_grads(slots, normal0, gp_a0, qkv0[0], norms0, qkv_got0)
    gp_a0, last, final = pin(gp_a0, qkv_g_a0[0], final)
    act_got = flip(pick(final, middle), "section")
    near, far = branch_sum(lambda half: up_back(slots, (gp_a0, gp_b0), (gi_a0, gi_b0), qkv0, in0, norms0, half))
    stats = [
        [[pieces[0][1], pieces[1][1], pieces[0][2], pieces[1][2]] for pieces in pair]
        for pair in (((qkv_g_a0, qkv_g_b0), (rest_a0, rest_b0)), ((qkv_g_a1, qkv_g_b1), (rest_a1, rest_b1)))
    ]
    far, stats = pin(far, stats)
    far = flip(far, "tensor", 2)

    packed = []
    for grad_own, (qkv_t, in_t) in zip((grad1_low, grad2), stats):
        vectors = jnp.concatenate([(qkv_t[0] + qkv_t[1])[:, :2], (in_t[0] + in_t[1])[:, :2]], 1).T
        vectors = jnp.concatenate([vectors[0::2], vectors[1::2], jnp.sum(grad_own.astype(f32), 0, keepdims=True)], 0)
        everywhere = vectors.reshape(5, n_tensor, n_dp, part).transpose(1, 2, 0, 3).reshape(n_tensor, n_dp, -1)
        halves_q = ordered(qkv_t[2][0].reshape(3, heads // 2), qkv_t[3][0].reshape(3, heads // 2))
        bias_q = jnp.concatenate(halves_q, 1).reshape(3, n_dp, part).transpose(1, 0, 2).reshape(n_dp, -1)
        bias_i = jnp.concatenate(ordered(in_t[2][0], in_t[3][0])).reshape(n_dp, -1)
        mine = jnp.concatenate([bias_q, bias_i], 1)
        only = (jnp.arange(n_tensor) == me)[:, None, None]
        packed.append(jnp.concatenate([everywhere, jnp.where(only, mine[None], 0.0)], 2))
    total = pick(packed[0], packed[1]) + flip(pick(packed[1], packed[0]), "section")
    total = chosen(total, order, 0)
    small_sum = total[0::2] + flip(total[1::2], "tensor", 1)
    far, small_sum = pin(far, small_sum)
    last, reduced_rest0 = pin(last, reduced_rest0)
    reduced_qkv0 = scatter_late(last)
    grad0 = input_back(h_own, grad1_low, near + far.astype(f32))
    grad_got = flip(pick(grad1_low, grad0.astype(bf16)), "section")

    activations = jnp.stack(ordered(pick(middle, final), act_got))
    input_grads = jnp.stack(ordered(pick(grad0, grad1_low.astype(f32)), grad_got.astype(f32)))

    def settled(one, two):
        got = flip(pick(two, one), "section")
        return [piece.astype(f32) for piece in ordered(pick(one, two), got)]

    rest_g = settled(reduced_rest0, reduced_rest1)
    qkv_g = settled(reduced_qkv0, reduced_qkv1)
    qkv_grad = jnp.concatenate([piece.reshape(-1, 3, heads // 2) for piece in qkv_g], 2)
    in_grad = jnp.concatenate([piece[:, :in_cols] for piece in rest_g], 1)
    dense_grad = jnp.concatenate([piece[:, in_cols : in_cols + heads // 2].T for piece in rest_g], 0)
    out_grad = jnp.concatenate([piece[:, in_cols + heads // 2 :].T for piece in rest_g], 0)

    total = small_sum
    total = total[0] + flip(total[1], "tensor", 2)
    sums = lax.psum_scatter(total, "dp", scatter_dimension=0) if not direct else None
    if direct:
        total = chosen(total, slots, 0)
        got = [lax.ppermute(total[hop], "dp", [(i, (i - hop) % n_dp) for i in range(n_dp)]) for hop in range(1, n_dp)]
        sums = sum(got, total[0])
    return (
        activations[None],
        input_grads[None],
        qkv_grad[None],
        sums[5 * part : 8 * part].reshape(1, 3, part),
        dense_grad[None],
        in_grad[None],
        sums[8 * part :].reshape(1, -1),
        out_grad[None],
        sums[: 2 * part].reshape(1, 2, part),
        sums[2 * part : 4 * part].reshape(1, 2, part),
        jnp.stack([sums[4 * part : 5 * part]] * 2)[None],
    )


def solution(mesh):
    placed = (
        P("dp", "tensor", None),
        P("dp", "tensor", None),
        P("dp", None),
        P("section", "dp", None, "tensor"),
        P("section", None, ("tensor", "dp")),
        P("section", "tensor", "dp"),
        P("section", "dp", "tensor"),
        P("section", ("tensor", "dp")),
        P("section", "tensor", "dp"),
        P("section", None, ("tensor", "dp")),
        P("section", None, ("tensor", "dp")),
        P("section", None, ("tensor", "dp")),
    )
    return jax.shard_map(
        shards,
        mesh=mesh,
        in_specs=placed,
        out_specs=(
            P("section", "dp", "tensor", None),
            P("section", "dp", "tensor", None),
            P("section", "dp", None, "tensor"),
            P("section", None, ("tensor", "dp")),
            P("section", "tensor", "dp"),
            P("section", "dp", "tensor"),
            P("section", ("tensor", "dp")),
            P("section", "tensor", "dp"),
            P("section", None, ("tensor", "dp")),
            P("section", None, ("tensor", "dp")),
            P("section", None, ("tensor", "dp")),
        ),
        check_vma=False,
    )
```

time: 2210 us -> 771 us (0.35)
  matrix products: 849 us -> 0 us
  waiting for transfers between devices: 520 us -> 155 us
  Pallas kernels: 0 us -> 333 us
  other arithmetic: 324 us -> 82.6 us
  blocking collectives: 168 us -> 0 us
  local copies, waits for them, and re-layouts: 259 us -> 119 us
  starting transfers between devices: 12 us -> 55.9 us
  loops' own time: 41.9 us -> 0 us
    dot_general x120 -> x0, matrix products: 849 us -> none  [the longest x12 137 us: backward_block(): jnp.einsum('qhd,khd->hqk', grad_block, values_all, preferred_element_type...]
    pallas_call x0 -> x34, Pallas kernels: none -> 333 us  [the longest x4 97.5 us: attend_back(): pl.pallas_call(functools.partial(attend_back_kernel, shard_rows, tiles),...]
    reduce_scatter x13 -> x4, waiting for transfers between devices: 208 us -> 0.03 us  [scatter_late(): lax.psum_scatter(total.reshape(-1, total.shape[2]), 'dp', scatter_dimensi...]
    unnamed x33 -> x7, waiting for transfers between devices: 167 us -> 0.12 us
    all_gather x6 -> x0, blocking collectives: 157 us -> none  [the longest x1 48.3 us: shards(): lax.all_gather(norm_biases[0], ('tensor', 'dp'), axis=1, tiled=True)]
    dynamic_update_slice x24 -> x0, local copies, waits for them, and re-layouts: 140 us -> none  [attend_back(): lax.scan(backward_block, (empty, empty), jnp.arange(seq_len // QBLK, dtyp...]
    convert_element_type x33 -> x11, other arithmetic: 146 us -> 19.4 us  [the longest x3 4.38 us: branch_sum(): far = chip_sum(make(1)).astype(bf16)]
    reduce_sum x32 -> x9, other arithmetic: 91.9 us -> 16 us  [the longest x2 5.85 us: normal_of(): jnp.mean(centered * centered, -1, keepdims=True) + EPSILON]
  transfers between devices with their start and end apart: 33 -> 62, of which waited for: 16 -> 22; matrix products, arithmetic and copies ran while one was open for 61% -> 14% of each run, Pallas kernels for 0% -> 37%
where the time goes in v1:
time: 771 us; the launch traced here: 762 us
  Pallas kernels  333 us (43%)
  waiting for transfers between devices  155 us (20%)
  local copies, waits for them, and re-layouts  119 us (15%)
  other arithmetic  82.6 us (11%)
  starting transfers between devices  55.9 us (7%)
  between operations  17.1 us (2%)
    ppermute x46, waiting for transfers between devices, flip(): lax.ppermute(block, axis, [(i, i ^ bit) for i in range(lax.axis_size(axis...  128 us
    unnamed x420, local copies, waits for them, and re-layouts  97.9 us
    pallas_call x4, Pallas kernels, attend_back(): pl.pallas_call(functools.partial(attend_back_kernel, shard_rows, tiles),...  97.5 us
    pallas_call x8, Pallas kernels, weight_grads(): call(functools.partial(grads_kernel, len(ups), len(downs), got is not Non...  57.6 us
    pallas_call x4, Pallas kernels, attend(): pl.pallas_call(functools.partial(attend_kernel, shard_rows, tiles), grid_...  50.9 us
    ppermute x46, starting transfers between devices, flip(): lax.ppermute(block, axis, [(i, i ^ bit) for i in range(lax.axis_size(axis...  35.3 us
    pallas_call x4, Pallas kernels, gelu_up(): call(functools.partial(gelu_kernel, part), 'gelu_up', (seq // rows,), [pl...  31.6 us
    pallas_call x4, Pallas kernels, up_back(): call(up_back_kernel, 'up_back', (steps,), [pl.BlockSpec((rows, x.shape[1]...  28.2 us
  transfers between devices with their start and end apart: 62, of which 22 were waited for; matrix products, arithmetic and copies ran while one was open for 14% of the time, Pallas kernels for 37%

profile of v1, /device:TPU:0, one launch (start us, length us, event | category | flops | bytes accessed | tf_op | source)
XLA Modules:
  0.0 762.0 jit_solution(11400061512498490230)
XLA Ops:
  73.5 9.5 %project.2 = (bf16[2048,384]{1,0:T(8,128)(2,1)S(1)}, bf16[2048,1024]{1,0:T(8,128)(2,1)S(1)}, bf16[2048,1024]{1,0:T(8,128)(2,1)S(1)}, bf16[1024,2048]{1,0:T(8,128)(2,1)S(1)}) custom-call(s32[4]{0:T(128)S(1)} %and_select_fusion.2.slots, bf16[512,1024]{1,0:T(8,128)(2,1)} %select_bitcast_fusion.3.h0, bf16[512,1024]{1,0:T(8,128)(2,1)} %collective-permute-done.7.h1, ...), custom_call_target="tpu_custom_call" | custom-call | flops 200000000 | bytes 900000 | tf_op jit(solution)/shard_map/project/pallas_call | solution.py:326
  102.4 12.6 %attend.4 = (bf16[2048,128]{1,0:T(8,128)(2,1)S(1)}, f32[8,2048]{1,0:T(8,128)S(1)}) custom-call(s32[4]{0:T(128)S(1)} %iota_xor_fusion.table, bf16[2048,384]{1,0:T(8,128)(2,1)S(1)} %copy-done.66, bf16[2048,384]{1,0:T(8,128)(2,1)S(1)} %copy-done.66, bf16[2048,384]{1,0:T(8,128)(2,1)S(1)} %copy-done.66, bf16[2048,128]{1,0:T(8,128)(2,1)S(1)} %get-tuple-element.580.fq_ref, ...), custom_call_target="tpu_custom_call" | custom-call | flops 200000000 | bytes 150000 | tf_op jit(solution)/shard_map/attend/pallas_call | solution.py:109
  115.0 10.5 %collective-permute-done.12 = bf16[256,512]{1,0:T(8,128)(2,1)S(1)} collective-permute-done((bf16[256,512]{1,0:T(8,128)(2,1)}, bf16[256,512]{1,0:T(8,128)(2,1)S(1)}, u32[]{:S(2)}, u32[]{:S(2)}) %collective-permute-start.12) | collective-permute-done | bytes 262176 | tf_op jit(solution)/shard_map/ppermute | solution.py:619
  141.0 12.8 %attend.5 = (bf16[2048,128]{1,0:T(8,128)(2,1)S(1)}, f32[8,2048]{1,0:T(8,128)S(1)}) custom-call(s32[4]{0:T(128)S(1)} %iota_xor_fusion.table, bf16[2048,384]{1,0:T(8,128)(2,1)S(1)} %project_more.2.q_ref.k_ref.v_ref, bf16[2048,384]{1,0:T(8,128)(2,1)S(1)} %project_more.2.q_ref.k_ref.v_ref, bf16[2048,384]{1,0:T(8,128)(2,1)S(1)} %project_more.2.q_ref.k_ref.v_ref, ...), custom_call_target="tpu_custom_call" | custom-call | flops 200000000 | bytes 150000 | tf_op jit(solution)/shard_map/attend/pallas_call | solution.py:109
  167.0 9.4 %gelu_up.5 = (bf16[2048,512]{1,0:T(8,128)(2,1)S(1)}, bf16[2048,512]{1,0:T(8,128)(2,1)S(1)}) custom-call(s32[4]{0:T(128)S(1)} %and_select_fusion.2.slots, bf16[2048,1024]{1,0:T(8,128)(2,1)S(1)} %copy-done.50, bf16[4,256,512]{2,1,0:T(8,128)(2,1)} %collective-permute-done.16.weight_ref.refs_5_.in_other, f32[2,896]{1,0:T(2,128)S(1)} %get-tuple-element.573.bias_ref), custom_call_target="tpu_custom_call" | custom-call | flops 250000000 | bytes 500000 | tf_op jit(solution)/shard_map/gelu_up/pallas_call | solution.py:383
  197.3 10.4 %all-gather.6.cloned.1.call-done = bf16[1024,896]{1,0:T(8,128)(2,1)} async-done(((bf16[256,896]{1,0:T(8,128)(2,1)}), bf16[1024,896]{1,0:T(8,128)(2,1)}) %all-gather.6.cloned.1.call-update) | async-done | bytes 1835024 | tf_op jit(solution)/shard_map/all_gather | solution.py:684
  214.9 17.9 %collective-permute-done.22 = bf16[512,1024]{1,0:T(8,128)(2,1)S(1)} collective-permute-done((bf16[512,1024]{1,0:T(8,128)(2,1)}, bf16[512,1024]{1,0:T(8,128)(2,1)S(1)}, u32[]{:S(2)}, u32[]{:S(2)}) %collective-permute-start.22) | collective-permute-done | bytes 1048608 | tf_op jit(solution)/shard_map/ppermute | solution.py:32
  241.3 20.9 %collective-permute-done.26.h2 = bf16[512,1024]{1,0:T(8,128)(2,1)} collective-permute-done((bf16[512,1024]{1,0:T(8,128)(2,1)}, bf16[512,1024]{1,0:T(8,128)(2,1)}, u32[]{:S(2)}, u32[]{:S(2)}) %collective-permute-start.26) | collective-permute-done | bytes 1048608 | tf_op jit(solution)/shard_map/ppermute | solution.py:32
  266.2 9.1 %project.3 = (bf16[2048,384]{1,0:T(8,128)(2,1)S(1)}, bf16[2048,1024]{1,0:T(8,128)(2,1)S(1)}, bf16[2048,1024]{1,0:T(8,128)(2,1)S(1)}, bf16[1024,2048]{1,0:T(8,128)(2,1)S(1)}) custom-call(s32[4]{0:T(128)S(1)} %iota.124.slots, bf16[512,1024]{1,0:T(8,128)(2,1)} %get-tuple-element.280.h0, bf16[512,1024]{1,0:T(8,128)(2,1)S(1)} %collective-permute-done.25.h1, ...), custom_call_target="tpu_custom_call" | custom-call | flops 200000000 | bytes 900000 | tf_op jit(solution)/shard_map/project/pallas_call | solution.py:326
  281.4 12.6 %attend.6 = (bf16[2048,128]{1,0:T(8,128)(2,1)S(1)}, f32[8,2048]{1,0:T(8,128)S(1)}) custom-call(s32[4]{0:T(128)S(1)} %iota_xor_fusion.table, bf16[2048,384]{1,0:T(8,128)(2,1)S(1)} %get-tuple-element.284.q_ref.k_ref.v_ref, bf16[2048,384]{1,0:T(8,128)(2,1)S(1)} %get-tuple-element.284.q_ref.k_ref.v_ref, ...), custom_call_target="tpu_custom_call" | custom-call | flops 200000000 | bytes 150000 | tf_op jit(solution)/shard_map/attend/pallas_call | solution.py:109
  308.4 13.0 %attend.7 = (bf16[2048,128]{1,0:T(8,128)(2,1)S(1)}, f32[8,2048]{1,0:T(8,128)S(1)}) custom-call(s32[4]{0:T(128)S(1)} %iota_xor_fusion.table, bf16[2048,384]{1,0:T(8,128)(2,1)S(1)} %project_more.3.q_ref.k_ref.v_ref, bf16[2048,384]{1,0:T(8,128)(2,1)S(1)} %project_more.3.q_ref.k_ref.v_ref, bf16[2048,384]{1,0:T(8,128)(2,1)S(1)} %project_more.3.q_ref.k_ref.v_ref, ...), custom_call_target="tpu_custom_call" | custom-call | flops 200000000 | bytes 150000 | tf_op jit(solution)/shard_map/attend/pallas_call | solution.py:109
  336.1 11.6 %down_back.2 = (bf16[2048,128]{1,0:T(8,128)(2,1)S(1)}, bf16[2048,128]{1,0:T(8,128)(2,1)S(1)}, bf16[2048,512]{1,0:T(8,128)(2,1)S(1)}, bf16[2048,512]{1,0:T(8,128)(2,1)S(1)}, bf16[1024,2048]{1,0:T(8,128)(2,1)S(1)}) custom-call(s32[4]{0:T(128)S(1)} %iota.125.slots, bf16[512,1024]{1,0:T(8,128)(2,1)} %get-tuple-element.285.g0, bf16[512,1024]{1,0:T(8,128)(2,1)S(1)} %copy-done.127, ...), custom_call_target="tpu_custom_call" | custom-call | flops 400000000 | bytes 900000 | tf_op jit(solution)/shard_map/down_back/pallas_call | solution.py:455
  351.9 8.5 %weight_grads.8 = (bf16[4,256,1152]{2,1,0:T(8,128)(2,1)S(1)}, f32[1024,8]{1,0:T(8,128)S(1)}, f32[8,512]{1,0:T(8,128)S(1)}) custom-call(s32[4]{0:T(128)S(1)} %iota.129.slots, bf16[1024,2048]{1,0:T(8,128)(2,1)S(1)} %copy-done.14, bf16[1024,2048]{1,0:T(8,128)(2,1)S(1)} %copy-done.52, bf16[2048,512]{1,0:T(8,128)(2,1)S(1)} %get-tuple-element.312.refs_2_.inner_other, ...), custom_call_target="tpu_custom_call" | custom-call | flops 241591904 | bytes 400000 | tf_op jit(solution)/shard_map/weight_grads/pallas_call | solution.py:568
  362.8 24.1 %attend_back.4.proj_other.refs_1_ = bf16[2048,384]{1,0:T(8,128)(2,1)S(1)} custom-call(s32[4]{0:T(128)S(1)} %iota_xor_fusion.table, bf16[2048,384]{1,0:T(8,128)(2,1)S(1)} %project_more.3.q_ref.k_ref.v_ref, bf16[2048,384]{1,0:T(8,128)(2,1)S(1)} %project_more.3.q_ref.k_ref.v_ref, bf16[2048,384]{1,0:T(8,128)(2,1)S(1)} %project_more.3.q_ref.k_ref.v_ref, ...), custom_call_target="tpu_custom_call" | custom-call | flops 500000000 | bytes 300000 | tf_op jit(solution)/shard_map/attend_back/pallas_call | solution.py:217
  387.0 24.6 %attend_back.5.proj_mine.refs_1_ = bf16[2048,384]{1,0:T(8,128)(2,1)S(1)} custom-call(s32[4]{0:T(128)S(1)} %iota_xor_fusion.table, bf16[2048,384]{1,0:T(8,128)(2,1)S(1)} %copy-done.69, bf16[2048,384]{1,0:T(8,128)(2,1)S(1)} %copy-done.69, bf16[2048,384]{1,0:T(8,128)(2,1)S(1)} %copy-done.69, bf16[2048,128]{1,0:T(8,128)(2,1)S(1)} %get-tuple-element.319.gm_ref, ...), custom_call_target="tpu_custom_call" | custom-call | flops 500000000 | bytes 300000 | tf_op jit(solution)/shard_map/attend_back/pallas_call | solution.py:217
  430.9 8.7 %weight_grads.9 = (bf16[4,256,1152]{2,1,0:T(8,128)(2,1)S(1)}, f32[1024,8]{1,0:T(8,128)S(1)}, f32[8,512]{1,0:T(8,128)S(1)}) custom-call(s32[4]{0:T(128)S(1)} %iota.131.slots, bf16[1024,2048]{1,0:T(8,128)(2,1)S(1)} %copy-done.14, bf16[1024,2048]{1,0:T(8,128)(2,1)S(1)} %copy-done.53, bf16[2048,512]{1,0:T(8,128)(2,1)S(1)} %get-tuple-element.325.inner_mine.refs_2_, ...), custom_call_target="tpu_custom_call" | custom-call | flops 241591904 | bytes 400000 | tf_op jit(solution)/shard_map/weight_grads/pallas_call | solution.py:568
  465.0 19.0 %collective-permute-done.36.refs_4_ = bf16[4,256,384]{2,1,0:T(8,128)(2,1)S(1)} collective-permute-done((bf16[4,256,384]{2,1,0:T(8,128)(2,1)}, bf16[4,256,384]{2,1,0:T(8,128)(2,1)S(1)}, u32[]{:S(2)}, u32[]{:S(2)}) %collective-permute-start.36) | collective-permute-done | bytes 786464 | tf_op jit(solution)/shard_map/ppermute | solution.py:32
  502.6 8.6 %down_back.3 = (bf16[2048,128]{1,0:T(8,128)(2,1)S(1)}, bf16[2048,128]{1,0:T(8,128)(2,1)S(1)}, bf16[2048,512]{1,0:T(8,128)(2,1)S(1)}, bf16[2048,512]{1,0:T(8,128)(2,1)S(1)}, bf16[1024,2048]{1,0:T(8,128)(2,1)S(1)}) custom-call(s32[4]{0:T(128)S(1)} %iota.122.slots, bf16[512,1024]{1,0:T(8,128)(2,1)S(1)} %copy-done.20, ...), custom_call_target="tpu_custom_call" | custom-call | flops 400000000 | bytes 900000 | tf_op jit(solution)/shard_map/down_back/pallas_call | solution.py:455
  514.2 9.5 %weight_grads.12 = (bf16[4,256,1152]{2,1,0:T(8,128)(2,1)S(1)}, f32[1024,8]{1,0:T(8,128)S(1)}, f32[8,512]{1,0:T(8,128)S(1)}) custom-call(s32[4]{0:T(128)S(1)} %and_select_fusion.2.slots, bf16[1024,2048]{1,0:T(8,128)(2,1)S(1)} %copy-done.17, bf16[1024,2048]{1,0:T(8,128)(2,1)S(1)} %get-tuple-element.367.refs_1_, ...), custom_call_target="tpu_custom_call" | custom-call | flops 241591904 | bytes 400000 | tf_op jit(solution)/shard_map/weight_grads/pallas_call | solution.py:568
  537.1 24.5 %attend_back.6.refs_1_.proj_other = bf16[2048,384]{1,0:T(8,128)(2,1)S(1)} custom-call(s32[4]{0:T(128)S(1)} %iota_xor_fusion.table, bf16[2048,384]{1,0:T(8,128)(2,1)S(1)} %copy-done.27, bf16[2048,384]{1,0:T(8,128)(2,1)S(1)} %copy-done.27, bf16[2048,384]{1,0:T(8,128)(2,1)S(1)} %copy-done.27, bf16[2048,128]{1,0:T(8,128)(2,1)S(1)} %copy-done.134, ...), custom_call_target="tpu_custom_call" | custom-call | flops 500000000 | bytes 300000 | tf_op jit(solution)/shard_map/attend_back/pallas_call | solution.py:217
  591.3 24.3 %attend_back.7.refs_1_.proj_mine = bf16[2048,384]{1,0:T(8,128)(2,1)S(1)} custom-call(s32[4]{0:T(128)S(1)} %iota_xor_fusion.table, bf16[2048,384]{1,0:T(8,128)(2,1)S(1)} %copy-done.67, bf16[2048,384]{1,0:T(8,128)(2,1)S(1)} %copy-done.67, bf16[2048,384]{1,0:T(8,128)(2,1)S(1)} %copy-done.67, bf16[2048,128]{1,0:T(8,128)(2,1)S(1)} %copy-done.132, ...), custom_call_target="tpu_custom_call" | custom-call | flops 500000000 | bytes 300000 | tf_op jit(solution)/shard_map/attend_back/pallas_call | solution.py:217
  670.2 9.9 %collective-permute-done.42 = bf16[512,1024]{1,0:T(8,128)(2,1)} collective-permute-done((bf16[512,1024]{1,0:T(8,128)(2,1)}, bf16[512,1024]{1,0:T(8,128)(2,1)}, u32[]{:S(2)}, u32[]{:S(2)}) %collective-permute-start.42) | collective-permute-done | bytes 1048608 | tf_op jit(solution)/shard_map/ppermute | solution.py:32
  683.8 10.6 %collective-permute-done.45 = bf16[512,1024]{1,0:T(8,128)(2,1)S(1)} collective-permute-done((bf16[512,1024]{1,0:T(8,128)(2,1)S(1)}, bf16[512,1024]{1,0:T(8,128)(2,1)S(1)}, u32[]{:S(2)}, u32[]{:S(2)}) %collective-permute-start.45) | collective-permute-done | bytes 1048608 | tf_op jit(solution)/shard_map/ppermute | solution.py:32
  717.5 18.1 %collective-permute-done.48 = bf16[512,1024]{1,0:T(8,128)(2,1)} collective-permute-done((bf16[512,1024]{1,0:T(8,128)(2,1)S(1)}, bf16[512,1024]{1,0:T(8,128)(2,1)}, u32[]{:S(2)}, u32[]{:S(2)}) %collective-permute-start.48) | collective-permute-done | bytes 1048608 | tf_op jit(solution)/shard_map/ppermute | solution.py:32
  (775 shorter events, 404.2 us)
Async XLA Ops:
  7.2 147.6 %all-gather.4.cloned.1.call-start = ((), (), s32[]{:S(2)}) async-start(), calls=%async_computation.4 | async-start | bytes 1638400 | tf_op jit(solution)/shard_map/all_gather | solution.py:684
  35.4 36.8 %collective-permute-start.7 = (bf16[512,1024]{1,0:T(8,128)(2,1)}, bf16[512,1024]{1,0:T(8,128)(2,1)}, u32[]{:S(2)}, u32[]{:S(2)}) collective-permute-start(bf16[512,1024]{1,0:T(8,128)(2,1)} %select_bitcast_fusion.3.h0), channel_id=1, source_target_pairs={{0,4},{4,0},{8,12},{12,8},{1,5},{5,1},{9,13},{13,9},{2,6},{6,2},{1... | collective-permute-start | bytes 3145736 | tf_op jit(solution)/shard_map/ppermute | solution.py:32
  90.3 117.5 %all-gather.6.cloned.1.call-start = ((), (), s32[]{:S(2)}) async-start(), calls=%async_computation.5 | async-start | bytes 2293760 | tf_op jit(solution)/shard_map/all_gather | solution.py:684
  91.8 34.9 %collective-permute-start.14 = (bf16[4,288,384]{2,1,0:T(8,128)(2,1)}, bf16[4,288,384]{2,1,0:T(8,128)(2,1)S(1)}, u32[]{:S(2)}, u32[]{:S(2)}) collective-permute-start(bf16[4,288,384]{2,1,0:T(8,128)(2,1)} %pad_maximum_fusion.1.weight_ref.refs_2_.qkv_mine), channel_id=1, source_target_pairs={{0,16},{16,0},{1,17},{17,1},{2,18},{18,2},{3,19},{19,3},{4,20},{20... | collective-permute-start | bytes 2654216 | tf_op jit(solution)/shard_map/ppermute | solution.py:32
  95.0 30.5 %collective-permute-start.12 = (bf16[256,512]{1,0:T(8,128)(2,1)}, bf16[256,512]{1,0:T(8,128)(2,1)S(1)}, u32[]{:S(2)}, u32[]{:S(2)}) collective-permute-start(bf16[256,512]{1,0:T(8,128)(2,1)} %slice.407), channel_id=1, source_target_pairs={{0,2},{1,3},{2,0},{3,1},{4,6},{5,7},{6,4},{7,5},{8,10},{9,11},{10,... | collective-permute-start | bytes 786440 | tf_op jit(solution)/shard_map/ppermute | solution.py:619
  97.1 29.5 %collective-permute-start.13 = (bf16[256,512]{1,0:T(8,128)(2,1)}, bf16[256,512]{1,0:T(8,128)(2,1)S(1)}, u32[]{:S(2)}, u32[]{:S(2)}) collective-permute-start(bf16[256,512]{1,0:T(8,128)(2,1)} %slice.407), channel_id=1, source_target_pairs={{0,3},{1,0},{2,1},{3,2},{4,7},{5,4},{6,5},{7,6},{8,11},{9,8},{10,9... | collective-permute-start | bytes 786440 | tf_op jit(solution)/shard_map/ppermute | solution.py:619
  102.0 52.7 %collective-permute-start.15 = (bf16[512,1024]{1,0:T(8,128)(2,1)}, bf16[512,1024]{1,0:T(8,128)(2,1)}, u32[]{:S(2)}, u32[]{:S(2)}) collective-permute-start(bf16[512,1024]{1,0:T(8,128)(2,1)} %get-tuple-element.285.g0), channel_id=1, source_target_pairs={{0,8},{4,12},{8,0},{12,4},{1,9},{5,13},{9,1},{13,5},{2,10},{6,14},... | collective-permute-start | bytes 3145736 | tf_op jit(solution)/shard_map/ppermute | solution.py:32
  154.8 141.8 %all-gather.8.cloned.1.call-start = ((), (), s32[]{:S(2)}) async-start(), calls=%async_computation.6 | async-start | bytes 1638400 | tf_op jit(solution)/shard_map/all_gather | solution.py:684
  154.8 29.7 %collective-permute-start.17 = (bf16[4,256,640]{2,1,0:T(8,128)(2,1)}, bf16[4,256,640]{2,1,0:T(8,128)(2,1)S(1)}, u32[]{:S(2)}, u32[]{:S(2)}) collective-permute-start(bf16[4,256,640]{2,1,0:T(8,128)(2,1)} %bitcast.159), channel_id=1, source_target_pairs={{0,16},{16,0},{1,17},{17,1},{2,18},{18,2},{3,19},{19,3},{4,20},{20... | collective-permute-start | bytes 3932168 | tf_op jit(solution)/shard_map/ppermute | solution.py:32
  239.3 289.8 %reduce-scatter.5.cloned.1.call-start = ((), (), s32[]{:S(2)}) async-start(), calls=%async_computation.7 | async-start | bytes 2949120 | tf_op jit(solution)/shard_map/reduce_scatter | solution.py:623
  296.6 39.4 %collective-permute-start.28 = (bf16[4,256,640]{2,1,0:T(8,128)(2,1)}, bf16[4,256,640]{2,1,0:T(8,128)(2,1)S(1)}, u32[]{:S(2)}, u32[]{:S(2)}) collective-permute-start(bf16[4,256,640]{2,1,0:T(8,128)(2,1)} %bitcast.163), channel_id=1, source_target_pairs={{0,16},{16,0},{1,17},{17,1},{2,18},{18,2},{3,19},{19,3},{4,20},{20... | collective-permute-start | bytes 3932168 | tf_op jit(solution)/shard_map/ppermute | solution.py:32
  361.3 52.7 %collective-permute-start.29 = (bf16[4,256,1152]{2,1,0:T(8,128)(2,1)S(1)}, bf16[4,256,1152]{2,1,0:T(8,128)(2,1)S(1)}, u32[]{:S(2)}, u32[]{:S(2)}) collective-permute-start(bf16[4,256,1152]{2,1,0:T(8,128)(2,1)S(1)} %get-tuple-element.322), channel_id=1, source_target_pairs={{0,16},{16,0},{1,17},{17,1},{2,18},{18,2},{3,19},{19,3},{4,20},{20... | collective-permute-start | bytes 7077896 | tf_op jit(solution)/shard_map/ppermute | solution.py:32
  422.9 32.8 %collective-permute-start.32 = (bf16[512,1024]{1,0:T(8,128)(2,1)S(1)}, bf16[512,1024]{1,0:T(8,128)(2,1)S(1)}, u32[]{:S(2)}, u32[]{:S(2)}) collective-permute-start(bf16[512,1024]{1,0:T(8,128)(2,1)S(1)} %add_convert_fusion.3), channel_id=1, source_target_pairs={{0,8},{4,12},{8,0},{12,4},{1,9},{5,13},{9,1},{13,5},{2,10},{6,14},... | collective-permute-start | bytes 3145736 | tf_op jit(solution)/shard_map/ppermute | solution.py:32
  462.8 119.6 %reduce-scatter.7.cloned.1.call-start = ((), (), s32[]{:S(2)}) async-start(), calls=%async_computation.8 | async-start | bytes 983040 | tf_op jit(solution)/shard_map/reduce_scatter | solution.py:623
  463.2 36.6 %collective-permute-start.35 = (bf16[512,1024]{1,0:T(8,128)(2,1)}, bf16[512,1024]{1,0:T(8,128)(2,1)S(1)}, u32[]{:S(2)}, u32[]{:S(2)}) collective-permute-start(bf16[512,1024]{1,0:T(8,128)(2,1)} %fusion.16.g0), channel_id=1, source_target_pairs={{0,8},{4,12},{8,0},{12,4},{1,9},{5,13},{9,1},{13,5},{2,10},{6,14},... | collective-permute-start | bytes 3145736 | tf_op jit(solution)/shard_map/ppermute | solution.py:32
  465.0 34.9 %collective-permute-start.34 = (bf16[512,1024]{1,0:T(8,128)(2,1)}, bf16[512,1024]{1,0:T(8,128)(2,1)S(1)}, u32[]{:S(2)}, u32[]{:S(2)}) collective-permute-start(bf16[512,1024]{1,0:T(8,128)(2,1)} %fusion.16.g0), channel_id=1, source_target_pairs={{0,4},{4,0},{8,12},{12,8},{1,5},{5,1},{9,13},{13,9},{2,6},{6,2},{1... | collective-permute-start | bytes 3145736 | tf_op jit(solution)/shard_map/ppermute | solution.py:32
  529.2 53.6 %collective-permute-start.39 = (bf16[4,256,1152]{2,1,0:T(8,128)(2,1)}, bf16[4,256,1152]{2,1,0:T(8,128)(2,1)}, u32[]{:S(2)}, u32[]{:S(2)}) collective-permute-start(bf16[4,256,1152]{2,1,0:T(8,128)(2,1)} %copy-done.159), channel_id=1, source_target_pairs={{0,16},{16,0},{1,17},{17,1},{2,18},{18,2},{3,19},{19,3},{4,20},{20... | collective-permute-start | bytes 7077896 | tf_op jit(solution)/shard_map/ppermute | solution.py:32
  529.5 184.6 %reduce-scatter.9.cloned.1.call-start = ((), (), s32[]{:S(2)}) async-start(), calls=%async_computation.9 | async-start | bytes 2949120 | tf_op jit(solution)/shard_map/reduce_scatter | solution.py:623
  529.6 32.1 %collective-permute-start.38 = (bf16[512,1024]{1,0:T(8,128)(2,1)}, bf16[512,1024]{1,0:T(8,128)(2,1)S(1)}, u32[]{:S(2)}, u32[]{:S(2)}) collective-permute-start(bf16[512,1024]{1,0:T(8,128)(2,1)} %add_convert_fusion.2), channel_id=1, source_target_pairs={{0,8},{4,12},{8,0},{12,4},{1,9},{5,13},{9,1},{13,5},{2,10},{6,14},... | collective-permute-start | bytes 3145736 | tf_op jit(solution)/shard_map/ppermute | solution.py:32
  530.3 48.9 %collective-permute-start.40 = (bf16[512,1024]{1,0:T(8,128)(2,1)}, bf16[512,1024]{1,0:T(8,128)(2,1)S(1)}, u32[]{:S(2)}, u32[]{:S(2)}) collective-permute-start(bf16[512,1024]{1,0:T(8,128)(2,1)} %copy-done.160), channel_id=1, source_target_pairs={{0,4},{4,0},{8,12},{12,8},{1,5},{5,1},{9,13},{13,9},{2,6},{6,2},{1... | collective-permute-start | bytes 3145736 | tf_op jit(solution)/shard_map/ppermute | solution.py:32
  582.8 32.9 %collective-permute-start.41 = (bf16[4,256,384]{2,1,0:T(8,128)(2,1)}, bf16[4,256,384]{2,1,0:T(8,128)(2,1)}, u32[]{:S(2)}, u32[]{:S(2)}) collective-permute-start(bf16[4,256,384]{2,1,0:T(8,128)(2,1)} %copy-done.162), channel_id=1, source_target_pairs={{0,16},{16,0},{1,17},{17,1},{2,18},{18,2},{3,19},{19,3},{4,20},{20... | collective-permute-start | bytes 2359304 | tf_op jit(solution)/shard_map/ppermute | solution.py:32
  636.5 110.0 %reduce-scatter.11.cloned.1.call-start = ((), (), s32[]{:S(2)}) async-start(), calls=%async_computation.10 | async-start | bytes 983040 | tf_op jit(solution)/shard_map/reduce_scatter | solution.py:623
  651.9 43.3 %collective-permute-start.43 = (bf16[512,1024]{1,0:T(8,128)(2,1)}, bf16[512,1024]{1,0:T(8,128)(2,1)}, u32[]{:S(2)}, u32[]{:S(2)}) collective-permute-start(bf16[512,1024]{1,0:T(8,128)(2,1)} %get-tuple-element.400), channel_id=1, source_target_pairs={{0,4},{4,0},{8,12},{12,8},{1,5},{5,1},{9,13},{13,9},{2,6},{6,2},{1... | collective-permute-start | bytes 3145736 | tf_op jit(solution)/shard_map/ppermute | solution.py:32
  715.1 29.8 %collective-permute-start.54 = (bf16[256,1152]{1,0:T(8,128)(2,1)}, bf16[256,1152]{1,0:T(8,128)(2,1)}, u32[]{:S(2)}, u32[]{:S(2)}) collective-permute-start(bf16[256,1152]{1,0:T(8,128)(2,1)} %broadcast_select_fusion.2), channel_id=1, source_target_pairs={{0,16},{16,0},{1,17},{17,1},{2,18},{18,2},{3,19},{19,3},{4,20},{20... | collective-permute-start | bytes 1769480 | tf_op jit(solution)/shard_map/ppermute | solution.py:32
  (241 other events, 2435.1 us)
Sparse Core Ops, SparseCore 0:
  90.4 49.6 all-gather.3
  154.9 52.7 all-gather.5
  239.4 34.1 all-gather.7
  462.9 49.3 reduce-scatter.4
  529.7 25.1 reduce-scatter.6
  636.6 49.4 reduce-scatter.8
  717.6 22.3 reduce-scatter.10

commit v2 on v1

--- a/solution.py
+++ b/solution.py
@@ -10,14 +10,15 @@
 
 HDIM = 64
 EPSILON = 1e-05
-TILE = 256
+TILE = 512
+KEYS = 512
 NT = (((1,), (1,)), ((), ()))
 NN = (((1,), (0,)), ((), ()))
 TN = (((0,), (0,)), ((), ()))
 LOG2E = math.log2(math.e)
 FAR = 1e15
 HURRY = 0.05
-LIMIT = pltpu.CompilerParams(vmem_limit_bytes=28 * 2**20)
+LIMIT = pltpu.CompilerParams(vmem_limit_bytes=20 * 2**20)
 
 
 def mm(a, b, dims=NN):
@@ -38,11 +39,6 @@
 
 def turn_back(grads, cosine, lead, trail):
     return grads * cosine - pltpu.roll(grads, 120, 1) * lead - pltpu.roll(grads, 8, 1) * trail
-
-
-def spot(table, tile, shard_rows):
-    per = shard_rows // TILE
-    return pl.multiple_of(table[tile // per] * shard_rows + (tile % per) * TILE, TILE)
 
 
 def head_part(block, head):
@@ -50,7 +46,18 @@
     return jnp.where((lane >= head * 64) & (lane < head * 64 + 64), block, jnp.zeros_like(block))
 
 
-def attend_kernel(shard_rows, tiles, table, q_ref, k_ref, v_ref, fq_ref, fk_ref, out_ref, lse_ref, vt):
+def tile_at(table, tile, size, shard_rows):
+    per = shard_rows // size
+    return pl.multiple_of(table[tile // per] * shard_rows + tile % per * size, size)
+
+
+def below(query_tile, key_tile, keys, queries):
+    rows = lax.broadcasted_iota(jnp.int32, (keys, queries), 0) + key_tile * keys
+    cols = lax.broadcasted_iota(jnp.int32, (keys, queries), 1) + query_tile * queries
+    return rows <= cols
+
+
+def attend_kernel(shard_rows, table, q_ref, k_ref, v_ref, fq_ref, fk_ref, out_ref, lse_ref, vt, wides, tops, totals):
     step = pl.program_id(0)
 
     @pl.when(step == 0)
@@ -60,57 +67,56 @@
             vt[head, 0:64, :] = flipped[head * 64 : head * 64 + 64, :]
             vt[head, 64:80, :] = jnp.ones((16, flipped.shape[1]), jnp.bfloat16)
 
-    def body(last):
-        query = q_ref[...]
-        feats = fq_ref[...]
-        outs = []
+    for head in range(2):
+        wides[head, :, 0:128] = head_part(q_ref[...], head)
+        wides[head, :, 128:256] = fq_ref[...]
+    tops[...] = jnp.full(tops.shape, -3e38, jnp.float32)
+    totals[...] = jnp.zeros_like(totals)
+
+    def tile(index, masked):
+        at = tile_at(table, index, KEYS, shard_rows)
+        keys = jnp.concatenate([k_ref[pl.ds(at, KEYS), :], fk_ref[pl.ds(at, KEYS), :]], 1)
+        blocks = [mm(keys, wides[head], NT) for head in range(2)]
+        blocks = [block * LOG2E for block in blocks]
+        if masked:
+            seen = below(step, index, KEYS, TILE)
+            blocks = [jnp.where(seen, block, -1e30) for block in blocks]
+        news = [jnp.maximum(tops[head], jnp.max(blocks[head], 0, keepdims=True)) for head in range(2)]
+        probs = [jnp.exp2(blocks[head] - news[head]).astype(jnp.bfloat16) for head in range(2)]
+        terms = [mm(vt[head, :, pl.ds(at, KEYS)], probs[head], NN) for head in range(2)]
         for head in range(2):
-            wide = jnp.concatenate([head_part(query, head), feats], 1)
-            scores = []
-            for tile in range(last + 1):
-                at = spot(table, tile, shard_rows)
-                keys = jnp.concatenate([k_ref[pl.ds(at, TILE), :], fk_ref[pl.ds(at, TILE), :]], 1)
-                block = mm(keys, wide, NT)
-                if tile == last:
-                    rows = lax.broadcasted_iota(jnp.int32, block.shape, 0)
-                    cols = lax.broadcasted_iota(jnp.int32, block.shape, 1)
-                    block = jnp.where(rows <= cols, block, -1e30)
-                scores.append(block)
-            top = jnp.max(scores[0], 0, keepdims=True)
-            for block in scores[1:]:
-                top = jnp.maximum(top, jnp.max(block, 0, keepdims=True))
-            shift = top * LOG2E
-            total = None
-            for tile in range(last + 1):
-                at = spot(table, tile, shard_rows)
-                probs = jnp.exp2(scores[tile] * LOG2E - shift).astype(jnp.bfloat16)
-                term = mm(vt[head, :, pl.ds(at, TILE)], probs, NN)
-                total = term if total is None else total + term
-            norm = total[64:65, :]
-            outs.append(total[0:64, :] / norm)
-            lse_ref[head : head + 1, :] = shift + jnp.log2(norm)
-        lse_ref[2:8, :] = jnp.zeros((6, TILE), jnp.float32)
-        both = jnp.concatenate(outs, 0)
-        out_ref[...] = both.T.astype(jnp.bfloat16)
-
-    for last in range(tiles):
-        pl.when(step == last)(functools.partial(body, last))
+            totals[head] = totals[head] * jnp.exp2(tops[head] - news[head]) + terms[head]
+            tops[head] = news[head]
+
+    def loop(index, carry):
+        tile(index, False)
+        return carry
+
+    whole = step * TILE // KEYS
+    lax.fori_loop(0, whole, loop, 0)
+    tile(whole, True)
+    outs = []
+    for head in range(2):
+        norm = totals[head, 64:65, :]
+        outs.append(totals[head, 0:64, :] / norm)
+        lse_ref[head : head + 1, :] = tops[head] + jnp.log2(norm)
+    lse_ref[2:8, :] = jnp.zeros((6, TILE), jnp.float32)
+    out_ref[...] = jnp.concatenate(outs, 0).T.astype(jnp.bfloat16)
 
 
 def attend(table, qkv, fq, fk):
     seq = qkv.shape[0]
     shard_rows = seq // 4
-    tiles = seq // TILE
     per = shard_rows // TILE
 
     def place(step, table):
         return table[step // per] * per + step % per
 
     return pl.pallas_call(
-        functools.partial(attend_kernel, shard_rows, tiles),
+        functools.partial(attend_kernel, shard_rows),
         grid_spec=pltpu.PrefetchScalarGridSpec(
             num_scalar_prefetch=1,
-            grid=(tiles,),
+            grid=(seq // TILE,),
             in_specs=[
                 pl.BlockSpec((TILE, 128), lambda i, t: (place(i, t), 0)),
                 pl.BlockSpec((seq, 128), lambda i, t: (0, 1)),
@@ -122,7 +128,12 @@
                 pl.BlockSpec((TILE, 128), lambda i, t: (place(i, t), 0)),
                 pl.BlockSpec((8, TILE), lambda i, t: (0, place(i, t))),
             ],
-            scratch_shapes=[pltpu.VMEM((2, 80, seq), jnp.bfloat16)],
+            scratch_shapes=[
+                pltpu.VMEM((2, 80, seq), jnp.bfloat16),
+                pltpu.VMEM((2, TILE, 256), jnp.bfloat16),
+                pltpu.VMEM((2, 1, TILE), jnp.float32),
+                pltpu.VMEM((2, 80, TILE), jnp.float32),
+            ],
         ),
         out_shape=[
             jax.ShapeDtypeStruct((seq, 128), jnp.bfloat16),
@@ -134,9 +145,10 @@
     )(table, qkv, qkv, qkv, fq, fk)
 
 
-def attend_back_kernel(shard_rows, tiles, table, q_ref, k_ref, v_ref, gm_ref, o_ref, lse_ref, fq_ref, fk_ref,
-                       cos_ref, lead_ref, trail_ref, out_ref, kt, dk, dv):
+def attend_back_kernel(shard_rows, table, q_ref, k_ref, v_ref, gm_ref, o_ref, lse_ref, fq_ref, fk_ref,
+                       cos_ref, lead_ref, trail_ref, out_ref, kt, dk, dv, wides, grads, deltas, dq):
     step = pl.program_id(0)
+    last = pl.num_programs(0) - 1 - step
 
     @pl.when(step == 0)
     def _():
@@ -144,63 +156,49 @@
         dk[...] = jnp.zeros_like(dk)
         dv[...] = jnp.zeros_like(dv)
 
-    def body(last):
-        here = spot(table, last, shard_rows)
-        query = q_ref[...]
-        feats = fq_ref[...]
-        grad = gm_ref[...]
-        product = grad.astype(jnp.float32) * o_ref[...].astype(jnp.float32)
-        high = product.astype(jnp.bfloat16)
-        low = (product - high.astype(jnp.float32)).astype(jnp.bfloat16)
-        lane = lax.broadcasted_iota(jnp.int32, (8, 128), 1)
-        wides, grads, shifts, deltas, queries = [], [], [], [], []
+    grad = gm_ref[...]
+    product = grad.astype(jnp.float32) * o_ref[...].astype(jnp.float32)
+    high = product.astype(jnp.bfloat16)
+    low = (product - high.astype(jnp.float32)).astype(jnp.bfloat16)
+    lane = lax.broadcasted_iota(jnp.int32, (8, 128), 1)
+    for head in range(2):
+        ones = jnp.where((lane >= head * 64) & (lane < head * 64 + 64), 1.0, 0.0).astype(jnp.bfloat16)
+        deltas[head] = (mm(ones, high, NT) + mm(ones, low, NT))[0:1, :]
+        wides[head, :, 0:128] = head_part(q_ref[...], head)
+        wides[head, :, 128:256] = fq_ref[...]
+        grads[head] = head_part(grad, head)
+    dq[...] = jnp.zeros_like(dq)
+
+    def tile(index, masked):
+        at = tile_at(table, index, KEYS, shard_rows)
+        rows = pl.ds(at, KEYS)
+        keys = jnp.concatenate([k_ref[rows, :], fk_ref[rows, :]], 1)
+        values = v_ref[rows, :]
+        blocks = [mm(keys, wides[head], NT) for head in range(2)]
+        backs = [mm(values, grads[head], NT) for head in range(2)]
+        probs = [jnp.exp2(blocks[head] * LOG2E - lse_ref[head : head + 1, :]) for head in range(2)]
+        if masked:
+            seen = below(last, index, KEYS, TILE)
+            probs = [jnp.where(seen, one, 0.0) for one in probs]
+        slopes = [(probs[head] * (backs[head] - deltas[head])).astype(jnp.bfloat16) for head in range(2)]
+        probs = [one.astype(jnp.bfloat16) for one in probs]
+        dv[rows, :] += mm(jnp.concatenate(probs, 1), grads[...].reshape(2 * TILE, 128), NN)
+        dk[rows, :] += mm(jnp.concatenate(slopes, 1), wides[:, :, 0:128].reshape(2 * TILE, 128), NN)
         for head in range(2):
-            ones = jnp.where((lane >= head * 64) & (lane < head * 64 + 64), 1.0, 0.0).astype(jnp.bfloat16)
-            deltas.append((mm(ones, high, NT) + mm(ones, low, NT))[0:1, :])
-            queries.append(head_part(query, head))
-            wides.append(jnp.concatenate([queries[head], feats], 1))
-            grads.append(head_part(grad, head))
-            shifts.append(lse_ref[head : head + 1, :])
-        turned = [None, None]
-        for tile in range(last + 1):
-            at = spot(table, tile, shard_rows)
-            keys = jnp.concatenate([k_ref[pl.ds(at, TILE), :], fk_ref[pl.ds(at, TILE), :]], 1)
-            values = v_ref[pl.ds(at, TILE), :]
-            dk_term = dv_term = None
-            for head in range(2):
-                block = mm(keys, wides[head], NT)
-                probs = jnp.exp2(block * LOG2E - shifts[head])
-                if tile == last:
-                    rows = lax.broadcasted_iota(jnp.int32, block.shape, 0)
-                    cols = lax.broadcasted_iota(jnp.int32, block.shape, 1)
-                    probs = jnp.where(rows <= cols, probs, 0.0)
-                back = mm(values, grads[head], NT)
-                slope = (probs * (back - deltas[head])).astype(jnp.bfloat16)
-                dv_one = mm(probs.astype(jnp.bfloat16), grads[head], NN)
-                dk_one = mm(slope, queries[head], NN)
-                dv_term = dv_one if head == 0 else dv_term + dv_one
-                dk_term = dk_one if head == 0 else dk_term + dk_one
-                dq = mm(kt[head * 64 : head * 64 + 64, pl.ds(at, TILE)], slope, NN)
-                turned[head] = dq if tile == 0 else turned[head] + dq
-            dv[pl.ds(at, TILE), :] += dv_term
-            dk[pl.ds(at, TILE), :] += dk_term
-        dq = jnp.concatenate(turned, 0).T * 0.125
-        dq = turn_back(dq, cos_ref[pl.ds(here, TILE), :], lead_ref[pl.ds(here, TILE), :], trail_ref[pl.ds(here, TILE), :])
-        out_ref[pl.ds(here, TILE), 0:128] = dq.astype(jnp.bfloat16)
-
-    for last in range(tiles):
-        pl.when(step == last)(functools.partial(body, last))
-
-    @pl.when(step == tiles - 1)
-    def _():
-        def finish(block, carry):
-            rows = pl.ds(pl.multiple_of(block * TILE, TILE), TILE)
-            turned = turn_back(dk[rows, :], cos_ref[rows, :], lead_ref[rows, :], trail_ref[rows, :])
-            out_ref[rows, 128:256] = turned.astype(jnp.bfloat16)
-            out_ref[rows, 256:384] = dv[rows, :].astype(jnp.bfloat16)
-            return carry
-
-        lax.fori_loop(0, tiles, finish, 0)
+            dq[head * 64 : head * 64 + 64, :] += mm(kt[head * 64 : head * 64 + 64, rows], slopes[head], NN)
+
+    def loop(index, carry):
+        tile(index, False)
+        return carry
+
+    whole = last * TILE // KEYS
+    lax.fori_loop(0, whole, loop, 0)
+    tile(whole, True)
+    here = pl.ds(tile_at(table, last, TILE, shard_rows), TILE)
+    turns = (cos_ref[...], lead_ref[...], trail_ref[...])
+    out_ref[:, 0:128] = turn_back(dq[...].T * 0.125, *turns).astype(jnp.bfloat16)
+    out_ref[:, 128:256] = turn_back(dk[here, :], *turns).astype(jnp.bfloat16)
+    out_ref[:, 256:384] = dv[here, :].astype(jnp.bfloat16)
 
 
 def attend_back(table, qkv, grad_mixed, mixed, lse, fq, fk, turns):
@@ -210,12 +208,12 @@
     per = shard_rows // TILE
 
     def place(step, table):
-        return table[step // per] * per + step % per
-
-    whole = pl.BlockSpec((seq, 128), lambda i, t: (0, 0))
+        tile = tiles - 1 - step
+        return table[tile // per] * per + tile % per
+
     block = pl.BlockSpec((TILE, 128), lambda i, t: (place(i, t), 0))
     return pl.pallas_call(
-        functools.partial(attend_back_kernel, shard_rows, tiles),
+        functools.partial(attend_back_kernel, shard_rows),
         grid_spec=pltpu.PrefetchScalarGridSpec(
             num_scalar_prefetch=1,
             grid=(tiles,),
@@ -227,19 +225,23 @@
                 block,
                 pl.BlockSpec((8, TILE), lambda i, t: (0, place(i, t))),
                 block,
-                whole,
-                whole,
-                whole,
-                whole,
+                pl.BlockSpec((seq, 128), lambda i, t: (0, 0)),
+                block,
+                block,
+                block,
             ],
-            out_specs=pl.BlockSpec((seq, 384), lambda i, t: (0, 0)),
+            out_specs=pl.BlockSpec((TILE, 384), lambda i, t: (place(i, t), 0)),
             scratch_shapes=[
                 pltpu.VMEM((128, seq), jnp.bfloat16),
                 pltpu.VMEM((seq, 128), jnp.float32),
                 pltpu.VMEM((seq, 128), jnp.float32),
+                pltpu.VMEM((2, TILE, 256), jnp.bfloat16),
+                pltpu.VMEM((2, TILE, 128), jnp.bfloat16),
+                pltpu.VMEM((2, 1, TILE), jnp.float32),
+                pltpu.VMEM((128, TILE), jnp.float32),
             ],
         ),
-        out_shape=jax.ShapeDtypeStruct((seq, 384), jnp.bfloat16),
+        out_shape=pltpu.HBM((seq, 384), jnp.bfloat16),
         compiler_params=LIMIT,
         cost_estimate=cost(10e9, 6e6, 5e6),
         name="attend_back",
@@ -301,8 +303,12 @@
     )
 
 
-def struct(*shape):
-    return jax.ShapeDtypeStruct(shape, jnp.bfloat16)
+def struct(*shape, far=False):
+    return pltpu.HBM(shape, jnp.bfloat16) if far else jax.ShapeDtypeStruct(shape, jnp.bfloat16)
+
+
+def stay(*arrays):
+    return [pltpu.with_memory_space_constraint(array, pltpu.HBM) for array in arrays]
 
 
 def project_kernel(
@@ -319,7 +325,7 @@
     heads_of(first, weight[...], bias_ref[0:1, 0 : weight.shape[1]], (cos_ref[...], lead_ref[...], trail_ref[...]), out_ref)
 
 
-def project(slots, pieces, weight, cols, bias, norms, turns):
+def project(slots, pieces, weight, cols, bias, norms, turns, far=False):
     rows, width = pieces[0].shape
     seq = rows * len(pieces)
     block = pl.BlockSpec((rows, width), lambda i, s: (i, 0))
@@ -329,7 +335,7 @@
         (seq // rows,),
         [whole_of(x) for x in (*pieces, weight, bias, norms)] + [pl.BlockSpec((rows, 128), lambda i, s: (i, 0))] * 3,
         [pl.BlockSpec((rows, cols), lambda i, s: (i, 0)), block, block, pl.BlockSpec((width, rows), lambda i, s: (0, i))],
-        [struct(seq, cols), struct(seq, width), struct(seq, width), struct(width, seq)],
+        [struct(seq, cols)] + [struct(*shape, far=far) for shape in ((seq, width), (seq, width), (width, seq))],
         [weight_scratch(width, weight, cols), pltpu.VMEM((rows, width), jnp.bfloat16)],
         4e9,
         18e6,
@@ -376,7 +382,7 @@
     slope_ref[...] = (below + inner * bell * (1.0 / math.sqrt(2 * math.pi))).astype(jnp.bfloat16)
 
 
-def gelu_up(slots, second, weight, cols, bias, part):
+def gelu_up(slots, second, weight, cols, bias, part, far=False):
     seq, width = second.shape
     rows = 256
     block = pl.BlockSpec((rows, cols), lambda i, s: (i, 0))
@@ -386,7 +392,7 @@
         (seq // rows,),
         [pl.BlockSpec((rows, width), lambda i, s: (i, 0)), whole_of(weight), whole_of(bias)],
         [block, block],
-        [struct(seq, cols), struct(seq, cols)],
+        [struct(seq, cols), struct(seq, cols, far=far)],
         [weight_scratch(width, weight, cols)],
         5e9,
         10e6,
@@ -447,7 +453,7 @@
         inner[...] = (mm(grad_ref[...], weight[:, heads:]) * slope[...].astype(jnp.float32)).astype(jnp.bfloat16)
 
 
-def down_back(slots, pieces, slopes, weights, heads):
+def down_back(slots, pieces, slopes, weights, heads, far=False):
     rows, width = pieces[0].shape
     seq = rows * len(pieces)
     hidden = slopes[0].shape[1]
@@ -458,7 +464,7 @@
         (seq // rows,),
         [whole_of(x) for x in pieces] + [wide, wide] + [whole_of(w) for w in weights],
         [pl.BlockSpec((rows, heads), lambda i, s: (i, 0))] * 2 + [wide, wide, pl.BlockSpec((width, rows), lambda i, s: (0, i))],
-        [struct(seq, heads)] * 2 + [struct(seq, hidden)] * 2 + [struct(width, seq)],
+        [struct(seq, heads)] * 2 + [struct(seq, hidden, far=far)] * 2 + [struct(width, seq, far=far)],
         [weight_scratch(width, w) for w in weights] + [pltpu.VMEM((rows, width), jnp.bfloat16)],
         8e9,
         18e6,
@@ -466,12 +472,12 @@
 
 
 def up_back_kernel(
-    slots, proj_mine, proj_other, inner_mine, inner_other, qkv_mine, qkv_other, in_mine, in_other, gain_ref, near_ref, beside_ref, *weights
+    slots, in_slots, proj_mine, proj_other, inner_mine, inner_other, qkv_mine, qkv_other, in_mine, in_other, gain_ref, near_ref, beside_ref, *weights
 ):
     for source, target in zip((qkv_mine, qkv_other), weights[:2]):
         settle(slots, source, target)
     for source, target in zip((in_mine, in_other), weights[2:]):
-        settle(slots, source, target, source.shape[2] - target.shape[1])
+        settle(in_slots, source, target, source.shape[2] - target.shape[1])
     qkv_a, qkv_b, in_a, in_b = weights
     first = mm(proj_mine[...], qkv_a[...], NT) + mm(proj_other[...], qkv_b[...], NT)
     second = mm(inner_mine[...], in_a[...], NT) + mm(inner_other[...], in_b[...], NT)
@@ -487,14 +493,15 @@
         up_back_kernel,
         "up_back",
         (steps,),
-        [pl.BlockSpec((rows, x.shape[1]), lambda i, s: (i + half * steps, 0)) for x in (*proj, *inner)]
+        [pl.BlockSpec((rows, x.shape[1]), lambda i, *s: (i + half * steps, 0)) for x in (*proj, *inner)]
         + [whole_of(w) for w in (*qkv_w, *in_w, gains)],
-        [pl.BlockSpec((rows, width), lambda i, s: (0, 0))] * 2,
+        [pl.BlockSpec((rows, width), lambda i, *s: (0, 0))] * 2,
         [struct(rows, width)] * 2,
         [weight_scratch(width, w, x.shape[1]) for w, x in zip((*qkv_w, *in_w), (*proj, *inner))],
         4e9,
         10e6,
-    )(slots, *proj, *inner, *qkv_w, *in_w, gains)
+        scalars=2,
+    )(*slots, *proj, *inner, *qkv_w, *in_w, gains)
 
 
 def grads_kernel(ups, downs, adds, slots, *refs):
@@ -527,10 +534,10 @@
         store(at, at + cols, raw * gain_column + total * bias_column)
         first = weights[k].shape[2] - cols if downs else 0
         wide = weights[k][0, :, first : first + cols].astype(jnp.float32)
-        lane = lax.broadcasted_iota(jnp.int32, stat_ref.shape, 1)
         gain = jnp.sum(raw * wide, 1, keepdims=True)
         shift = jnp.sum(wide * total, 1, keepdims=True)
-        stat_ref[...] = jnp.where(lane == 0, gain, jnp.where(lane == 1, shift, 0.0))
+        lane = lax.broadcasted_iota(jnp.int32, (raw.shape[0], 128), 1)
+        stat_ref[...] = jnp.where(lane == 0, gain, jnp.where(lane == 1, shift, 0.0)).T[0:8, :]
         at += cols
     for source in sources:
         cols = source.shape[1]
@@ -561,10 +568,10 @@
     if got is not None:
         args.append(got)
         specs.append(out_specs[0])
-    out_shape = [struct(groups, rows, cols)]
+    out_shape = [struct(groups, rows, cols, far=True)]
     for back, _ in ups:
-        out_specs += [pl.BlockSpec((rows, 8), lambda i, s: (i, 0)), pl.BlockSpec((8, back.shape[1]), lambda i, s: (0, 0))]
-        out_shape += [jax.ShapeDtypeStruct((width, 8), jnp.float32), jax.ShapeDtypeStruct((8, back.shape[1]), jnp.float32)]
+        out_specs += [pl.BlockSpec((8, rows), lambda i, s: (0, i)), pl.BlockSpec((8, back.shape[1]), lambda i, s: (0, 0))]
+        out_shape += [pltpu.HBM((8, width), jnp.float32), pltpu.HBM((8, back.shape[1]), jnp.float32)]
     return call(
         functools.partial(grads_kernel, len(ups), len(downs), got is not None),
         "weight_grads",
@@ -608,9 +615,6 @@
     def ordered(mine, other):
         return pick(mine, other), pick(other, mine)
 
-    steps = jnp.arange(groups, dtype=jnp.int32)
-    slots = (depth - steps) % groups if direct else steps
-
     def gather_deep(piece):
         if not direct:
             return lax.all_gather(piece, "dp", axis=0, tiled=True).reshape(groups, -1, piece.shape[1])
@@ -651,19 +655,25 @@
     pair = jnp.zeros((extra * qkv_cols,), bf16).at[: pair.shape[0]].set(pair).reshape(extra, qkv_cols)
     deep = qkv_half[0].shape[0]
     qkv_shard = ordered(qkv_half[0], qkv_got)
+    first = jnp.concatenate([qkv_shard[0], pair], 0)
+    zero = jnp.zeros((), jnp.int32)
+    first, row, zero, cot, in_weight, dense_weight, out_weight = pin(
+        first, row, zero, cot, in_weight, dense_weight, out_weight
+    )
     rest_half = halves(
         [
             jnp.concatenate([cut(in_weight[0], 1, k), cut(dense_weight[0], 0, k).T, cut(out_weight[0], 0, k).T], 1)
             for k in range(2)
         ]
     )
-    first = jnp.concatenate([qkv_shard[0], pair], 0)
-    first, row, cot, rest_mine, rest_other = pin(first, row, cot, *rest_half)
     first = gather_deep(first) if direct else lax.all_gather(first, "dp", axis=0)
-    rest_shard = ordered(rest_mine, flip(rest_other, "section"))
+
+    steps = zero + jnp.arange(groups, dtype=jnp.int32)
+    slots = (depth - steps) % groups if direct else steps
+    rest_mine, rest_got = rest_half[0], flip(rest_half[1], "section")
     qkv0 = first if direct else first[:, :deep].reshape(groups, -1, qkv_cols)
     pair = first[:, deep:].reshape(n_dp, -1)[:, : 2 * n_tensor * n_small].reshape(n_dp, 2, n_tensor, n_small)
-    order = jnp.arange(n_tensor) ^ me
+    order = (zero + jnp.arange(n_tensor)) ^ me
     small_all = pair.astype(f32).transpose(1, 2, 0, 3)
 
     def chosen(array, index, axis):
@@ -688,14 +698,14 @@
 
     table = jnp.arange(n_tensor, dtype=jnp.int32) ^ me
     positions = jnp.concatenate(
-        [slot * shard_rows + jnp.arange(shard_rows, dtype=jnp.int32) for slot in (me, me ^ 1, me ^ 2, me ^ 3)]
+        [slot * shard_rows + zero + jnp.arange(shard_rows, dtype=jnp.int32) for slot in (me, me ^ 1, me ^ 2, me ^ 3)]
     )
     ends = jnp.cumsum(row)
     passed = positions[:, None] >= ends[None, :]
     doc = jnp.sum(passed.astype(jnp.int32), -1)
     offset = positions - jnp.sum(jnp.where(passed, row[None, :], 0), -1)
     valid_own = (positions < ends[-1])[:shard_rows]
-    lane = jnp.arange(128, dtype=jnp.int32)
+    lane = jnp.arange(128, dtype=jnp.int32) + zero
     same = doc[:, None] == lane[None, :]
     feats_q = jnp.where(same, -FAR, 0.0).astype(bf16)
     feats_k = jnp.where(same | (lane[None, :] > row.shape[0]), 0.0, FAR).astype(bf16)
@@ -717,7 +727,7 @@
     qkv_parts = here[..., : 3 * part].reshape(2, n_dp, 3, part).transpose(0, 2, 1, 3).reshape(2, 3, 2, heads // 2)
     qkv_parts = qkv_parts.transpose(0, 2, 1, 3).reshape(2, 2, qkv_cols)
     bias_all = jnp.concatenate([qkv_parts, here[..., 9 * part : n_small].reshape(2, 2, in_cols)], 2)
-    bias_all = pick(bias_all, bias_all[:, ::-1])
+    bias_all = jnp.stack(ordered(bias_all[:, 0], bias_all[:, 1]), 1)
 
     def chip_sum(terms):
         return terms[0].astype(f32) + flip(terms[1], "tensor", 1).astype(f32)
@@ -740,53 +750,58 @@
 
     def attend_back_one(qkv, attended, grad_mixed):
         mixed, lse = attended
-        return attend_back(table, qkv, grad_mixed, mixed, lse, feats_q, feats_k, rotary_turns)
+        return attend_back(table, qkv, grad_mixed, mixed, lse, feats_q, feats_k, stay(*rotary_turns))
 
     def rows_of(own, far):
         return own, flip(own, "tensor", 1), far, flip(far, "tensor", 1)
 
-    (in_shard0, out_shard0), (in_shard1, out_shard1) = shares(rest_shard[0]), shares(rest_shard[1])
-    qkv0, rows_all, bias_all, *h_all = pin(qkv0, rows_all, bias_all, *rows_of(h_own, h_far))
+    in_shard0 = pick(rest_mine[:, :in_cols], rest_got[:, :in_cols])
+    qkv0, rows_all, bias_all, in_shard0, *h_all = pin(qkv0, rows_all, bias_all, in_shard0, *rows_of(h_own, h_far))
+    in0 = gather_deep(in_shard0)
     (norms0, norms1), (bias0, bias1) = rows_all, bias_all
     qkv0_other = flip(qkv0, "section")
-    qkv_a0, normed, second, normal0 = project(slots, h_all, qkv0, qkv_cols, bias0, norms0, rotary_turns)
-    qkv_a0, cot, in_shard0, out_shard0 = pin(qkv_a0, cot, in_shard0, out_shard0)
-    in0 = gather_deep(in_shard0)
-    out0 = gather_early(out_shard0)
+    qkv_a0, normed, second, normal0 = project(slots, h_all, qkv0, qkv_cols, bias0, norms0, rotary_turns, True)
+    qkv_a0, cot, rest_mine, rest_got = pin(qkv_a0, cot, rest_mine, rest_got)
+    rest0, rest1 = ordered(rest_mine, rest_got)
+    (_, out_shard0), (in_shard1, out_shard1) = shares(rest0), shares(rest1)
     grad2 = cot * valid_own[:, None].astype(bf16)
     grad2_far = flip(grad2, "tensor", 2)
     mixed_a0 = attend_one(qkv_a0)
-    in0, qkv0_other, normed, *mixed_a0 = pin(in0, qkv0_other, normed, *mixed_a0)
+    in0, qkv0_other, normed, out_shard0, *mixed_a0 = pin(in0, qkv0_other, normed, out_shard0, *mixed_a0)
+    out0 = gather_early(out_shard0)
     in0_other = flip(in0, "section")
-    qkv0 = (qkv0, qkv0_other)
-    qkv_b0 = project_more(slots, normed, qkv0[1], qkv_cols, bias0, rotary_turns)
+    qkv0 = stay(qkv0, qkv0_other)
+    qkv_b0 = project_more(slots, *stay(normed), qkv0[1], qkv_cols, bias0, rotary_turns)
     mixed_b0 = attend_one(qkv_b0)
-    up_shard1 = jnp.concatenate([qkv_shard[1], in_shard1], 1)
-    second, grad2_far, in0_other, out0, up_shard1, out_shard1, *mixed_b0 = pin(
-        second, grad2_far, in0_other, out0, up_shard1, out_shard1, *mixed_b0
-    )
-    in0, out0 = (in0, in0_other), (out0, flip(out0, "section"))
-    up1 = gather_early(up_shard1)
-    hid_a0 = gelu_up(slots, second, in0[0], in_cols, bias0, 0)
+    second, grad2_far, in0_other, *mixed_b0 = pin(second, grad2_far, in0_other, *mixed_b0)
+    in0 = stay(in0, in0_other)
+    hid_a0 = gelu_up(slots, *stay(second), in0[0], in_cols, bias0, 0, True)
     grad_all1 = rows_of(grad2, grad2_far)
-    hid_b0 = gelu_up(slots, second, in0[1], in_cols, bias0, 1)
+    second, out0, hid_a0, qkv_shard1 = pin(second, out0, hid_a0, qkv_shard[1])
+    qkv1 = gather_deep(qkv_shard1)
+    out0 = stay(out0, flip(out0, "section"))
+    hid_b0 = gelu_up(slots, *stay(second), in0[1], in_cols, bias0, 1, True)
     mixed0 = (mixed_a0[0], mixed_b0[0])
-    near, far = branch_sum(lambda half: down(steps, mixed0, (hid_a0[0], hid_b0[0]), out0, half))
-    far, up1, out_shard1, *grad_all1 = pin(far, up1, out_shard1, *grad_all1)
+    hid_b0, qkv1, in_shard1 = pin(hid_b0, qkv1, in_shard1)
+    in1 = gather_early(in_shard1)
+    far = chip_sum(down(steps, stay(*mixed0), stay(hid_a0[0], hid_b0[0]), out0, 1)).astype(bf16)
+    far, mixed0, qkv1, *grad_all1 = pin(far, mixed0, qkv1, *grad_all1)
+    qkv1_other = flip(qkv1, "section")
+    near = chip_sum(down(steps, stay(*mixed0), stay(hid_a0[0], hid_b0[0]), out0, 0))
+    middle = result_of(h_own, near, flip(far, "tensor", 2), norms0)
+    middle, qkv1_other, out_shard1 = pin(middle, qkv1_other, out_shard1)
     out1 = gather_early(out_shard1)
-    qkv1_other = flip(up1[:, :, :qkv_cols], "section")
-    middle = result_of(h_own, near, flip(far, "tensor", 2), norms0)
-    middle, up1, qkv1_other = pin(middle, up1, qkv1_other)
-    in1_other = flip(up1[:, :, qkv_cols:], "section")
 
     h_all = rows_of(middle, flip(middle, "tensor", 2))
-    in1_other, *h_all = pin(in1_other, *h_all)
-    qkv1, in1 = (up1, qkv1_other), (up1, in1_other)
-    qkv_a1, normed, second, normal1 = project(steps, h_all, qkv1[0], qkv_cols, bias1, norms1, rotary_turns)
+    in1, *h_all = pin(in1, *h_all)
+    in1_other = flip(in1, "section")
+    qkv1 = (qkv1, qkv1_other)
+    qkv_a1, normed, second, normal1 = project(slots, h_all, qkv1[0], qkv_cols, bias1, norms1, rotary_turns)
     mixed_a1 = attend_one(qkv_a1)
-    normed, out1, *mixed_a1 = pin(normed, out1, *mixed_a1)
+    normed, out1, in1_other, *mixed_a1 = pin(normed, out1, in1_other, *mixed_a1)
+    in1 = (in1, in1_other)
     out1_other = flip(out1, "section")
-    qkv_b1 = project_more(steps, normed, qkv1[1], qkv_cols, bias1, rotary_turns)
+    qkv_b1 = project_more(slots, normed, qkv1[1], qkv_cols, bias1, rotary_turns)
     mixed_b1 = attend_one(qkv_b1)
     second, *mixed_b1 = pin(second, *mixed_b1)
     hid_a1 = gelu_up(steps, second, in1[0], in_cols, bias1, 0)
@@ -801,7 +816,7 @@
         return weight_grads(blocks, normal, flipped, ((gi, in_w),), (mixed, hid[0]), norms, got)
 
     def qkv_grads(blocks, normal, gp, qkv_w, norms, got=None):
-        return weight_grads(blocks, normal, None, ((gp, qkv_w),), (), norms, got)
+        return weight_grads(blocks, normal, None, ((*stay(gp), qkv_w),), (), norms, got)
 
     rest_b1 = rest_grads(steps, normal1, flipped1, gi_b1, in1[1], mixed1[1], hid_b1, norms1)
     gm_a, gm_b, rest_b1_grad = pin(gm_a, gm_b, rest_b1[0])
@@ -810,15 +825,15 @@
     gm_a, gp_b1 = pin(gm_a, gp_b1)
     gp_a1 = attend_back_one(qkv_a1, mixed_a1, gm_a)
     gp_a1, rest_got1 = pin(gp_a1, rest_got1)
-    near, far = branch_sum(lambda half: up_back(steps, (gp_a1, gp_b1), (gi_a1, gi_b1), qkv1, in1, norms1, half))
+    near, far = branch_sum(lambda half: up_back((slots, steps), stay(gp_a1, gp_b1), stay(gi_a1, gi_b1), qkv1, in1, norms1, half))
     far, normal1, flipped1, rest_got1 = pin(far, normal1, flipped1, rest_got1)
     far = flip(far, "tensor", 2)
     rest_a1 = rest_grads(steps, normal1, flipped1, gi_a1, in1[0], mixed1[0], hid_a1, norms1, rest_got1)
     normal1, rest_a1_grad = pin(normal1, rest_a1[0])
-    qkv_g_b1 = qkv_grads(steps, normal1, gp_b1, qkv1[1], norms1)
+    qkv_g_b1 = qkv_grads(slots, normal1, gp_b1, qkv1[1], norms1)
     normal1, qkv_b1_grad, mixed1_a, mixed1_b = pin(normal1, qkv_g_b1[0], *mixed1)
     qkv_got1 = flip(qkv_b1_grad, "section")
-    final_far = chip_sum(down(steps, (mixed1_a, mixed1_b), (hid_a1[0], hid_b1[0]), out1, 1)).astype(bf16)
+    final_far = chip_sum(down(steps, stay(mixed1_a, mixed1_b), stay(hid_a1[0], hid_b1[0]), stay(*out1), 1)).astype(bf16)
     far, normal1, rest_a1_grad = pin(far, normal1, rest_a1_grad)
     grad1 = input_back(middle, grad2, near + far.astype(f32))
     grad1_low = grad1.astype(bf16)
@@ -827,19 +842,21 @@
     )
     grad1_far = flip(grad1_low, "tensor", 2)
     reduced_rest1 = scatter_late(rest_a1_grad)
-    qkv_g_a1 = qkv_grads(steps, normal1, gp_a1, qkv1[0], norms1, qkv_got1)
-    near_terms = down(steps, (mixed1_a, mixed1_b), (hid_a1[0], hid_b1[0]), out1, 0)
-    grad1_far, qkv_a1_grad, *near_terms = pin(grad1_far, qkv_g_a1[0], *near_terms)
+    near_terms = down(steps, stay(mixed1_a, mixed1_b), stay(hid_a1[0], hid_b1[0]), stay(*out1), 0)
+    qkv_got1, normal1, *near_terms = pin(qkv_got1, normal1, *near_terms)
+    qkv_g_a1 = qkv_grads(slots, normal1, gp_a1, qkv1[0], norms1, qkv_got1)
+    grad1_far, qkv_a1_grad = pin(grad1_far, qkv_g_a1[0])
     grad_all0 = rows_of(grad1_low, grad1_far)
     final_far, *grad_all0 = pin(final_far, *grad_all0)
     final_far = flip(final_far, "tensor", 2)
 
-    gm_a, gm_b, gi_a0, gi_b0, flipped0 = down_back(steps, grad_all0, (hid_a0[1], hid_b0[1]), out0, heads // 2)
+    (normal0,) = stay(normal0)
+    gm_a, gm_b, gi_a0, gi_b0, flipped0 = down_back(steps, grad_all0, stay(hid_a0[1], hid_b0[1]), out0, heads // 2, True)
     rest_b0 = rest_grads(slots, normal0, flipped0, gi_b0, in0[1], mixed0[1], hid_b0, norms0)
     gm_a, gm_b, rest_b0_grad, qkv_a1_grad, reduced_rest1 = pin(gm_a, gm_b, rest_b0[0], qkv_a1_grad, reduced_rest1)
     rest_got0 = flip(rest_b0_grad, "section")
     reduced_qkv1 = scatter_late(qkv_a1_grad)
-    gp_b0 = attend_back_one(qkv_b0, mixed_b0, gm_b)
+    gp_b0 = attend_back_one(*stay(qkv_b0), stay(*mixed_b0), gm_b)
     gp_b0, gm_a, normal0, final_far = pin(gp_b0, gm_a, normal0, final_far)
     final = result_of(middle, chip_sum(near_terms), final_far, norms1)
     qkv_g_b0 = qkv_grads(slots, normal0, gp_b0, qkv0[1], norms0)
@@ -849,24 +866,25 @@
         gm_a, qkv_b0_grad, rest_a0[0], rest_got0, final, reduced_qkv1
     )
     qkv_got0 = flip(qkv_b0_grad, "section")
-    reduced_rest0 = scatter_late((rest_a0_grad.astype(f32) + rest_got0.astype(f32)).astype(bf16))
-    gp_a0 = attend_back_one(qkv_a0, mixed_a0, gm_a)
+    rest_total0 = (rest_a0_grad.astype(f32) + rest_got0.astype(f32)).astype(bf16)
+    gm_a, rest_total0 = pin(gm_a, rest_total0)
+    reduced_in0 = scatter_late(rest_total0[:, :, :in_cols])
+    gp_a0 = attend_back_one(*stay(qkv_a0), stay(*mixed_a0), gm_a)
     gp_a0, normal0, qkv_got0 = pin(gp_a0, normal0, qkv_got0)
     qkv_g_a0 = qkv_grads(slots, normal0, gp_a0, qkv0[0], norms0, qkv_got0)
-    gp_a0, last, final = pin(gp_a0, qkv_g_a0[0], final)
+    gp_a0, last, final, reduced_in0, rest_total0 = pin(gp_a0, qkv_g_a0[0], final, reduced_in0, rest_total0)
     act_got = flip(pick(final, middle), "section")
-    near, far = branch_sum(lambda half: up_back(slots, (gp_a0, gp_b0), (gi_a0, gi_b0), qkv0, in0, norms0, half))
+    reduced_out0 = scatter_late(rest_total0[:, :, in_cols:])
+    reduced_qkv0 = scatter_late(last)
     stats = [
         [[pieces[0][1], pieces[1][1], pieces[0][2], pieces[1][2]] for pieces in pair]
         for pair in (((qkv_g_a0, qkv_g_b0), (rest_a0, rest_b0)), ((qkv_g_a1, qkv_g_b1), (rest_a1, rest_b1)))
     ]
-    far, stats = pin(far, stats)
-    far = flip(far, "tensor", 2)
-
     packed = []
     for grad_own, (qkv_t, in_t) in zip((grad1_low, grad2), stats):
-        vectors = jnp.concatenate([(qkv_t[0] + qkv_t[1])[:, :2], (in_t[0] + in_t[1])[:, :2]], 1).T
-        vectors = jnp.concatenate([vectors[0::2], vectors[1::2], jnp.sum(grad_own.astype(f32), 0, keepdims=True)], 0)
+        qkv_sum, in_sum = qkv_t[0] + qkv_t[1], in_t[0] + in_t[1]
+        bias_sum = jnp.sum(grad_own.astype(f32), 0, keepdims=True)
+        vectors = jnp.concatenate([qkv_sum[0:1], in_sum[0:1], qkv_sum[1:2], in_sum[1:2], bias_sum], 0)
         everywhere = vectors.reshape(5, n_tensor, n_dp, part).transpose(1, 2, 0, 3).reshape(n_tensor, n_dp, -1)
         halves_q = ordered(qkv_t[2][0].reshape(3, heads // 2), qkv_t[3][0].reshape(3, heads // 2))
         bias_q = jnp.concatenate(halves_q, 1).reshape(3, n_dp, part).transpose(1, 0, 2).reshape(n_dp, -1)
@@ -874,28 +892,23 @@
         mine = jnp.concatenate([bias_q, bias_i], 1)
         only = (jnp.arange(n_tensor) == me)[:, None, None]
         packed.append(jnp.concatenate([everywhere, jnp.where(only, mine[None], 0.0)], 2))
+    gp_a0, gp_b0, *packed = pin(gp_a0, gp_b0, *packed)
+
+    def last_terms(half):
+        return up_back((slots, slots), stay(gp_a0, gp_b0), stay(gi_a0, gi_b0), qkv0, in0, norms0, half)
+
+    far = chip_sum(last_terms(1)).astype(bf16)
+    far, gp_a0, gp_b0 = pin(far, gp_a0, gp_b0)
+    near, beside = last_terms(0)
+    near = (near, flip(beside, "tensor", 1))
+    far = flip(far, "tensor", 2)
     total = pick(packed[0], packed[1]) + flip(pick(packed[1], packed[0]), "section")
     total = chosen(total, order, 0)
     small_sum = total[0::2] + flip(total[1::2], "tensor", 1)
-    far, small_sum = pin(far, small_sum)
-    last, reduced_rest0 = pin(last, reduced_rest0)
-    reduced_qkv0 = scatter_late(last)
+    far, small_sum, reduced_qkv0, reduced_out0, *near = pin(far, small_sum, reduced_qkv0, reduced_out0, *near)
+    near = near[0].astype(f32) + near[1].astype(f32)
     grad0 = input_back(h_own, grad1_low, near + far.astype(f32))
     grad_got = flip(pick(grad1_low, grad0.astype(bf16)), "section")
-
-    activations = jnp.stack(ordered(pick(middle, final), act_got))
-    input_grads = jnp.stack(ordered(pick(grad0, grad1_low.astype(f32)), grad_got.astype(f32)))
-
-    def settled(one, two):
-        got = flip(pick(two, one), "section")
-        return [piece.astype(f32) for piece in ordered(pick(one, two), got)]
-
-    rest_g = settled(reduced_rest0, reduced_rest1)
-    qkv_g = settled(reduced_qkv0, reduced_qkv1)
-    qkv_grad = jnp.concatenate([piece.reshape(-1, 3, heads // 2) for piece in qkv_g], 2)
-    in_grad = jnp.concatenate([piece[:, :in_cols] for piece in rest_g], 1)
-    dense_grad = jnp.concatenate([piece[:, in_cols : in_cols + heads // 2].T for piece in rest_g], 0)
-    out_grad = jnp.concatenate([piece[:, in_cols + heads // 2 :].T for piece in rest_g], 0)
 
     total = small_sum
     total = total[0] + flip(total[1], "tensor", 2)
@@ -904,6 +917,22 @@
         total = chosen(total, slots, 0)
         got = [lax.ppermute(total[hop], "dp", [(i, (i - hop) % n_dp) for i in range(n_dp)]) for hop in range(1, n_dp)]
         sums = sum(got, total[0])
+    grad_got, sums = pin(grad_got, sums)
+
+    activations = jnp.stack(ordered(pick(middle, final), act_got))
+    input_grads = jnp.stack(ordered(pick(grad0, grad1_low.astype(f32)), grad_got.astype(f32)))
+
+    def settled(one, two):
+        got = flip(pick(two, one), "section")
+        return [piece.astype(f32) for piece in ordered(pick(one, two), got)]
+
+    rest_g = settled(jnp.concatenate([reduced_in0, reduced_out0], 1), reduced_rest1)
+    qkv_g = settled(reduced_qkv0, reduced_qkv1)
+    qkv_grad = jnp.concatenate([piece.reshape(-1, 3, heads // 2) for piece in qkv_g], 2)
+    in_grad = jnp.concatenate([piece[:, :in_cols] for piece in rest_g], 1)
+    dense_grad = jnp.concatenate([piece[:, in_cols : in_cols + heads // 2].T for piece in rest_g], 0)
+    out_grad = jnp.concatenate([piece[:, in_cols + heads // 2 :].T for piece in rest_g], 0)
+
     return (
         activations[None],
         input_grads[None],

time: 771 us -> 706 us (0.916)
  local copies, waits for them, and re-layouts: 119 us -> 58.3 us
  Pallas kernels: 333 us -> 360 us
  waiting for transfers between devices: 155 us -> 140 us
  starting transfers between devices: 55.9 us -> 46.6 us
    unnamed x420 -> x233, local copies, waits for them, and re-layouts: 97.9 us -> 36 us
    ppermute x6 -> x9, waiting for transfers between devices: 16 us -> 1.56 us  [gather_deep(): lax.ppermute(piece, 'dp', [(i, (i + hop) % n_dp) for i in range(n_dp)])]
    pallas_call x8, Pallas kernels: 148 us -> 135 us  [the longest x4 87.2 us: attend_back(): pl.pallas_call(functools.partial(attend_back_kernel, shard_rows), grid_sp...]
    pallas_call x8, Pallas kernels: 57.6 us -> 71.3 us  [weight_grads(): call(functools.partial(grads_kernel, len(ups), len(downs), got is not Non...]
    all_gather x3, waiting for transfers between devices: 10.5 us -> 0.02 us  [gather_early(): lax.all_gather(piece, 'dp', axis=0, tiled=True)]
    ppermute x46, waiting for transfers between devices: 128 us -> 138 us  [flip(): lax.ppermute(block, axis, [(i, i ^ bit) for i in range(lax.axis_size(axis...]
    pallas_call x4, Pallas kernels: 19.4 us -> 29.3 us  [down(): call(down_kernel, 'down', (steps,), [pl.BlockSpec((rows, x.shape[1]), lam...]
    select_n x16 -> x19, other arithmetic: 16.5 us -> 20.3 us  [pick(): return jnp.where(lefthand, first, second)]
  transfers between devices with their start and end apart: 62 -> 66, of which waited for: 22 -> 26; matrix products, arithmetic and copies ran while one was open for 14% -> 12% of each run, Pallas kernels for 37% -> 45%
where the time goes in v2:
time: 706 us; the launch traced here: 698 us
  Pallas kernels  360 us (51%)
  waiting for transfers between devices  140 us (20%)
  other arithmetic  77.3 us (11%)
  local copies, waits for them, and re-layouts  58.3 us (8%)
  starting transfers between devices  46.6 us (7%)
  between operations  16.2 us (2%)
    ppermute x46, waiting for transfers between devices, flip(): lax.ppermute(block, axis, [(i, i ^ bit) for i in range(lax.axis_size(axis...  138 us
    pallas_call x4, Pallas kernels, attend_back(): pl.pallas_call(functools.partial(attend_back_kernel, shard_rows), grid_sp...  87.2 us
    pallas_call x8, Pallas kernels, weight_grads(): call(functools.partial(grads_kernel, len(ups), len(downs), got is not Non...  71.3 us
    pallas_call x4, Pallas kernels, attend(): pl.pallas_call(functools.partial(attend_kernel, shard_rows), grid_spec=pl...  47.3 us
    pallas_call x4, Pallas kernels, gelu_up(): call(functools.partial(gelu_kernel, part), 'gelu_up', (seq // rows,), [pl...  37.5 us
    unnamed x233, local copies, waits for them, and re-layouts  36 us
    pallas_call x4, Pallas kernels, up_back(): call(up_back_kernel, 'up_back', (steps,), [pl.BlockSpec((rows, x.shape[1]...  34.2 us
    pallas_call x4, Pallas kernels, down(): call(down_kernel, 'down', (steps,), [pl.BlockSpec((rows, x.shape[1]), lam...  29.3 us
  transfers between devices with their start and end apart: 66, of which 26 were waited for; matrix products, arithmetic and copies ran while one was open for 12% of the time, Pallas kernels for 45%

profile of v2, /device:TPU:0, one launch (start us, length us, event | category | flops | bytes accessed | tf_op | source)
XLA Modules:
  0.0 697.8 jit_solution(7805431353301163412)
XLA Ops:
  64.1 10.9 %project.2 = (bf16[2048,384]{1,0:T(8,128)(2,1)S(1)}, bf16[2048,1024]{1,0:T(8,128)(2,1)}, bf16[2048,1024]{1,0:T(8,128)(2,1)}, bf16[1024,2048]{1,0:T(8,128)(2,1)}) custom-call(s32[4]{0:T(128)S(1)} %get-tuple-element.552.slots.in_slots, bf16[512,1024]{1,0:T(8,128)(2,1)} %select_bitcast_fusion.3.h0, bf16[512,1024]{1,0:T(8,128)(2,1)} %collective-permute-done.8.h1, ...), custom_call_target="tpu_custom_call" | custom-call | flops 200000000 | bytes 900000 | tf_op jit(solution)/shard_map/project/pallas_call | solution.py:332
  74.9 11.8 %attend.4 = (bf16[2048,128]{1,0:T(8,128)(2,1)S(1)}, f32[8,2048]{1,0:T(8,128)S(1)}) custom-call(s32[4]{0:T(128)S(1)} %iota_xor_fusion.table, bf16[2048,384]{1,0:T(8,128)(2,1)S(1)} %get-tuple-element.267.q_ref.k_ref.v_ref, bf16[2048,384]{1,0:T(8,128)(2,1)S(1)} %get-tuple-element.267.q_ref.k_ref.v_ref, ...), custom_call_target="tpu_custom_call" | custom-call | flops 200000000 | bytes 150000 | tf_op jit(solution)/shard_map/attend/pallas_call | solution.py:115
  103.6 11.8 %attend.5 = (bf16[2048,128]{1,0:T(8,128)(2,1)S(1)}, f32[8,2048]{1,0:T(8,128)S(1)}) custom-call(s32[4]{0:T(128)S(1)} %iota_xor_fusion.table, bf16[2048,384]{1,0:T(8,128)(2,1)S(1)} %project_more.2.q_ref.k_ref.v_ref, bf16[2048,384]{1,0:T(8,128)(2,1)S(1)} %project_more.2.q_ref.k_ref.v_ref, bf16[2048,384]{1,0:T(8,128)(2,1)S(1)} %project_more.2.q_ref.k_ref.v_ref, ...), custom_call_target="tpu_custom_call" | custom-call | flops 200000000 | bytes 150000 | tf_op jit(solution)/shard_map/attend/pallas_call | solution.py:115
  119.9 10.4 %gelu_up.4 = (bf16[2048,512]{1,0:T(8,128)(2,1)S(1)}, bf16[2048,512]{1,0:T(8,128)(2,1)}) custom-call(s32[4]{0:T(128)S(1)} %get-tuple-element.552.slots.in_slots, bf16[2048,1024]{1,0:T(8,128)(2,1)} %get-tuple-element.284.a_ref, bf16[4,256,512]{2,1,0:T(8,128)(2,1)} %pad_maximum_fusion.weight_ref.refs_5_.in_mine, f32[2,896]{1,0:T(2,128)S(1)} %get-tuple-element.598.bias_ref), custom_call_target="tpu_custom_call" | custom-call | flops 250000000 | bytes 500000 | tf_op jit(solution)/shard_map/gelu_up/pallas_call | solution.py:389
  139.5 10.4 %gelu_up.5 = (bf16[2048,512]{1,0:T(8,128)(2,1)S(1)}, bf16[2048,512]{1,0:T(8,128)(2,1)}) custom-call(s32[4]{0:T(128)S(1)} %get-tuple-element.552.slots.in_slots, bf16[2048,1024]{1,0:T(8,128)(2,1)} %get-tuple-element.284.a_ref, bf16[4,256,512]{2,1,0:T(8,128)(2,1)} %copy-done.66, f32[2,896]{1,0:T(2,128)S(1)} %get-tuple-element.598.bias_ref), custom_call_target="tpu_custom_call" | custom-call | flops 250000000 | bytes 500000 | tf_op jit(solution)/shard_map/gelu_up/pallas_call | solution.py:389
  186.1 21.2 %collective-permute-done.25 = bf16[512,1024]{1,0:T(8,128)(2,1)} collective-permute-done((bf16[512,1024]{1,0:T(8,128)(2,1)}, bf16[512,1024]{1,0:T(8,128)(2,1)}, u32[]{:S(2)}, u32[]{:S(2)}) %collective-permute-start.25) | collective-permute-done | bytes 1048608 | tf_op jit(solution)/shard_map/ppermute | solution.py:33
  212.3 24.0 %collective-permute-done.28.h2 = bf16[512,1024]{1,0:T(8,128)(2,1)} collective-permute-done((bf16[512,1024]{1,0:T(8,128)(2,1)}, bf16[512,1024]{1,0:T(8,128)(2,1)}, u32[]{:S(2)}, u32[]{:S(2)}) %collective-permute-start.28) | collective-permute-done | bytes 1048608 | tf_op jit(solution)/shard_map/ppermute | solution.py:33
  239.7 10.0 %project.3 = (bf16[2048,384]{1,0:T(8,128)(2,1)S(1)}, bf16[2048,1024]{1,0:T(8,128)(2,1)S(1)}, bf16[2048,1024]{1,0:T(8,128)(2,1)S(1)}, bf16[1024,2048]{1,0:T(8,128)(2,1)S(1)}) custom-call(s32[4]{0:T(128)S(1)} %get-tuple-element.552.slots.in_slots, bf16[512,1024]{1,0:T(8,128)(2,1)} %get-tuple-element.303.h0, bf16[512,1024]{1,0:T(8,128)(2,1)} %collective-permute-done.27.h1, ...), custom_call_target="tpu_custom_call" | custom-call | flops 200000000 | bytes 900000 | tf_op jit(solution)/shard_map/project/pallas_call | solution.py:332
  255.7 11.8 %attend.6 = (bf16[2048,128]{1,0:T(8,128)(2,1)S(1)}, f32[8,2048]{1,0:T(8,128)S(1)}) custom-call(s32[4]{0:T(128)S(1)} %iota_xor_fusion.table, bf16[2048,384]{1,0:T(8,128)(2,1)S(1)} %get-tuple-element.307.q_ref.k_ref.v_ref, bf16[2048,384]{1,0:T(8,128)(2,1)S(1)} %get-tuple-element.307.q_ref.k_ref.v_ref, ...), custom_call_target="tpu_custom_call" | custom-call | flops 200000000 | bytes 150000 | tf_op jit(solution)/shard_map/attend/pallas_call | solution.py:115
  279.1 11.8 %attend.7 = (bf16[2048,128]{1,0:T(8,128)(2,1)S(1)}, f32[8,2048]{1,0:T(8,128)S(1)}) custom-call(s32[4]{0:T(128)S(1)} %iota_xor_fusion.table, bf16[2048,384]{1,0:T(8,128)(2,1)S(1)} %project_more.3.q_ref.k_ref.v_ref, bf16[2048,384]{1,0:T(8,128)(2,1)S(1)} %project_more.3.q_ref.k_ref.v_ref, bf16[2048,384]{1,0:T(8,128)(2,1)S(1)} %project_more.3.q_ref.k_ref.v_ref, ...), custom_call_target="tpu_custom_call" | custom-call | flops 200000000 | bytes 150000 | tf_op jit(solution)/shard_map/attend/pallas_call | solution.py:115
  298.3 9.5 %gelu_up.7 = (bf16[2048,512]{1,0:T(8,128)(2,1)S(1)}, bf16[2048,512]{1,0:T(8,128)(2,1)S(1)}) custom-call(s32[4]{0:T(128)S(1)} %iota_add_fusion.5.slots.in_slots, bf16[2048,1024]{1,0:T(8,128)(2,1)S(1)} %copy-done.21, bf16[4,256,512]{2,1,0:T(8,128)(2,1)} %collective-permute-done.30.weight_ref.refs_5_.in_other, f32[2,896]{1,0:T(2,128)S(1)} %get-tuple-element.597.bias_ref), custom_call_target="tpu_custom_call" | custom-call | flops 250000000 | bytes 500000 | tf_op jit(solution)/shard_map/gelu_up/pallas_call | solution.py:389
  317.9 10.5 %weight_grads.8 = (bf16[4,256,1152]{2,1,0:T(8,128)(2,1)}, f32[8,1024]{1,0:T(8,128)}, f32[8,512]{1,0:T(8,128)}) custom-call(s32[4]{0:T(128)S(1)} %iota_add_fusion.5.slots.in_slots, bf16[1024,2048]{1,0:T(8,128)(2,1)S(1)} %copy-done.4, bf16[1024,2048]{1,0:T(8,128)(2,1)S(1)} %get-tuple-element.357.refs_1_, ...), custom_call_target="tpu_custom_call" | custom-call | flops 241591904 | bytes 400000 | tf_op jit(solution)/shard_map/weight_grads/pallas_call | solution.py:575
  328.8 21.3 %attend_back.4.proj_other.refs_1_ = bf16[2048,384]{1,0:T(8,128)(2,1)} custom-call(s32[4]{0:T(128)S(1)} %iota_xor_fusion.table, bf16[2048,384]{1,0:T(8,128)(2,1)S(1)} %project_more.3.q_ref.k_ref.v_ref, bf16[2048,384]{1,0:T(8,128)(2,1)S(1)} %project_more.3.q_ref.k_ref.v_ref, bf16[2048,384]{1,0:T(8,128)(2,1)S(1)} %project_more.3.q_ref.k_ref.v_ref, ...), custom_call_target="tpu_custom_call" | custom-call | flops 500000000 | bytes 300000 | tf_op jit(solution)/shard_map/attend_back/pallas_call | solution.py:215
  350.0 21.3 %attend_back.5.proj_mine.refs_1_ = bf16[2048,384]{1,0:T(8,128)(2,1)} custom-call(s32[4]{0:T(128)S(1)} %iota_xor_fusion.table, bf16[2048,384]{1,0:T(8,128)(2,1)S(1)} %copy-done.27, bf16[2048,384]{1,0:T(8,128)(2,1)S(1)} %copy-done.27, bf16[2048,384]{1,0:T(8,128)(2,1)S(1)} %copy-done.27, bf16[2048,128]{1,0:T(8,128)(2,1)S(1)} %get-tuple-element.343.gm_ref, ...), custom_call_target="tpu_custom_call" | custom-call | flops 500000000 | bytes 300000 | tf_op jit(solution)/shard_map/attend_back/pallas_call | solution.py:215
  371.3 10.1 %collective-permute-done.32.refs_7_ = bf16[4,256,1152]{2,1,0:T(8,128)(2,1)S(1)} collective-permute-done((bf16[4,256,1152]{2,1,0:T(8,128)(2,1)}, bf16[4,256,1152]{2,1,0:T(8,128)(2,1)S(1)}, u32[]{:S(2)}, u32[]{:S(2)}) %collective-permute-start.32) | collective-permute-done | bytes 2359328 | tf_op jit(solution)/shard_map/ppermute | solution.py:33
  403.7 9.6 %weight_grads.9 = (bf16[4,256,1152]{2,1,0:T(8,128)(2,1)}, f32[8,1024]{1,0:T(8,128)}, f32[8,512]{1,0:T(8,128)}) custom-call(s32[4]{0:T(128)S(1)} %iota_add_fusion.5.slots.in_slots, bf16[1024,2048]{1,0:T(8,128)(2,1)S(1)} %copy-done.4, bf16[1024,2048]{1,0:T(8,128)(2,1)S(1)} %get-tuple-element.357.refs_1_, bf16[2048,512]{1,0:T(8,128)(2,1)S(1)} %copy-done.11, ...), custom_call_target="tpu_custom_call" | custom-call | flops 241591904 | bytes 400000 | tf_op jit(solution)/shard_map/weight_grads/pallas_call | solution.py:575
  466.2 11.6 %down_back.3 = (bf16[2048,128]{1,0:T(8,128)(2,1)S(1)}, bf16[2048,128]{1,0:T(8,128)(2,1)S(1)}, bf16[2048,512]{1,0:T(8,128)(2,1)}, bf16[2048,512]{1,0:T(8,128)(2,1)}, bf16[1024,2048]{1,0:T(8,128)(2,1)}) custom-call(s32[4]{0:T(128)S(1)} %iota_add_fusion.5.slots.in_slots, bf16[512,1024]{1,0:T(8,128)(2,1)S(1)} %fusion.16.g0, ...), custom_call_target="tpu_custom_call" | custom-call | flops 400000000 | bytes 900000 | tf_op jit(solution)/shard_map/down_back/pallas_call | solution.py:461
  481.6 10.7 %weight_grads.12 = (bf16[4,256,1152]{2,1,0:T(8,128)(2,1)}, f32[8,1024]{1,0:T(8,128)}, f32[8,512]{1,0:T(8,128)}) custom-call(s32[4]{0:T(128)S(1)} %get-tuple-element.552.slots.in_slots, bf16[1024,2048]{1,0:T(8,128)(2,1)} %get-tuple-element.422.refs_0_, bf16[1024,2048]{1,0:T(8,128)(2,1)S(1)} %copy-done.22, bf16[2048,512]{1,0:T(8,128)(2,1)S(1)} %copy-done.17, ...), custom_call_target="tpu_custom_call" | custom-call | flops 241591904 | bytes 400000 | tf_op jit(solution)/shard_map/weight_grads/pallas_call | solution.py:575
  493.7 22.5 %attend_back.6.refs_1_.proj_other = bf16[2048,384]{1,0:T(8,128)(2,1)} custom-call(s32[4]{0:T(128)S(1)} %iota_xor_fusion.table, bf16[2048,384]{1,0:T(8,128)(2,1)} %copy-done.6, bf16[2048,384]{1,0:T(8,128)(2,1)} %copy-done.6, bf16[2048,384]{1,0:T(8,128)(2,1)} %copy-done.6, bf16[2048,128]{1,0:T(8,128)(2,1)S(1)} %get-tuple-element.398.gm_ref, ...), custom_call_target="tpu_custom_call" | custom-call | flops 500000000 | bytes 300000 | tf_op jit(solution)/shard_map/attend_back/pallas_call | solution.py:215
  525.6 10.7 %weight_grads.14 = (bf16[4,256,1152]{2,1,0:T(8,128)(2,1)}, f32[8,1024]{1,0:T(8,128)}, f32[8,512]{1,0:T(8,128)}) custom-call(s32[4]{0:T(128)S(1)} %get-tuple-element.552.slots.in_slots, bf16[1024,2048]{1,0:T(8,128)(2,1)} %get-tuple-element.422.refs_0_, bf16[1024,2048]{1,0:T(8,128)(2,1)S(1)} %copy-done.23, bf16[2048,512]{1,0:T(8,128)(2,1)S(1)} %copy-done.16, ...), custom_call_target="tpu_custom_call" | custom-call | flops 241591904 | bytes 400000 | tf_op jit(solution)/shard_map/weight_grads/pallas_call | solution.py:575
  551.9 22.1 %attend_back.7.refs_1_.proj_mine = bf16[2048,384]{1,0:T(8,128)(2,1)} custom-call(s32[4]{0:T(128)S(1)} %iota_xor_fusion.table, bf16[2048,384]{1,0:T(8,128)(2,1)} %copy-done.25, bf16[2048,384]{1,0:T(8,128)(2,1)} %copy-done.25, bf16[2048,384]{1,0:T(8,128)(2,1)} %copy-done.25, bf16[2048,128]{1,0:T(8,128)(2,1)S(1)} %get-tuple-element.418.gm_ref, ...), custom_call_target="tpu_custom_call" | custom-call | flops 500000000 | bytes 300000 | tf_op jit(solution)/shard_map/attend_back/pallas_call | solution.py:215
  614.4 10.1 %collective-permute-done.45 = bf16[512,1024]{1,0:T(8,128)(2,1)S(1)} collective-permute-done((bf16[512,1024]{1,0:T(8,128)(2,1)S(1)}, bf16[512,1024]{1,0:T(8,128)(2,1)S(1)}, u32[]{:S(2)}, u32[]{:S(2)}) %collective-permute-start.45) | collective-permute-done | bytes 1048608 | tf_op jit(solution)/shard_map/ppermute | solution.py:33
  627.5 10.1 %collective-permute-done.47 = bf16[512,1024]{1,0:T(8,128)(2,1)} collective-permute-done((bf16[512,1024]{1,0:T(8,128)(2,1)}, bf16[512,1024]{1,0:T(8,128)(2,1)}, u32[]{:S(2)}, u32[]{:S(2)}) %collective-permute-start.47) | collective-permute-done | bytes 1048608 | tf_op jit(solution)/shard_map/ppermute | solution.py:33
  673.3 9.9 %collective-permute-done.51 = bf16[512,1024]{1,0:T(8,128)(2,1)} collective-permute-done((bf16[512,1024]{1,0:T(8,128)(2,1)}, bf16[512,1024]{1,0:T(8,128)(2,1)}, u32[]{:S(2)}, u32[]{:S(2)}) %collective-permute-start.51) | collective-permute-done | bytes 1048608 | tf_op jit(solution)/shard_map/ppermute | solution.py:33
  (583 shorter events, 357.5 us)
Async XLA Ops:
  7.2 124.5 %all-gather.4.cloned.1.call-start = ((), (), s32[]{:S(2)}) async-start(), calls=%async_computation.5 | async-start | bytes 1638400 | tf_op jit(solution)/shard_map/all_gather | solution.py:694
  22.9 35.1 %collective-permute-start.8 = (bf16[512,1024]{1,0:T(8,128)(2,1)}, bf16[512,1024]{1,0:T(8,128)(2,1)}, u32[]{:S(2)}, u32[]{:S(2)}) collective-permute-start(bf16[512,1024]{1,0:T(8,128)(2,1)} %select_bitcast_fusion.3.h0), channel_id=1, source_target_pairs={{0,4},{4,0},{8,12},{12,8},{1,5},{5,1},{9,13},{13,9},{2,6},{6,2},{1... | collective-permute-start | bytes 3145736 | tf_op jit(solution)/shard_map/ppermute | solution.py:33
  58.0 34.3 %collective-permute-start.14 = (bf16[4,288,384]{2,1,0:T(8,128)(2,1)}, bf16[4,288,384]{2,1,0:T(8,128)(2,1)}, u32[]{:S(2)}, u32[]{:S(2)}) collective-permute-start(bf16[4,288,384]{2,1,0:T(8,128)(2,1)} %copy-done.7), channel_id=1, source_target_pairs={{0,16},{16,0},{1,17},{17,1},{2,18},{18,2},{3,19},{19,3},{4,20},{20... | collective-permute-start | bytes 2654216 | tf_op jit(solution)/shard_map/ppermute | solution.py:33
  59.8 30.2 %collective-permute-start.11 = (bf16[256,512]{1,0:T(8,128)(2,1)}, bf16[256,512]{1,0:T(8,128)(2,1)}, u32[]{:S(2)}, u32[]{:S(2)}) collective-permute-start(bf16[256,512]{1,0:T(8,128)(2,1)} %slice_select_fusion.1), channel_id=1, source_target_pairs={{0,1},{1,2},{2,3},{3,0},{4,5},{5,6},{6,7},{7,4},{8,9},{9,10},{10,1... | collective-permute-start | bytes 786440 | tf_op jit(solution)/shard_map/ppermute | solution.py:623
  60.6 29.5 %collective-permute-start.12 = (bf16[256,512]{1,0:T(8,128)(2,1)}, bf16[256,512]{1,0:T(8,128)(2,1)}, u32[]{:S(2)}, u32[]{:S(2)}) collective-permute-start(bf16[256,512]{1,0:T(8,128)(2,1)} %slice_select_fusion.1), channel_id=1, source_target_pairs={{0,2},{1,3},{2,0},{3,1},{4,6},{5,7},{6,4},{7,5},{8,10},{9,11},{10,... | collective-permute-start | bytes 786440 | tf_op jit(solution)/shard_map/ppermute | solution.py:623
  61.0 29.0 %collective-permute-start.13 = (bf16[256,512]{1,0:T(8,128)(2,1)}, bf16[256,512]{1,0:T(8,128)(2,1)}, u32[]{:S(2)}, u32[]{:S(2)}) collective-permute-start(bf16[256,512]{1,0:T(8,128)(2,1)} %slice_select_fusion.1), channel_id=1, source_target_pairs={{0,3},{1,0},{2,1},{3,2},{4,7},{5,4},{6,5},{7,6},{8,11},{9,8},{10,9... | collective-permute-start | bytes 786440 | tf_op jit(solution)/shard_map/ppermute | solution.py:623
  92.3 144.5 %all-gather.6.cloned.1.call-start = ((), (), s32[]{:S(2)}) async-start(), calls=%async_computation.6 | async-start | bytes 1310720 | tf_op jit(solution)/shard_map/all_gather | solution.py:694
  131.6 27.4 %collective-permute-start.20 = (bf16[4,256,640]{2,1,0:T(8,128)(2,1)}, bf16[4,256,640]{2,1,0:T(8,128)(2,1)}, u32[]{:S(2)}, u32[]{:S(2)}) collective-permute-start(bf16[4,256,640]{2,1,0:T(8,128)(2,1)} %bitcast.174), channel_id=1, source_target_pairs={{0,16},{16,0},{1,17},{17,1},{2,18},{18,2},{3,19},{19,3},{4,20},{20... | collective-permute-start | bytes 3932168 | tf_op jit(solution)/shard_map/ppermute | solution.py:33
  184.0 27.4 %collective-permute-start.26 = (bf16[4,256,384]{2,1,0:T(8,128)(2,1)}, bf16[4,256,384]{2,1,0:T(8,128)(2,1)}, u32[]{:S(2)}, u32[]{:S(2)}) collective-permute-start(bf16[4,256,384]{2,1,0:T(8,128)(2,1)} %pad_maximum_fusion.2.weight_ref.qkv_mine.refs_2_), channel_id=1, source_target_pairs={{0,16},{16,0},{1,17},{17,1},{2,18},{18,2},{3,19},{19,3},{4,20},{20... | collective-permute-start | bytes 2359304 | tf_op jit(solution)/shard_map/ppermute | solution.py:33
  184.3 85.2 %all-gather.8.cloned.1.call-start = ((), (), s32[]{:S(2)}) async-start(), calls=%async_computation.7 | async-start | bytes 1638400 | tf_op jit(solution)/shard_map/all_gather | solution.py:694
  236.4 255.8 %reduce-scatter.6.cloned.1.call-start = ((), (), s32[]{:S(2)}) async-start(), calls=%async_computation.8 | async-start | bytes 2949120 | tf_op jit(solution)/shard_map/reduce_scatter | solution.py:627
  239.4 30.2 %collective-permute-start.30 = (bf16[4,256,512]{2,1,0:T(8,128)(2,1)}, bf16[4,256,512]{2,1,0:T(8,128)(2,1)}, u32[]{:S(2)}, u32[]{:S(2)}) collective-permute-start(bf16[4,256,512]{2,1,0:T(8,128)(2,1)} %bitcast.165), channel_id=1, source_target_pairs={{0,16},{16,0},{1,17},{17,1},{2,18},{18,2},{3,19},{19,3},{4,20},{20... | collective-permute-start | bytes 3145736 | tf_op jit(solution)/shard_map/ppermute | solution.py:33
  269.6 38.2 %collective-permute-start.31 = (bf16[4,256,640]{2,1,0:T(8,128)(2,1)}, bf16[4,256,640]{2,1,0:T(8,128)(2,1)S(1)}, u32[]{:S(2)}, u32[]{:S(2)}) collective-permute-start(bf16[4,256,640]{2,1,0:T(8,128)(2,1)} %bitcast.170), channel_id=1, source_target_pairs={{0,16},{16,0},{1,17},{17,1},{2,18},{18,2},{3,19},{19,3},{4,20},{20... | collective-permute-start | bytes 3932168 | tf_op jit(solution)/shard_map/ppermute | solution.py:33
  328.4 53.0 %collective-permute-start.32 = (bf16[4,256,1152]{2,1,0:T(8,128)(2,1)}, bf16[4,256,1152]{2,1,0:T(8,128)(2,1)S(1)}, u32[]{:S(2)}, u32[]{:S(2)}) collective-permute-start(bf16[4,256,1152]{2,1,0:T(8,128)(2,1)} %get-tuple-element.346), channel_id=1, source_target_pairs={{0,16},{16,0},{1,17},{17,1},{2,18},{18,2},{3,19},{19,3},{4,20},{20... | collective-permute-start | bytes 7077896 | tf_op jit(solution)/shard_map/ppermute | solution.py:33
  393.0 36.6 %collective-permute-start.35 = (bf16[512,1024]{1,0:T(8,128)(2,1)S(1)}, bf16[512,1024]{1,0:T(8,128)(2,1)S(1)}, u32[]{:S(2)}, u32[]{:S(2)}) collective-permute-start(bf16[512,1024]{1,0:T(8,128)(2,1)S(1)} %add_convert_fusion.3), channel_id=1, source_target_pairs={{0,8},{4,12},{8,0},{12,4},{1,9},{5,13},{9,1},{13,5},{2,10},{6,14},... | collective-permute-start | bytes 3145736 | tf_op jit(solution)/shard_map/ppermute | solution.py:33
  402.2 27.4 %collective-permute-start.33 = (bf16[512,1024]{1,0:T(8,128)(2,1)S(1)}, bf16[512,1024]{1,0:T(8,128)(2,1)S(1)}, u32[]{:S(2)}, u32[]{:S(2)}) collective-permute-start(bf16[512,1024]{1,0:T(8,128)(2,1)S(1)} %get-tuple-element.351), channel_id=1, source_target_pairs={{0,4},{4,0},{8,12},{12,8},{1,5},{5,1},{9,13},{13,9},{2,6},{6,2},{1... | collective-permute-start | bytes 3145736 | tf_op jit(solution)/shard_map/ppermute | solution.py:33
  435.4 104.2 %reduce-scatter.8.cloned.1.call-start = ((), (), s32[]{:S(2)}) async-start(), calls=%async_computation.9 | async-start | bytes 983040 | tf_op jit(solution)/shard_map/reduce_scatter | solution.py:627
  435.5 28.0 %collective-permute-start.38 = (bf16[512,1024]{1,0:T(8,128)(2,1)S(1)}, bf16[512,1024]{1,0:T(8,128)(2,1)S(1)}, u32[]{:S(2)}, u32[]{:S(2)}) collective-permute-start(bf16[512,1024]{1,0:T(8,128)(2,1)S(1)} %fusion.16.g0), channel_id=1, source_target_pairs={{0,8},{4,12},{8,0},{12,4},{1,9},{5,13},{9,1},{13,5},{2,10},{6,14},... | collective-permute-start | bytes 3145736 | tf_op jit(solution)/shard_map/ppermute | solution.py:33
  492.2 53.6 %collective-permute-start.42 = (bf16[4,256,1152]{2,1,0:T(8,128)(2,1)}, bf16[4,256,1152]{2,1,0:T(8,128)(2,1)}, u32[]{:S(2)}, u32[]{:S(2)}) collective-permute-start(bf16[4,256,1152]{2,1,0:T(8,128)(2,1)} %get-tuple-element.410), channel_id=1, source_target_pairs={{0,16},{16,0},{1,17},{17,1},{2,18},{18,2},{3,19},{19,3},{4,20},{20... | collective-permute-start | bytes 7077896 | tf_op jit(solution)/shard_map/ppermute | solution.py:33
  492.7 89.1 %reduce-scatter.10.cloned.1.call-start = ((), (), s32[]{:S(2)}) async-start(), calls=%async_computation.10 | async-start | bytes 1310720 | tf_op jit(solution)/shard_map/reduce_scatter | solution.py:627
  493.7 42.6 %collective-permute-start.43 = (bf16[512,1024]{1,0:T(8,128)(2,1)}, bf16[512,1024]{1,0:T(8,128)(2,1)S(1)}, u32[]{:S(2)}, u32[]{:S(2)}) collective-permute-start(bf16[512,1024]{1,0:T(8,128)(2,1)} %copy-done.64), channel_id=1, source_target_pairs={{0,4},{4,0},{8,12},{12,8},{1,5},{5,1},{9,13},{13,9},{2,6},{6,2},{1... | collective-permute-start | bytes 3145736 | tf_op jit(solution)/shard_map/ppermute | solution.py:33
  551.3 76.1 %reduce-scatter.12.cloned.1.call-start = ((), (), s32[]{:S(2)}) async-start(), calls=%async_computation.11 | async-start | bytes 983040 | tf_op jit(solution)/shard_map/reduce_scatter | solution.py:627
  581.8 55.8 %reduce-scatter.14.cloned.1.call-start = ((), (), s32[]{:S(2)}) async-start(), calls=%async_computation.12 | async-start | bytes 1638400 | tf_op jit(solution)/shard_map/reduce_scatter | solution.py:627
  655.6 27.5 %collective-permute-start.51 = (bf16[512,1024]{1,0:T(8,128)(2,1)}, bf16[512,1024]{1,0:T(8,128)(2,1)}, u32[]{:S(2)}, u32[]{:S(2)}) collective-permute-start(bf16[512,1024]{1,0:T(8,128)(2,1)} %get-tuple-element.543), channel_id=1, source_target_pairs={{0,16},{16,0},{1,17},{17,1},{2,18},{18,2},{3,19},{19,3},{4,20},{20... | collective-permute-start | bytes 3145736 | tf_op jit(solution)/shard_map/ppermute | solution.py:33
  (155 other events, 2267.6 us)
Sparse Core Ops, SparseCore 0:
  92.5 31.2 all-gather.3
  184.5 26.8 all-gather.5
  236.5 30.4 all-gather.7
  435.5 45.6 reduce-scatter.5
  492.8 21.7 reduce-scatter.7
  551.4 24.4 reduce-scatter.9
  581.9 21.7 reduce-scatter.11
  606.8 30.4 reduce-scatter.13

commit v3 on v2

--- a/solution.py
+++ b/solution.py
@@ -822,16 +822,16 @@
     gm_a, gm_b, rest_b1_grad = pin(gm_a, gm_b, rest_b1[0])
     rest_got1 = flip(rest_b1_grad, "section")
     gp_b1 = attend_back_one(qkv_b1, mixed_b1, gm_b)
-    gm_a, gp_b1 = pin(gm_a, gp_b1)
+    gm_a, gp_b1, normal1 = pin(gm_a, gp_b1, normal1)
+    qkv_g_b1 = qkv_grads(slots, normal1, gp_b1, qkv1[1], norms1)
+    gm_a, gp_b1, qkv_b1_grad = pin(gm_a, gp_b1, qkv_g_b1[0])
     gp_a1 = attend_back_one(qkv_a1, mixed_a1, gm_a)
     gp_a1, rest_got1 = pin(gp_a1, rest_got1)
     near, far = branch_sum(lambda half: up_back((slots, steps), stay(gp_a1, gp_b1), stay(gi_a1, gi_b1), qkv1, in1, norms1, half))
     far, normal1, flipped1, rest_got1 = pin(far, normal1, flipped1, rest_got1)
     far = flip(far, "tensor", 2)
     rest_a1 = rest_grads(steps, normal1, flipped1, gi_a1, in1[0], mixed1[0], hid_a1, norms1, rest_got1)
-    normal1, rest_a1_grad = pin(normal1, rest_a1[0])
-    qkv_g_b1 = qkv_grads(slots, normal1, gp_b1, qkv1[1], norms1)
-    normal1, qkv_b1_grad, mixed1_a, mixed1_b = pin(normal1, qkv_g_b1[0], *mixed1)
+    normal1, rest_a1_grad, qkv_b1_grad, mixed1_a, mixed1_b = pin(normal1, rest_a1[0], qkv_b1_grad, *mixed1)
     qkv_got1 = flip(qkv_b1_grad, "section")
     final_far = chip_sum(down(steps, stay(mixed1_a, mixed1_b), stay(hid_a1[0], hid_b1[0]), stay(*out1), 1)).astype(bf16)
     far, normal1, rest_a1_grad = pin(far, normal1, rest_a1_grad)

time: 706 us -> 699 us (0.990)
    ppermute x46, waiting for transfers between devices: 138 us -> 131 us  [flip(): lax.ppermute(block, axis, [(i, i ^ bit) for i in range(lax.axis_size(axis...]
  transfers between devices with their start and end apart: 66 -> 66, of which waited for: 26 -> 26; matrix products, arithmetic and copies ran while one was open for 12% -> 12% of each run, Pallas kernels for 45% -> 46%
where the time goes in v3:
time: 699 us; the launch traced here: 691 us
  Pallas kernels  360 us (52%)
  waiting for transfers between devices  133 us (19%)
  other arithmetic  77.3 us (11%)
  local copies, waits for them, and re-layouts  58.3 us (8%)
  starting transfers between devices  46.5 us (7%)
  between operations  16.2 us (2%)
    ppermute x46, waiting for transfers between devices, flip(): lax.ppermute(block, axis, [(i, i ^ bit) for i in range(lax.axis_size(axis...  131 us
    pallas_call x4, Pallas kernels, attend_back(): pl.pallas_call(functools.partial(attend_back_kernel, shard_rows), grid_sp...  87.2 us
    pallas_call x8, Pallas kernels, weight_grads(): call(functools.partial(grads_kernel, len(ups), len(downs), got is not Non...  71.3 us
    pallas_call x4, Pallas kernels, attend(): pl.pallas_call(functools.partial(attend_kernel, shard_rows), grid_spec=pl...  47.3 us
    pallas_call x4, Pallas kernels, gelu_up(): call(functools.partial(gelu_kernel, part), 'gelu_up', (seq // rows,), [pl...  37.5 us
    unnamed x233, local copies, waits for them, and re-layouts  36 us
    pallas_call x4, Pallas kernels, up_back(): call(up_back_kernel, 'up_back', (steps,), [pl.BlockSpec((rows, x.shape[1]...  34.2 us
    pallas_call x4, Pallas kernels, down(): call(down_kernel, 'down', (steps,), [pl.BlockSpec((rows, x.shape[1]), lam...  29.3 us
  transfers between devices with their start and end apart: 66, of which 26 were waited for; matrix products, arithmetic and copies ran while one was open for 12% of the time, Pallas kernels for 46%

profile of v3, /device:TPU:0, one launch (start us, length us, event | category | flops | bytes accessed | tf_op | source)
XLA Modules:
  0.0 690.5 jit_solution(8979312816289015090)
XLA Ops:
  64.1 10.9 %project.2 = (bf16[2048,384]{1,0:T(8,128)(2,1)S(1)}, bf16[2048,1024]{1,0:T(8,128)(2,1)}, bf16[2048,1024]{1,0:T(8,128)(2,1)}, bf16[1024,2048]{1,0:T(8,128)(2,1)}) custom-call(s32[4]{0:T(128)S(1)} %get-tuple-element.558.slots.in_slots, bf16[512,1024]{1,0:T(8,128)(2,1)} %select_bitcast_fusion.3.h0, bf16[512,1024]{1,0:T(8,128)(2,1)} %collective-permute-done.8.h1, ...), custom_call_target="tpu_custom_call" | custom-call | flops 200000000 | bytes 900000 | tf_op jit(solution)/shard_map/project/pallas_call | solution.py:332
  74.9 11.8 %attend.4 = (bf16[2048,128]{1,0:T(8,128)(2,1)S(1)}, f32[8,2048]{1,0:T(8,128)S(1)}) custom-call(s32[4]{0:T(128)S(1)} %iota_xor_fusion.table, bf16[2048,384]{1,0:T(8,128)(2,1)S(1)} %get-tuple-element.270.q_ref.k_ref.v_ref, bf16[2048,384]{1,0:T(8,128)(2,1)S(1)} %get-tuple-element.270.q_ref.k_ref.v_ref, ...), custom_call_target="tpu_custom_call" | custom-call | flops 200000000 | bytes 150000 | tf_op jit(solution)/shard_map/attend/pallas_call | solution.py:115
  103.6 11.8 %attend.5 = (bf16[2048,128]{1,0:T(8,128)(2,1)S(1)}, f32[8,2048]{1,0:T(8,128)S(1)}) custom-call(s32[4]{0:T(128)S(1)} %iota_xor_fusion.table, bf16[2048,384]{1,0:T(8,128)(2,1)S(1)} %project_more.2.q_ref.k_ref.v_ref, bf16[2048,384]{1,0:T(8,128)(2,1)S(1)} %project_more.2.q_ref.k_ref.v_ref, bf16[2048,384]{1,0:T(8,128)(2,1)S(1)} %project_more.2.q_ref.k_ref.v_ref, ...), custom_call_target="tpu_custom_call" | custom-call | flops 200000000 | bytes 150000 | tf_op jit(solution)/shard_map/attend/pallas_call | solution.py:115
  119.9 10.4 %gelu_up.4 = (bf16[2048,512]{1,0:T(8,128)(2,1)S(1)}, bf16[2048,512]{1,0:T(8,128)(2,1)}) custom-call(s32[4]{0:T(128)S(1)} %get-tuple-element.558.slots.in_slots, bf16[2048,1024]{1,0:T(8,128)(2,1)} %get-tuple-element.287.a_ref, bf16[4,256,512]{2,1,0:T(8,128)(2,1)} %pad_maximum_fusion.weight_ref.refs_5_.in_mine, f32[2,896]{1,0:T(2,128)S(1)} %get-tuple-element.604.bias_ref), custom_call_target="tpu_custom_call" | custom-call | flops 250000000 | bytes 500000 | tf_op jit(solution)/shard_map/gelu_up/pallas_call | solution.py:389
  139.5 10.4 %gelu_up.5 = (bf16[2048,512]{1,0:T(8,128)(2,1)S(1)}, bf16[2048,512]{1,0:T(8,128)(2,1)}) custom-call(s32[4]{0:T(128)S(1)} %get-tuple-element.558.slots.in_slots, bf16[2048,1024]{1,0:T(8,128)(2,1)} %get-tuple-element.287.a_ref, bf16[4,256,512]{2,1,0:T(8,128)(2,1)} %copy-done.66, f32[2,896]{1,0:T(2,128)S(1)} %get-tuple-element.604.bias_ref), custom_call_target="tpu_custom_call" | custom-call | flops 250000000 | bytes 500000 | tf_op jit(solution)/shard_map/gelu_up/pallas_call | solution.py:389
  186.1 21.2 %collective-permute-done.25 = bf16[512,1024]{1,0:T(8,128)(2,1)} collective-permute-done((bf16[512,1024]{1,0:T(8,128)(2,1)}, bf16[512,1024]{1,0:T(8,128)(2,1)}, u32[]{:S(2)}, u32[]{:S(2)}) %collective-permute-start.25) | collective-permute-done | bytes 1048608 | tf_op jit(solution)/shard_map/ppermute | solution.py:33
  212.3 24.0 %collective-permute-done.28.h2 = bf16[512,1024]{1,0:T(8,128)(2,1)} collective-permute-done((bf16[512,1024]{1,0:T(8,128)(2,1)}, bf16[512,1024]{1,0:T(8,128)(2,1)}, u32[]{:S(2)}, u32[]{:S(2)}) %collective-permute-start.28) | collective-permute-done | bytes 1048608 | tf_op jit(solution)/shard_map/ppermute | solution.py:33
  239.7 10.0 %project.3 = (bf16[2048,384]{1,0:T(8,128)(2,1)S(1)}, bf16[2048,1024]{1,0:T(8,128)(2,1)S(1)}, bf16[2048,1024]{1,0:T(8,128)(2,1)S(1)}, bf16[1024,2048]{1,0:T(8,128)(2,1)S(1)}) custom-call(s32[4]{0:T(128)S(1)} %get-tuple-element.558.slots.in_slots, bf16[512,1024]{1,0:T(8,128)(2,1)} %get-tuple-element.306.h0, bf16[512,1024]{1,0:T(8,128)(2,1)} %collective-permute-done.27.h1, ...), custom_call_target="tpu_custom_call" | custom-call | flops 200000000 | bytes 900000 | tf_op jit(solution)/shard_map/project/pallas_call | solution.py:332
  255.7 11.8 %attend.6 = (bf16[2048,128]{1,0:T(8,128)(2,1)S(1)}, f32[8,2048]{1,0:T(8,128)S(1)}) custom-call(s32[4]{0:T(128)S(1)} %iota_xor_fusion.table, bf16[2048,384]{1,0:T(8,128)(2,1)S(1)} %get-tuple-element.310.q_ref.k_ref.v_ref, bf16[2048,384]{1,0:T(8,128)(2,1)S(1)} %get-tuple-element.310.q_ref.k_ref.v_ref, ...), custom_call_target="tpu_custom_call" | custom-call | flops 200000000 | bytes 150000 | tf_op jit(solution)/shard_map/attend/pallas_call | solution.py:115
  279.1 11.8 %attend.7 = (bf16[2048,128]{1,0:T(8,128)(2,1)S(1)}, f32[8,2048]{1,0:T(8,128)S(1)}) custom-call(s32[4]{0:T(128)S(1)} %iota_xor_fusion.table, bf16[2048,384]{1,0:T(8,128)(2,1)S(1)} %project_more.3.q_ref.k_ref.v_ref, bf16[2048,384]{1,0:T(8,128)(2,1)S(1)} %project_more.3.q_ref.k_ref.v_ref, bf16[2048,384]{1,0:T(8,128)(2,1)S(1)} %project_more.3.q_ref.k_ref.v_ref, ...), custom_call_target="tpu_custom_call" | custom-call | flops 200000000 | bytes 150000 | tf_op jit(solution)/shard_map/attend/pallas_call | solution.py:115
  298.3 9.5 %gelu_up.7 = (bf16[2048,512]{1,0:T(8,128)(2,1)S(1)}, bf16[2048,512]{1,0:T(8,128)(2,1)S(1)}) custom-call(s32[4]{0:T(128)S(1)} %iota_add_fusion.5.slots.in_slots, bf16[2048,1024]{1,0:T(8,128)(2,1)S(1)} %copy-done.21, bf16[4,256,512]{2,1,0:T(8,128)(2,1)} %collective-permute-done.30.weight_ref.refs_5_.in_other, f32[2,896]{1,0:T(2,128)S(1)} %get-tuple-element.603.bias_ref), custom_call_target="tpu_custom_call" | custom-call | flops 250000000 | bytes 500000 | tf_op jit(solution)/shard_map/gelu_up/pallas_call | solution.py:389
  317.9 10.5 %weight_grads.8 = (bf16[4,256,1152]{2,1,0:T(8,128)(2,1)}, f32[8,1024]{1,0:T(8,128)}, f32[8,512]{1,0:T(8,128)}) custom-call(s32[4]{0:T(128)S(1)} %iota_add_fusion.5.slots.in_slots, bf16[1024,2048]{1,0:T(8,128)(2,1)S(1)} %copy-done.4, bf16[1024,2048]{1,0:T(8,128)(2,1)S(1)} %get-tuple-element.364.refs_1_, ...), custom_call_target="tpu_custom_call" | custom-call | flops 241591904 | bytes 400000 | tf_op jit(solution)/shard_map/weight_grads/pallas_call | solution.py:575
  328.7 21.3 %attend_back.4.refs_1_.proj_other = bf16[2048,384]{1,0:T(8,128)(2,1)} custom-call(s32[4]{0:T(128)S(1)} %iota_xor_fusion.table, bf16[2048,384]{1,0:T(8,128)(2,1)S(1)} %project_more.3.q_ref.k_ref.v_ref, bf16[2048,384]{1,0:T(8,128)(2,1)S(1)} %project_more.3.q_ref.k_ref.v_ref, bf16[2048,384]{1,0:T(8,128)(2,1)S(1)} %project_more.3.q_ref.k_ref.v_ref, ...), custom_call_target="tpu_custom_call" | custom-call | flops 500000000 | bytes 300000 | tf_op jit(solution)/shard_map/attend_back/pallas_call | solution.py:215
  357.2 21.3 %attend_back.5.proj_mine.refs_1_ = bf16[2048,384]{1,0:T(8,128)(2,1)} custom-call(s32[4]{0:T(128)S(1)} %iota_xor_fusion.table, bf16[2048,384]{1,0:T(8,128)(2,1)S(1)} %copy-done.27, bf16[2048,384]{1,0:T(8,128)(2,1)S(1)} %copy-done.27, bf16[2048,384]{1,0:T(8,128)(2,1)S(1)} %copy-done.27, bf16[2048,128]{1,0:T(8,128)(2,1)S(1)} %get-tuple-element.350.gm_ref, ...), custom_call_target="tpu_custom_call" | custom-call | flops 500000000 | bytes 300000 | tf_op jit(solution)/shard_map/attend_back/pallas_call | solution.py:215
  403.6 9.6 %weight_grads.10 = (bf16[4,256,1152]{2,1,0:T(8,128)(2,1)}, f32[8,1024]{1,0:T(8,128)}, f32[8,512]{1,0:T(8,128)}) custom-call(s32[4]{0:T(128)S(1)} %iota_add_fusion.5.slots.in_slots, bf16[1024,2048]{1,0:T(8,128)(2,1)S(1)} %copy-done.4, bf16[1024,2048]{1,0:T(8,128)(2,1)S(1)} %get-tuple-element.364.refs_1_, bf16[2048,512]{1,0:T(8,128)(2,1)S(1)} %copy-done.11, ...), custom_call_target="tpu_custom_call" | custom-call | flops 241591904 | bytes 400000 | tf_op jit(solution)/shard_map/weight_grads/pallas_call | solution.py:575
  439.6 9.3 %collective-permute-done.39.refs_4_ = bf16[4,256,384]{2,1,0:T(8,128)(2,1)S(1)} collective-permute-done((bf16[4,256,384]{2,1,0:T(8,128)(2,1)}, bf16[4,256,384]{2,1,0:T(8,128)(2,1)S(1)}, u32[]{:S(2)}, u32[]{:S(2)}) %collective-permute-start.39) | collective-permute-done | bytes 786464 | tf_op jit(solution)/shard_map/ppermute | solution.py:33
  458.9 11.6 %down_back.3 = (bf16[2048,128]{1,0:T(8,128)(2,1)S(1)}, bf16[2048,128]{1,0:T(8,128)(2,1)S(1)}, bf16[2048,512]{1,0:T(8,128)(2,1)}, bf16[2048,512]{1,0:T(8,128)(2,1)}, bf16[1024,2048]{1,0:T(8,128)(2,1)}) custom-call(s32[4]{0:T(128)S(1)} %iota_add_fusion.5.slots.in_slots, bf16[512,1024]{1,0:T(8,128)(2,1)S(1)} %fusion.16.g0, ...), custom_call_target="tpu_custom_call" | custom-call | flops 400000000 | bytes 900000 | tf_op jit(solution)/shard_map/down_back/pallas_call | solution.py:461
  474.3 10.7 %weight_grads.12 = (bf16[4,256,1152]{2,1,0:T(8,128)(2,1)}, f32[8,1024]{1,0:T(8,128)}, f32[8,512]{1,0:T(8,128)}) custom-call(s32[4]{0:T(128)S(1)} %get-tuple-element.558.slots.in_slots, bf16[1024,2048]{1,0:T(8,128)(2,1)} %get-tuple-element.428.refs_0_, bf16[1024,2048]{1,0:T(8,128)(2,1)S(1)} %copy-done.22, bf16[2048,512]{1,0:T(8,128)(2,1)S(1)} %copy-done.17, ...), custom_call_target="tpu_custom_call" | custom-call | flops 241591904 | bytes 400000 | tf_op jit(solution)/shard_map/weight_grads/pallas_call | solution.py:575
  486.4 22.5 %attend_back.6.refs_1_.proj_other = bf16[2048,384]{1,0:T(8,128)(2,1)} custom-call(s32[4]{0:T(128)S(1)} %iota_xor_fusion.table, bf16[2048,384]{1,0:T(8,128)(2,1)} %copy-done.6, bf16[2048,384]{1,0:T(8,128)(2,1)} %copy-done.6, bf16[2048,384]{1,0:T(8,128)(2,1)} %copy-done.6, bf16[2048,128]{1,0:T(8,128)(2,1)S(1)} %get-tuple-element.404.gm_ref, ...), custom_call_target="tpu_custom_call" | custom-call | flops 500000000 | bytes 300000 | tf_op jit(solution)/shard_map/attend_back/pallas_call | solution.py:215
  518.3 10.7 %weight_grads.14 = (bf16[4,256,1152]{2,1,0:T(8,128)(2,1)}, f32[8,1024]{1,0:T(8,128)}, f32[8,512]{1,0:T(8,128)}) custom-call(s32[4]{0:T(128)S(1)} %get-tuple-element.558.slots.in_slots, bf16[1024,2048]{1,0:T(8,128)(2,1)} %get-tuple-element.428.refs_0_, bf16[1024,2048]{1,0:T(8,128)(2,1)S(1)} %copy-done.23, bf16[2048,512]{1,0:T(8,128)(2,1)S(1)} %copy-done.16, ...), custom_call_target="tpu_custom_call" | custom-call | flops 241591904 | bytes 400000 | tf_op jit(solution)/shard_map/weight_grads/pallas_call | solution.py:575
  544.6 22.1 %attend_back.7.refs_1_.proj_mine = bf16[2048,384]{1,0:T(8,128)(2,1)} custom-call(s32[4]{0:T(128)S(1)} %iota_xor_fusion.table, bf16[2048,384]{1,0:T(8,128)(2,1)} %copy-done.25, bf16[2048,384]{1,0:T(8,128)(2,1)} %copy-done.25, bf16[2048,384]{1,0:T(8,128)(2,1)} %copy-done.25, bf16[2048,128]{1,0:T(8,128)(2,1)S(1)} %get-tuple-element.424.gm_ref, ...), custom_call_target="tpu_custom_call" | custom-call | flops 500000000 | bytes 300000 | tf_op jit(solution)/shard_map/attend_back/pallas_call | solution.py:215
  607.1 10.1 %collective-permute-done.45 = bf16[512,1024]{1,0:T(8,128)(2,1)S(1)} collective-permute-done((bf16[512,1024]{1,0:T(8,128)(2,1)S(1)}, bf16[512,1024]{1,0:T(8,128)(2,1)S(1)}, u32[]{:S(2)}, u32[]{:S(2)}) %collective-permute-start.45) | collective-permute-done | bytes 1048608 | tf_op jit(solution)/shard_map/ppermute | solution.py:33
  620.2 10.1 %collective-permute-done.47 = bf16[512,1024]{1,0:T(8,128)(2,1)} collective-permute-done((bf16[512,1024]{1,0:T(8,128)(2,1)}, bf16[512,1024]{1,0:T(8,128)(2,1)}, u32[]{:S(2)}, u32[]{:S(2)}) %collective-permute-start.47) | collective-permute-done | bytes 1048608 | tf_op jit(solution)/shard_map/ppermute | solution.py:33
  666.0 9.9 %collective-permute-done.51 = bf16[512,1024]{1,0:T(8,128)(2,1)} collective-permute-done((bf16[512,1024]{1,0:T(8,128)(2,1)}, bf16[512,1024]{1,0:T(8,128)(2,1)}, u32[]{:S(2)}, u32[]{:S(2)}) %collective-permute-start.51) | collective-permute-done | bytes 1048608 | tf_op jit(solution)/shard_map/ppermute | solution.py:33
  (583 shorter events, 351.1 us)
Async XLA Ops:
  7.2 124.5 %all-gather.4.cloned.1.call-start = ((), (), s32[]{:S(2)}) async-start(), calls=%async_computation.5 | async-start | bytes 1638400 | tf_op jit(solution)/shard_map/all_gather | solution.py:694
  22.9 35.1 %collective-permute-start.8 = (bf16[512,1024]{1,0:T(8,128)(2,1)}, bf16[512,1024]{1,0:T(8,128)(2,1)}, u32[]{:S(2)}, u32[]{:S(2)}) collective-permute-start(bf16[512,1024]{1,0:T(8,128)(2,1)} %select_bitcast_fusion.3.h0), channel_id=1, source_target_pairs={{0,4},{4,0},{8,12},{12,8},{1,5},{5,1},{9,13},{13,9},{2,6},{6,2},{1... | collective-permute-start | bytes 3145736 | tf_op jit(solution)/shard_map/ppermute | solution.py:33
  58.0 34.3 %collective-permute-start.14 = (bf16[4,288,384]{2,1,0:T(8,128)(2,1)}, bf16[4,288,384]{2,1,0:T(8,128)(2,1)}, u32[]{:S(2)}, u32[]{:S(2)}) collective-permute-start(bf16[4,288,384]{2,1,0:T(8,128)(2,1)} %copy-done.7), channel_id=1, source_target_pairs={{0,16},{16,0},{1,17},{17,1},{2,18},{18,2},{3,19},{19,3},{4,20},{20... | collective-permute-start | bytes 2654216 | tf_op jit(solution)/shard_map/ppermute | solution.py:33
  59.8 30.2 %collective-permute-start.11 = (bf16[256,512]{1,0:T(8,128)(2,1)}, bf16[256,512]{1,0:T(8,128)(2,1)}, u32[]{:S(2)}, u32[]{:S(2)}) collective-permute-start(bf16[256,512]{1,0:T(8,128)(2,1)} %slice_select_fusion.1), channel_id=1, source_target_pairs={{0,1},{1,2},{2,3},{3,0},{4,5},{5,6},{6,7},{7,4},{8,9},{9,10},{10,1... | collective-permute-start | bytes 786440 | tf_op jit(solution)/shard_map/ppermute | solution.py:623
  60.6 29.5 %collective-permute-start.12 = (bf16[256,512]{1,0:T(8,128)(2,1)}, bf16[256,512]{1,0:T(8,128)(2,1)}, u32[]{:S(2)}, u32[]{:S(2)}) collective-permute-start(bf16[256,512]{1,0:T(8,128)(2,1)} %slice_select_fusion.1), channel_id=1, source_target_pairs={{0,2},{1,3},{2,0},{3,1},{4,6},{5,7},{6,4},{7,5},{8,10},{9,11},{10,... | collective-permute-start | bytes 786440 | tf_op jit(solution)/shard_map/ppermute | solution.py:623
  61.0 29.0 %collective-permute-start.13 = (bf16[256,512]{1,0:T(8,128)(2,1)}, bf16[256,512]{1,0:T(8,128)(2,1)}, u32[]{:S(2)}, u32[]{:S(2)}) collective-permute-start(bf16[256,512]{1,0:T(8,128)(2,1)} %slice_select_fusion.1), channel_id=1, source_target_pairs={{0,3},{1,0},{2,1},{3,2},{4,7},{5,4},{6,5},{7,6},{8,11},{9,8},{10,9... | collective-permute-start | bytes 786440 | tf_op jit(solution)/shard_map/ppermute | solution.py:623
  92.3 144.5 %all-gather.6.cloned.1.call-start = ((), (), s32[]{:S(2)}) async-start(), calls=%async_computation.6 | async-start | bytes 1310720 | tf_op jit(solution)/shard_map/all_gather | solution.py:694
  131.6 27.4 %collective-permute-start.20 = (bf16[4,256,640]{2,1,0:T(8,128)(2,1)}, bf16[4,256,640]{2,1,0:T(8,128)(2,1)}, u32[]{:S(2)}, u32[]{:S(2)}) collective-permute-start(bf16[4,256,640]{2,1,0:T(8,128)(2,1)} %bitcast.174), channel_id=1, source_target_pairs={{0,16},{16,0},{1,17},{17,1},{2,18},{18,2},{3,19},{19,3},{4,20},{20... | collective-permute-start | bytes 3932168 | tf_op jit(solution)/shard_map/ppermute | solution.py:33
  184.0 27.4 %collective-permute-start.26 = (bf16[4,256,384]{2,1,0:T(8,128)(2,1)}, bf16[4,256,384]{2,1,0:T(8,128)(2,1)}, u32[]{:S(2)}, u32[]{:S(2)}) collective-permute-start(bf16[4,256,384]{2,1,0:T(8,128)(2,1)} %pad_maximum_fusion.2.weight_ref.qkv_mine.refs_2_), channel_id=1, source_target_pairs={{0,16},{16,0},{1,17},{17,1},{2,18},{18,2},{3,19},{19,3},{4,20},{20... | collective-permute-start | bytes 2359304 | tf_op jit(solution)/shard_map/ppermute | solution.py:33
  184.3 85.2 %all-gather.8.cloned.1.call-start = ((), (), s32[]{:S(2)}) async-start(), calls=%async_computation.7 | async-start | bytes 1638400 | tf_op jit(solution)/shard_map/all_gather | solution.py:694
  236.4 248.6 %reduce-scatter.6.cloned.1.call-start = ((), (), s32[]{:S(2)}) async-start(), calls=%async_computation.8 | async-start | bytes 2949120 | tf_op jit(solution)/shard_map/reduce_scatter | solution.py:627
  239.4 30.2 %collective-permute-start.30 = (bf16[4,256,512]{2,1,0:T(8,128)(2,1)}, bf16[4,256,512]{2,1,0:T(8,128)(2,1)}, u32[]{:S(2)}, u32[]{:S(2)}) collective-permute-start(bf16[4,256,512]{2,1,0:T(8,128)(2,1)} %bitcast.165), channel_id=1, source_target_pairs={{0,16},{16,0},{1,17},{17,1},{2,18},{18,2},{3,19},{19,3},{4,20},{20... | collective-permute-start | bytes 3145736 | tf_op jit(solution)/shard_map/ppermute | solution.py:33
  269.6 38.2 %collective-permute-start.31 = (bf16[4,256,640]{2,1,0:T(8,128)(2,1)}, bf16[4,256,640]{2,1,0:T(8,128)(2,1)S(1)}, u32[]{:S(2)}, u32[]{:S(2)}) collective-permute-start(bf16[4,256,640]{2,1,0:T(8,128)(2,1)} %bitcast.170), channel_id=1, source_target_pairs={{0,16},{16,0},{1,17},{17,1},{2,18},{18,2},{3,19},{19,3},{4,20},{20... | collective-permute-start | bytes 3932168 | tf_op jit(solution)/shard_map/ppermute | solution.py:33
  328.4 53.0 %collective-permute-start.32 = (bf16[4,256,1152]{2,1,0:T(8,128)(2,1)}, bf16[4,256,1152]{2,1,0:T(8,128)(2,1)S(1)}, u32[]{:S(2)}, u32[]{:S(2)}) collective-permute-start(bf16[4,256,1152]{2,1,0:T(8,128)(2,1)} %get-tuple-element.353), channel_id=1, source_target_pairs={{0,16},{16,0},{1,17},{17,1},{2,18},{18,2},{3,19},{19,3},{4,20},{20... | collective-permute-start | bytes 7077896 | tf_op jit(solution)/shard_map/ppermute | solution.py:33
  392.9 29.4 %collective-permute-start.35 = (bf16[512,1024]{1,0:T(8,128)(2,1)S(1)}, bf16[512,1024]{1,0:T(8,128)(2,1)S(1)}, u32[]{:S(2)}, u32[]{:S(2)}) collective-permute-start(bf16[512,1024]{1,0:T(8,128)(2,1)S(1)} %add_convert_fusion.3), channel_id=1, source_target_pairs={{0,8},{4,12},{8,0},{12,4},{1,9},{5,13},{9,1},{13,5},{2,10},{6,14},... | collective-permute-start | bytes 3145736 | tf_op jit(solution)/shard_map/ppermute | solution.py:33
  428.1 104.1 %reduce-scatter.8.cloned.1.call-start = ((), (), s32[]{:S(2)}) async-start(), calls=%async_computation.9 | async-start | bytes 983040 | tf_op jit(solution)/shard_map/reduce_scatter | solution.py:627
  428.2 28.0 %collective-permute-start.38 = (bf16[512,1024]{1,0:T(8,128)(2,1)S(1)}, bf16[512,1024]{1,0:T(8,128)(2,1)S(1)}, u32[]{:S(2)}, u32[]{:S(2)}) collective-permute-start(bf16[512,1024]{1,0:T(8,128)(2,1)S(1)} %fusion.16.g0), channel_id=1, source_target_pairs={{0,8},{4,12},{8,0},{12,4},{1,9},{5,13},{9,1},{13,5},{2,10},{6,14},... | collective-permute-start | bytes 3145736 | tf_op jit(solution)/shard_map/ppermute | solution.py:33
  429.8 26.4 %collective-permute-start.37 = (bf16[512,1024]{1,0:T(8,128)(2,1)S(1)}, bf16[512,1024]{1,0:T(8,128)(2,1)S(1)}, u32[]{:S(2)}, u32[]{:S(2)}) collective-permute-start(bf16[512,1024]{1,0:T(8,128)(2,1)S(1)} %fusion.16.g0), channel_id=1, source_target_pairs={{0,4},{4,0},{8,12},{12,8},{1,5},{5,1},{9,13},{13,9},{2,6},{6,2},{1... | collective-permute-start | bytes 3145736 | tf_op jit(solution)/shard_map/ppermute | solution.py:33
  485.0 53.6 %collective-permute-start.42 = (bf16[4,256,1152]{2,1,0:T(8,128)(2,1)}, bf16[4,256,1152]{2,1,0:T(8,128)(2,1)}, u32[]{:S(2)}, u32[]{:S(2)}) collective-permute-start(bf16[4,256,1152]{2,1,0:T(8,128)(2,1)} %get-tuple-element.416), channel_id=1, source_target_pairs={{0,16},{16,0},{1,17},{17,1},{2,18},{18,2},{3,19},{19,3},{4,20},{20... | collective-permute-start | bytes 7077896 | tf_op jit(solution)/shard_map/ppermute | solution.py:33
  485.4 89.1 %reduce-scatter.10.cloned.1.call-start = ((), (), s32[]{:S(2)}) async-start(), calls=%async_computation.10 | async-start | bytes 1310720 | tf_op jit(solution)/shard_map/reduce_scatter | solution.py:627
  486.4 42.6 %collective-permute-start.43 = (bf16[512,1024]{1,0:T(8,128)(2,1)}, bf16[512,1024]{1,0:T(8,128)(2,1)S(1)}, u32[]{:S(2)}, u32[]{:S(2)}) collective-permute-start(bf16[512,1024]{1,0:T(8,128)(2,1)} %copy-done.64), channel_id=1, source_target_pairs={{0,4},{4,0},{8,12},{12,8},{1,5},{5,1},{9,13},{13,9},{2,6},{6,2},{1... | collective-permute-start | bytes 3145736 | tf_op jit(solution)/shard_map/ppermute | solution.py:33
  544.1 76.1 %reduce-scatter.12.cloned.1.call-start = ((), (), s32[]{:S(2)}) async-start(), calls=%async_computation.11 | async-start | bytes 983040 | tf_op jit(solution)/shard_map/reduce_scatter | solution.py:627
  574.6 55.8 %reduce-scatter.14.cloned.1.call-start = ((), (), s32[]{:S(2)}) async-start(), calls=%async_computation.12 | async-start | bytes 1638400 | tf_op jit(solution)/shard_map/reduce_scatter | solution.py:627
  648.4 27.5 %collective-permute-start.51 = (bf16[512,1024]{1,0:T(8,128)(2,1)}, bf16[512,1024]{1,0:T(8,128)(2,1)}, u32[]{:S(2)}, u32[]{:S(2)}) collective-permute-start(bf16[512,1024]{1,0:T(8,128)(2,1)} %get-tuple-element.549), channel_id=1, source_target_pairs={{0,16},{16,0},{1,17},{17,1},{2,18},{18,2},{3,19},{19,3},{4,20},{20... | collective-permute-start | bytes 3145736 | tf_op jit(solution)/shard_map/ppermute | solution.py:33
  (155 other events, 2232.5 us)
Sparse Core Ops, SparseCore 0:
  92.5 31.2 all-gather.3
  184.5 26.8 all-gather.5
  236.5 30.4 all-gather.7
  428.2 45.6 reduce-scatter.5
  485.5 21.7 reduce-scatter.7
  544.2 24.4 reduce-scatter.9
  574.7 21.7 reduce-scatter.11
  599.5 30.4 reduce-scatter.13

commit v4 on v3

--- a/solution.py
+++ b/solution.py
@@ -905,7 +905,7 @@
     total = pick(packed[0], packed[1]) + flip(pick(packed[1], packed[0]), "section")
     total = chosen(total, order, 0)
     small_sum = total[0::2] + flip(total[1::2], "tensor", 1)
-    far, small_sum, reduced_qkv0, reduced_out0, *near = pin(far, small_sum, reduced_qkv0, reduced_out0, *near)
+    far, small_sum, reduced_qkv0, reduced_out0, act_got = pin(far, small_sum, reduced_qkv0, reduced_out0, act_got)
     near = near[0].astype(f32) + near[1].astype(f32)
     grad0 = input_back(h_own, grad1_low, near + far.astype(f32))
     grad_got = flip(pick(grad1_low, grad0.astype(bf16)), "section")

time: 699 us -> 699 us (level)
  transfers between devices with their start and end apart: 66 -> 66, of which waited for: 26 -> 25; matrix products, arithmetic and copies ran while one was open for 12% -> 12% of each run, Pallas kernels for 46% -> 46%
where the time goes in v4:
time: 699 us; the launch traced here: 690 us
  Pallas kernels  360 us (52%)
  waiting for transfers between devices  132 us (19%)
  other arithmetic  77.6 us (11%)
  local copies, waits for them, and re-layouts  58.4 us (8%)
  starting transfers between devices  46.2 us (7%)
  between operations  16.3 us (2%)
    ppermute x46, waiting for transfers between devices, flip(): lax.ppermute(block, axis, [(i, i ^ bit) for i in range(lax.axis_size(axis...  127 us
    pallas_call x4, Pallas kernels, attend_back(): pl.pallas_call(functools.partial(attend_back_kernel, shard_rows), grid_sp...  87.2 us
    pallas_call x8, Pallas kernels, weight_grads(): call(functools.partial(grads_kernel, len(ups), len(downs), got is not Non...  71.3 us
    pallas_call x4, Pallas kernels, attend(): pl.pallas_call(functools.partial(attend_kernel, shard_rows), grid_spec=pl...  47.3 us
    pallas_call x4, Pallas kernels, gelu_up(): call(functools.partial(gelu_kernel, part), 'gelu_up', (seq // rows,), [pl...  37.5 us
    unnamed x233, local copies, waits for them, and re-layouts  36.1 us
    pallas_call x4, Pallas kernels, up_back(): call(up_back_kernel, 'up_back', (steps,), [pl.BlockSpec((rows, x.shape[1]...  34.2 us
    pallas_call x4, Pallas kernels, down(): call(down_kernel, 'down', (steps,), [pl.BlockSpec((rows, x.shape[1]), lam...  29.3 us
  transfers between devices with their start and end apart: 66, of which 25 were waited for; matrix products, arithmetic and copies ran while one was open for 12% of the time, Pallas kernels for 46%

profile of v4, /device:TPU:0, one launch (start us, length us, event | category | flops | bytes accessed | tf_op | source)
XLA Modules:
  0.0 690.3 jit_solution(4379736387636661624)
XLA Ops:
  64.1 10.9 %project.2 = (bf16[2048,384]{1,0:T(8,128)(2,1)S(1)}, bf16[2048,1024]{1,0:T(8,128)(2,1)}, bf16[2048,1024]{1,0:T(8,128)(2,1)}, bf16[1024,2048]{1,0:T(8,128)(2,1)}) custom-call(s32[4]{0:T(128)S(1)} %get-tuple-element.556.slots.in_slots, bf16[512,1024]{1,0:T(8,128)(2,1)} %select_bitcast_fusion.3.h0, bf16[512,1024]{1,0:T(8,128)(2,1)} %collective-permute-done.8.h1, ...), custom_call_target="tpu_custom_call" | custom-call | flops 200000000 | bytes 900000 | tf_op jit(solution)/shard_map/project/pallas_call | solution.py:332
  74.9 11.8 %attend.4 = (bf16[2048,128]{1,0:T(8,128)(2,1)S(1)}, f32[8,2048]{1,0:T(8,128)S(1)}) custom-call(s32[4]{0:T(128)S(1)} %iota_xor_fusion.table, bf16[2048,384]{1,0:T(8,128)(2,1)S(1)} %get-tuple-element.269.q_ref.k_ref.v_ref, bf16[2048,384]{1,0:T(8,128)(2,1)S(1)} %get-tuple-element.269.q_ref.k_ref.v_ref, ...), custom_call_target="tpu_custom_call" | custom-call | flops 200000000 | bytes 150000 | tf_op jit(solution)/shard_map/attend/pallas_call | solution.py:115
  103.6 11.8 %attend.5 = (bf16[2048,128]{1,0:T(8,128)(2,1)S(1)}, f32[8,2048]{1,0:T(8,128)S(1)}) custom-call(s32[4]{0:T(128)S(1)} %iota_xor_fusion.table, bf16[2048,384]{1,0:T(8,128)(2,1)S(1)} %project_more.2.q_ref.k_ref.v_ref, bf16[2048,384]{1,0:T(8,128)(2,1)S(1)} %project_more.2.q_ref.k_ref.v_ref, bf16[2048,384]{1,0:T(8,128)(2,1)S(1)} %project_more.2.q_ref.k_ref.v_ref, ...), custom_call_target="tpu_custom_call" | custom-call | flops 200000000 | bytes 150000 | tf_op jit(solution)/shard_map/attend/pallas_call | solution.py:115
  120.0 10.4 %gelu_up.4 = (bf16[2048,512]{1,0:T(8,128)(2,1)S(1)}, bf16[2048,512]{1,0:T(8,128)(2,1)}) custom-call(s32[4]{0:T(128)S(1)} %get-tuple-element.556.slots.in_slots, bf16[2048,1024]{1,0:T(8,128)(2,1)} %get-tuple-element.286.a_ref, bf16[4,256,512]{2,1,0:T(8,128)(2,1)} %pad_maximum_fusion.weight_ref.refs_5_.in_mine, f32[2,896]{1,0:T(2,128)S(1)} %get-tuple-element.602.bias_ref), custom_call_target="tpu_custom_call" | custom-call | flops 250000000 | bytes 500000 | tf_op jit(solution)/shard_map/gelu_up/pallas_call | solution.py:389
  139.5 10.4 %gelu_up.5 = (bf16[2048,512]{1,0:T(8,128)(2,1)S(1)}, bf16[2048,512]{1,0:T(8,128)(2,1)}) custom-call(s32[4]{0:T(128)S(1)} %get-tuple-element.556.slots.in_slots, bf16[2048,1024]{1,0:T(8,128)(2,1)} %get-tuple-element.286.a_ref, bf16[4,256,512]{2,1,0:T(8,128)(2,1)} %copy-done.66, f32[2,896]{1,0:T(2,128)S(1)} %get-tuple-element.602.bias_ref), custom_call_target="tpu_custom_call" | custom-call | flops 250000000 | bytes 500000 | tf_op jit(solution)/shard_map/gelu_up/pallas_call | solution.py:389
  186.2 21.2 %collective-permute-done.25 = bf16[512,1024]{1,0:T(8,128)(2,1)} collective-permute-done((bf16[512,1024]{1,0:T(8,128)(2,1)}, bf16[512,1024]{1,0:T(8,128)(2,1)}, u32[]{:S(2)}, u32[]{:S(2)}) %collective-permute-start.25) | collective-permute-done | bytes 1048608 | tf_op jit(solution)/shard_map/ppermute | solution.py:33
  212.4 24.0 %collective-permute-done.28.h2 = bf16[512,1024]{1,0:T(8,128)(2,1)} collective-permute-done((bf16[512,1024]{1,0:T(8,128)(2,1)}, bf16[512,1024]{1,0:T(8,128)(2,1)}, u32[]{:S(2)}, u32[]{:S(2)}) %collective-permute-start.28) | collective-permute-done | bytes 1048608 | tf_op jit(solution)/shard_map/ppermute | solution.py:33
  239.7 10.0 %project.3 = (bf16[2048,384]{1,0:T(8,128)(2,1)S(1)}, bf16[2048,1024]{1,0:T(8,128)(2,1)S(1)}, bf16[2048,1024]{1,0:T(8,128)(2,1)S(1)}, bf16[1024,2048]{1,0:T(8,128)(2,1)S(1)}) custom-call(s32[4]{0:T(128)S(1)} %get-tuple-element.556.slots.in_slots, bf16[512,1024]{1,0:T(8,128)(2,1)} %get-tuple-element.305.h0, bf16[512,1024]{1,0:T(8,128)(2,1)} %collective-permute-done.27.h1, ...), custom_call_target="tpu_custom_call" | custom-call | flops 200000000 | bytes 900000 | tf_op jit(solution)/shard_map/project/pallas_call | solution.py:332
  255.8 11.8 %attend.6 = (bf16[2048,128]{1,0:T(8,128)(2,1)S(1)}, f32[8,2048]{1,0:T(8,128)S(1)}) custom-call(s32[4]{0:T(128)S(1)} %iota_xor_fusion.table, bf16[2048,384]{1,0:T(8,128)(2,1)S(1)} %get-tuple-element.309.q_ref.k_ref.v_ref, bf16[2048,384]{1,0:T(8,128)(2,1)S(1)} %get-tuple-element.309.q_ref.k_ref.v_ref, ...), custom_call_target="tpu_custom_call" | custom-call | flops 200000000 | bytes 150000 | tf_op jit(solution)/shard_map/attend/pallas_call | solution.py:115
  279.1 11.8 %attend.7 = (bf16[2048,128]{1,0:T(8,128)(2,1)S(1)}, f32[8,2048]{1,0:T(8,128)S(1)}) custom-call(s32[4]{0:T(128)S(1)} %iota_xor_fusion.table, bf16[2048,384]{1,0:T(8,128)(2,1)S(1)} %project_more.3.q_ref.k_ref.v_ref, bf16[2048,384]{1,0:T(8,128)(2,1)S(1)} %project_more.3.q_ref.k_ref.v_ref, bf16[2048,384]{1,0:T(8,128)(2,1)S(1)} %project_more.3.q_ref.k_ref.v_ref, ...), custom_call_target="tpu_custom_call" | custom-call | flops 200000000 | bytes 150000 | tf_op jit(solution)/shard_map/attend/pallas_call | solution.py:115
  298.3 9.5 %gelu_up.7 = (bf16[2048,512]{1,0:T(8,128)(2,1)S(1)}, bf16[2048,512]{1,0:T(8,128)(2,1)S(1)}) custom-call(s32[4]{0:T(128)S(1)} %iota_add_fusion.5.slots.in_slots, bf16[2048,1024]{1,0:T(8,128)(2,1)S(1)} %copy-done.21, bf16[4,256,512]{2,1,0:T(8,128)(2,1)} %collective-permute-done.30.weight_ref.refs_5_.in_other, f32[2,896]{1,0:T(2,128)S(1)} %get-tuple-element.601.bias_ref), custom_call_target="tpu_custom_call" | custom-call | flops 250000000 | bytes 500000 | tf_op jit(solution)/shard_map/gelu_up/pallas_call | solution.py:389
  318.0 10.5 %weight_grads.8 = (bf16[4,256,1152]{2,1,0:T(8,128)(2,1)}, f32[8,1024]{1,0:T(8,128)}, f32[8,512]{1,0:T(8,128)}) custom-call(s32[4]{0:T(128)S(1)} %iota_add_fusion.5.slots.in_slots, bf16[1024,2048]{1,0:T(8,128)(2,1)S(1)} %copy-done.4, bf16[1024,2048]{1,0:T(8,128)(2,1)S(1)} %get-tuple-element.363.refs_1_, ...), custom_call_target="tpu_custom_call" | custom-call | flops 241591904 | bytes 400000 | tf_op jit(solution)/shard_map/weight_grads/pallas_call | solution.py:575
  328.7 21.3 %attend_back.4.refs_1_.proj_other = bf16[2048,384]{1,0:T(8,128)(2,1)} custom-call(s32[4]{0:T(128)S(1)} %iota_xor_fusion.table, bf16[2048,384]{1,0:T(8,128)(2,1)S(1)} %project_more.3.q_ref.k_ref.v_ref, bf16[2048,384]{1,0:T(8,128)(2,1)S(1)} %project_more.3.q_ref.k_ref.v_ref, bf16[2048,384]{1,0:T(8,128)(2,1)S(1)} %project_more.3.q_ref.k_ref.v_ref, ...), custom_call_target="tpu_custom_call" | custom-call | flops 500000000 | bytes 300000 | tf_op jit(solution)/shard_map/attend_back/pallas_call | solution.py:215
  357.2 21.3 %attend_back.5.proj_mine.refs_1_ = bf16[2048,384]{1,0:T(8,128)(2,1)} custom-call(s32[4]{0:T(128)S(1)} %iota_xor_fusion.table, bf16[2048,384]{1,0:T(8,128)(2,1)S(1)} %copy-done.27, bf16[2048,384]{1,0:T(8,128)(2,1)S(1)} %copy-done.27, bf16[2048,384]{1,0:T(8,128)(2,1)S(1)} %copy-done.27, bf16[2048,128]{1,0:T(8,128)(2,1)S(1)} %get-tuple-element.349.gm_ref, ...), custom_call_target="tpu_custom_call" | custom-call | flops 500000000 | bytes 300000 | tf_op jit(solution)/shard_map/attend_back/pallas_call | solution.py:215
  403.7 9.6 %weight_grads.10 = (bf16[4,256,1152]{2,1,0:T(8,128)(2,1)}, f32[8,1024]{1,0:T(8,128)}, f32[8,512]{1,0:T(8,128)}) custom-call(s32[4]{0:T(128)S(1)} %iota_add_fusion.5.slots.in_slots, bf16[1024,2048]{1,0:T(8,128)(2,1)S(1)} %copy-done.4, bf16[1024,2048]{1,0:T(8,128)(2,1)S(1)} %get-tuple-element.363.refs_1_, bf16[2048,512]{1,0:T(8,128)(2,1)S(1)} %copy-done.11, ...), custom_call_target="tpu_custom_call" | custom-call | flops 241591904 | bytes 400000 | tf_op jit(solution)/shard_map/weight_grads/pallas_call | solution.py:575
  439.6 9.3 %collective-permute-done.39.refs_4_ = bf16[4,256,384]{2,1,0:T(8,128)(2,1)S(1)} collective-permute-done((bf16[4,256,384]{2,1,0:T(8,128)(2,1)}, bf16[4,256,384]{2,1,0:T(8,128)(2,1)S(1)}, u32[]{:S(2)}, u32[]{:S(2)}) %collective-permute-start.39) | collective-permute-done | bytes 786464 | tf_op jit(solution)/shard_map/ppermute | solution.py:33
  458.9 11.6 %down_back.3 = (bf16[2048,128]{1,0:T(8,128)(2,1)S(1)}, bf16[2048,128]{1,0:T(8,128)(2,1)S(1)}, bf16[2048,512]{1,0:T(8,128)(2,1)}, bf16[2048,512]{1,0:T(8,128)(2,1)}, bf16[1024,2048]{1,0:T(8,128)(2,1)}) custom-call(s32[4]{0:T(128)S(1)} %iota_add_fusion.5.slots.in_slots, bf16[512,1024]{1,0:T(8,128)(2,1)S(1)} %fusion.16.g0, ...), custom_call_target="tpu_custom_call" | custom-call | flops 400000000 | bytes 900000 | tf_op jit(solution)/shard_map/down_back/pallas_call | solution.py:461
  474.3 10.7 %weight_grads.12 = (bf16[4,256,1152]{2,1,0:T(8,128)(2,1)}, f32[8,1024]{1,0:T(8,128)}, f32[8,512]{1,0:T(8,128)}) custom-call(s32[4]{0:T(128)S(1)} %get-tuple-element.556.slots.in_slots, bf16[1024,2048]{1,0:T(8,128)(2,1)} %get-tuple-element.427.refs_0_, bf16[1024,2048]{1,0:T(8,128)(2,1)S(1)} %copy-done.22, bf16[2048,512]{1,0:T(8,128)(2,1)S(1)} %copy-done.17, ...), custom_call_target="tpu_custom_call" | custom-call | flops 241591904 | bytes 400000 | tf_op jit(solution)/shard_map/weight_grads/pallas_call | solution.py:575
  486.5 22.5 %attend_back.6.refs_1_.proj_other = bf16[2048,384]{1,0:T(8,128)(2,1)} custom-call(s32[4]{0:T(128)S(1)} %iota_xor_fusion.table, bf16[2048,384]{1,0:T(8,128)(2,1)} %copy-done.6, bf16[2048,384]{1,0:T(8,128)(2,1)} %copy-done.6, bf16[2048,384]{1,0:T(8,128)(2,1)} %copy-done.6, bf16[2048,128]{1,0:T(8,128)(2,1)S(1)} %get-tuple-element.403.gm_ref, ...), custom_call_target="tpu_custom_call" | custom-call | flops 500000000 | bytes 300000 | tf_op jit(solution)/shard_map/attend_back/pallas_call | solution.py:215
  518.4 10.7 %weight_grads.14 = (bf16[4,256,1152]{2,1,0:T(8,128)(2,1)}, f32[8,1024]{1,0:T(8,128)}, f32[8,512]{1,0:T(8,128)}) custom-call(s32[4]{0:T(128)S(1)} %get-tuple-element.556.slots.in_slots, bf16[1024,2048]{1,0:T(8,128)(2,1)} %get-tuple-element.427.refs_0_, bf16[1024,2048]{1,0:T(8,128)(2,1)S(1)} %copy-done.23, bf16[2048,512]{1,0:T(8,128)(2,1)S(1)} %copy-done.16, ...), custom_call_target="tpu_custom_call" | custom-call | flops 241591904 | bytes 400000 | tf_op jit(solution)/shard_map/weight_grads/pallas_call | solution.py:575
  544.6 22.1 %attend_back.7.refs_1_.proj_mine = bf16[2048,384]{1,0:T(8,128)(2,1)} custom-call(s32[4]{0:T(128)S(1)} %iota_xor_fusion.table, bf16[2048,384]{1,0:T(8,128)(2,1)} %copy-done.25, bf16[2048,384]{1,0:T(8,128)(2,1)} %copy-done.25, bf16[2048,384]{1,0:T(8,128)(2,1)} %copy-done.25, bf16[2048,128]{1,0:T(8,128)(2,1)S(1)} %get-tuple-element.423.gm_ref, ...), custom_call_target="tpu_custom_call" | custom-call | flops 500000000 | bytes 300000 | tf_op jit(solution)/shard_map/attend_back/pallas_call | solution.py:215
  578.7 8.9 %up_back.6 = (bf16[512,1024]{1,0:T(8,128)(2,1)S(1)}, bf16[512,1024]{1,0:T(8,128)(2,1)S(1)}) custom-call(s32[4]{0:T(128)S(1)} %get-tuple-element.556.slots.in_slots, s32[4]{0:T(128)S(1)} %get-tuple-element.556.slots.in_slots, bf16[2048,384]{1,0:T(8,128)(2,1)} %attend_back.7.refs_1_.proj_mine, bf16[2048,384]{1,0:T(8,128)(2,1)} %attend_back.6.refs_1_.proj_other, ...), custom_call_target="tpu_custom_call" | custom-call | flops 200000000 | bytes 500000 | tf_op jit(solution)/shard_map/up_back/pallas_call | solution.py:492
  595.9 21.1 %collective-permute-done.47 = f32[4,4,768]{2,1,0:T(4,128)S(1)} collective-permute-done((f32[4,4,768]{2,1,0:T(4,128)S(1)}, f32[4,4,768]{2,1,0:T(4,128)S(1)}, u32[]{:S(2)}, u32[]{:S(2)}) %collective-permute-start.47) | collective-permute-done | bytes 49184 | tf_op jit(solution)/shard_map/ppermute | solution.py:33
  665.0 10.7 %collective-permute-done.51 = bf16[512,1024]{1,0:T(8,128)(2,1)} collective-permute-done((bf16[512,1024]{1,0:T(8,128)(2,1)}, bf16[512,1024]{1,0:T(8,128)(2,1)}, u32[]{:S(2)}, u32[]{:S(2)}) %collective-permute-start.51) | collective-permute-done | bytes 1048608 | tf_op jit(solution)/shard_map/ppermute | solution.py:33
  (583 shorter events, 340.3 us)
Async XLA Ops:
  7.2 124.5 %all-gather.4.cloned.1.call-start = ((), (), s32[]{:S(2)}) async-start(), calls=%async_computation.5 | async-start | bytes 1638400 | tf_op jit(solution)/shard_map/all_gather | solution.py:694
  22.9 35.1 %collective-permute-start.8 = (bf16[512,1024]{1,0:T(8,128)(2,1)}, bf16[512,1024]{1,0:T(8,128)(2,1)}, u32[]{:S(2)}, u32[]{:S(2)}) collective-permute-start(bf16[512,1024]{1,0:T(8,128)(2,1)} %select_bitcast_fusion.3.h0), channel_id=1, source_target_pairs={{0,4},{4,0},{8,12},{12,8},{1,5},{5,1},{9,13},{13,9},{2,6},{6,2},{1... | collective-permute-start | bytes 3145736 | tf_op jit(solution)/shard_map/ppermute | solution.py:33
  58.1 34.3 %collective-permute-start.14 = (bf16[4,288,384]{2,1,0:T(8,128)(2,1)}, bf16[4,288,384]{2,1,0:T(8,128)(2,1)}, u32[]{:S(2)}, u32[]{:S(2)}) collective-permute-start(bf16[4,288,384]{2,1,0:T(8,128)(2,1)} %copy-done.7), channel_id=1, source_target_pairs={{0,16},{16,0},{1,17},{17,1},{2,18},{18,2},{3,19},{19,3},{4,20},{20... | collective-permute-start | bytes 2654216 | tf_op jit(solution)/shard_map/ppermute | solution.py:33
  59.8 30.2 %collective-permute-start.11 = (bf16[256,512]{1,0:T(8,128)(2,1)}, bf16[256,512]{1,0:T(8,128)(2,1)}, u32[]{:S(2)}, u32[]{:S(2)}) collective-permute-start(bf16[256,512]{1,0:T(8,128)(2,1)} %slice_select_fusion.1), channel_id=1, source_target_pairs={{0,1},{1,2},{2,3},{3,0},{4,5},{5,6},{6,7},{7,4},{8,9},{9,10},{10,1... | collective-permute-start | bytes 786440 | tf_op jit(solution)/shard_map/ppermute | solution.py:623
  60.6 29.5 %collective-permute-start.12 = (bf16[256,512]{1,0:T(8,128)(2,1)}, bf16[256,512]{1,0:T(8,128)(2,1)}, u32[]{:S(2)}, u32[]{:S(2)}) collective-permute-start(bf16[256,512]{1,0:T(8,128)(2,1)} %slice_select_fusion.1), channel_id=1, source_target_pairs={{0,2},{1,3},{2,0},{3,1},{4,6},{5,7},{6,4},{7,5},{8,10},{9,11},{10,... | collective-permute-start | bytes 786440 | tf_op jit(solution)/shard_map/ppermute | solution.py:623
  61.0 29.0 %collective-permute-start.13 = (bf16[256,512]{1,0:T(8,128)(2,1)}, bf16[256,512]{1,0:T(8,128)(2,1)}, u32[]{:S(2)}, u32[]{:S(2)}) collective-permute-start(bf16[256,512]{1,0:T(8,128)(2,1)} %slice_select_fusion.1), channel_id=1, source_target_pairs={{0,3},{1,0},{2,1},{3,2},{4,7},{5,4},{6,5},{7,6},{8,11},{9,8},{10,9... | collective-permute-start | bytes 786440 | tf_op jit(solution)/shard_map/ppermute | solution.py:623
  92.3 144.6 %all-gather.6.cloned.1.call-start = ((), (), s32[]{:S(2)}) async-start(), calls=%async_computation.6 | async-start | bytes 1310720 | tf_op jit(solution)/shard_map/all_gather | solution.py:694
  131.7 27.4 %collective-permute-start.20 = (bf16[4,256,640]{2,1,0:T(8,128)(2,1)}, bf16[4,256,640]{2,1,0:T(8,128)(2,1)}, u32[]{:S(2)}, u32[]{:S(2)}) collective-permute-start(bf16[4,256,640]{2,1,0:T(8,128)(2,1)} %bitcast.174), channel_id=1, source_target_pairs={{0,16},{16,0},{1,17},{17,1},{2,18},{18,2},{3,19},{19,3},{4,20},{20... | collective-permute-start | bytes 3932168 | tf_op jit(solution)/shard_map/ppermute | solution.py:33
  184.0 27.5 %collective-permute-start.26 = (bf16[4,256,384]{2,1,0:T(8,128)(2,1)}, bf16[4,256,384]{2,1,0:T(8,128)(2,1)}, u32[]{:S(2)}, u32[]{:S(2)}) collective-permute-start(bf16[4,256,384]{2,1,0:T(8,128)(2,1)} %pad_maximum_fusion.2.weight_ref.qkv_mine.refs_2_), channel_id=1, source_target_pairs={{0,16},{16,0},{1,17},{17,1},{2,18},{18,2},{3,19},{19,3},{4,20},{20... | collective-permute-start | bytes 2359304 | tf_op jit(solution)/shard_map/ppermute | solution.py:33
  184.4 85.2 %all-gather.8.cloned.1.call-start = ((), (), s32[]{:S(2)}) async-start(), calls=%async_computation.7 | async-start | bytes 1638400 | tf_op jit(solution)/shard_map/all_gather | solution.py:694
  236.4 248.6 %reduce-scatter.6.cloned.1.call-start = ((), (), s32[]{:S(2)}) async-start(), calls=%async_computation.8 | async-start | bytes 2949120 | tf_op jit(solution)/shard_map/reduce_scatter | solution.py:627
  239.4 30.2 %collective-permute-start.30 = (bf16[4,256,512]{2,1,0:T(8,128)(2,1)}, bf16[4,256,512]{2,1,0:T(8,128)(2,1)}, u32[]{:S(2)}, u32[]{:S(2)}) collective-permute-start(bf16[4,256,512]{2,1,0:T(8,128)(2,1)} %bitcast.165), channel_id=1, source_target_pairs={{0,16},{16,0},{1,17},{17,1},{2,18},{18,2},{3,19},{19,3},{4,20},{20... | collective-permute-start | bytes 3145736 | tf_op jit(solution)/shard_map/ppermute | solution.py:33
  269.6 38.3 %collective-permute-start.31 = (bf16[4,256,640]{2,1,0:T(8,128)(2,1)}, bf16[4,256,640]{2,1,0:T(8,128)(2,1)S(1)}, u32[]{:S(2)}, u32[]{:S(2)}) collective-permute-start(bf16[4,256,640]{2,1,0:T(8,128)(2,1)} %bitcast.170), channel_id=1, source_target_pairs={{0,16},{16,0},{1,17},{17,1},{2,18},{18,2},{3,19},{19,3},{4,20},{20... | collective-permute-start | bytes 3932168 | tf_op jit(solution)/shard_map/ppermute | solution.py:33
  328.4 53.0 %collective-permute-start.32 = (bf16[4,256,1152]{2,1,0:T(8,128)(2,1)}, bf16[4,256,1152]{2,1,0:T(8,128)(2,1)S(1)}, u32[]{:S(2)}, u32[]{:S(2)}) collective-permute-start(bf16[4,256,1152]{2,1,0:T(8,128)(2,1)} %get-tuple-element.352), channel_id=1, source_target_pairs={{0,16},{16,0},{1,17},{17,1},{2,18},{18,2},{3,19},{19,3},{4,20},{20... | collective-permute-start | bytes 7077896 | tf_op jit(solution)/shard_map/ppermute | solution.py:33
  393.0 29.4 %collective-permute-start.35 = (bf16[512,1024]{1,0:T(8,128)(2,1)S(1)}, bf16[512,1024]{1,0:T(8,128)(2,1)S(1)}, u32[]{:S(2)}, u32[]{:S(2)}) collective-permute-start(bf16[512,1024]{1,0:T(8,128)(2,1)S(1)} %add_convert_fusion.3), channel_id=1, source_target_pairs={{0,8},{4,12},{8,0},{12,4},{1,9},{5,13},{9,1},{13,5},{2,10},{6,14},... | collective-permute-start | bytes 3145736 | tf_op jit(solution)/shard_map/ppermute | solution.py:33
  428.1 104.2 %reduce-scatter.8.cloned.1.call-start = ((), (), s32[]{:S(2)}) async-start(), calls=%async_computation.9 | async-start | bytes 983040 | tf_op jit(solution)/shard_map/reduce_scatter | solution.py:627
  428.2 28.0 %collective-permute-start.38 = (bf16[512,1024]{1,0:T(8,128)(2,1)S(1)}, bf16[512,1024]{1,0:T(8,128)(2,1)S(1)}, u32[]{:S(2)}, u32[]{:S(2)}) collective-permute-start(bf16[512,1024]{1,0:T(8,128)(2,1)S(1)} %fusion.16.g0), channel_id=1, source_target_pairs={{0,8},{4,12},{8,0},{12,4},{1,9},{5,13},{9,1},{13,5},{2,10},{6,14},... | collective-permute-start | bytes 3145736 | tf_op jit(solution)/shard_map/ppermute | solution.py:33
  485.0 53.6 %collective-permute-start.42 = (bf16[4,256,1152]{2,1,0:T(8,128)(2,1)}, bf16[4,256,1152]{2,1,0:T(8,128)(2,1)}, u32[]{:S(2)}, u32[]{:S(2)}) collective-permute-start(bf16[4,256,1152]{2,1,0:T(8,128)(2,1)} %get-tuple-element.415), channel_id=1, source_target_pairs={{0,16},{16,0},{1,17},{17,1},{2,18},{18,2},{3,19},{19,3},{4,20},{20... | collective-permute-start | bytes 7077896 | tf_op jit(solution)/shard_map/ppermute | solution.py:33
  485.4 89.1 %reduce-scatter.10.cloned.1.call-start = ((), (), s32[]{:S(2)}) async-start(), calls=%async_computation.10 | async-start | bytes 1310720 | tf_op jit(solution)/shard_map/reduce_scatter | solution.py:627
  486.4 42.6 %collective-permute-start.43 = (bf16[512,1024]{1,0:T(8,128)(2,1)}, bf16[512,1024]{1,0:T(8,128)(2,1)S(1)}, u32[]{:S(2)}, u32[]{:S(2)}) collective-permute-start(bf16[512,1024]{1,0:T(8,128)(2,1)} %copy-done.64), channel_id=1, source_target_pairs={{0,4},{4,0},{8,12},{12,8},{1,5},{5,1},{9,13},{13,9},{2,6},{6,2},{1... | collective-permute-start | bytes 3145736 | tf_op jit(solution)/shard_map/ppermute | solution.py:33
  544.1 83.2 %reduce-scatter.12.cloned.1.call-start = ((), (), s32[]{:S(2)}) async-start(), calls=%async_computation.11 | async-start | bytes 983040 | tf_op jit(solution)/shard_map/reduce_scatter | solution.py:627
  574.6 55.4 %reduce-scatter.14.cloned.1.call-start = ((), (), s32[]{:S(2)}) async-start(), calls=%async_computation.12 | async-start | bytes 1638400 | tf_op jit(solution)/shard_map/reduce_scatter | solution.py:627
  590.3 37.0 %collective-permute-start.49 = (bf16[512,1024]{1,0:T(8,128)(2,1)S(1)}, bf16[512,1024]{1,0:T(8,128)(2,1)}, u32[]{:S(2)}, u32[]{:S(2)}) collective-permute-start(bf16[512,1024]{1,0:T(8,128)(2,1)S(1)} %broadcast_select_fusion), channel_id=1, source_target_pairs={{0,16},{16,0},{1,17},{17,1},{2,18},{18,2},{3,19},{19,3},{4,20},{20... | collective-permute-start | bytes 3145736 | tf_op jit(solution)/shard_map/ppermute | solution.py:33
  595.0 32.3 %collective-permute-start.46 = (bf16[512,1024]{1,0:T(8,128)(2,1)}, bf16[512,1024]{1,0:T(8,128)(2,1)}, u32[]{:S(2)}, u32[]{:S(2)}) collective-permute-start(bf16[512,1024]{1,0:T(8,128)(2,1)} %add_convert_fusion.1), channel_id=1, source_target_pairs={{0,8},{4,12},{8,0},{12,4},{1,9},{5,13},{9,1},{13,5},{2,10},{6,14},... | collective-permute-start | bytes 3145736 | tf_op jit(solution)/shard_map/ppermute | solution.py:33
  (155 other events, 2278.2 us)
Sparse Core Ops, SparseCore 0:
  92.5 31.2 all-gather.3
  184.5 26.8 all-gather.5
  236.5 30.4 all-gather.7
  428.3 45.6 reduce-scatter.5
  485.6 21.7 reduce-scatter.7
  544.2 24.5 reduce-scatter.9
  574.7 21.7 reduce-scatter.11
  599.5 30.4 reduce-scatter.13
